TPU v7x, 32 devices: a whole 2x2x4 slice. The times are simulated.
32 devices in a mesh: wide: 8 (over z, core), narrow: 4 (over y, x).
Axes of the slice: x: 2, y: 2, z: 4, core: 2. Of those that a mesh axis runs over, the one named last changes fastest.
Arguments:
- features: float32 [12288, 512], P(('wide', 'narrow')), may hold values from -6 to 6
- weight: float32 [512, 512], replicated, may hold values from -0.25 to 0.25
- bias_vec: float32 [512], replicated, may hold values from -3 to 3
- adj_tiles: float32 [96, 8, 2, 128, 128], P('narrow', 'wide'), may hold values from -0.125 to 0.125
- pattern: int32 [96, 8, 2], P('narrow', 'wide'), may hold values from 0 to 11, as said below
- upstream: float32 [12288, 512], P(('narrow', 'wide')), may hold values from -6 to 6
Outputs:
- output: float32 [12288, 512], P(('narrow', 'wide'))
- input_grad: float32 [12288, 512], P(('wide', 'narrow'))
- weight_grad: float32 [512, 512], replicated
- bias_grad: float32 [512], replicated
Inputs may be any that keep to these rules, and one draw needn't show every extreme that they name: Within one block row and group the 2 entries differ; tile t of block row r in group g lies in block column g * 12 + pattern[r, g, t].
All inputs are finite; a program needn't handle non-finite values.
Results may differ from a plain program's by a relative error of at most 0.0003.
Values sent between devices are 32-bit elements; how exact they have to be, the bound alone decides.
No kernel may reach another device: no remote copies, remote signals or barrier semaphores. Data moves between devices by JAX's collectives and lax.ppermute only.
A program may use at most 64 MiB of HBM per device.

v0:
```python
import math

import jax
import jax.numpy as jnp
from jax import lax
from jax.sharding import PartitionSpec as P

highest = lax.Precision.HIGHEST


def silu_slope(preact):
    sigmoid_z = jax.nn.sigmoid(preact)
    return sigmoid_z * (1.0 + preact * (1.0 - sigmoid_z))


def body(features, weight, bias_vec, adj_tiles, pattern, upstream):
    own_rows, feat_width = features.shape
    block_rows = adj_tiles.shape[0]
    per_group = adj_tiles.shape[2]
    block_size = adj_tiles.shape[3]
    projected = jnp.dot(features, weight, precision=highest, preferred_element_type=jnp.float32)
    column_rows = lax.all_gather(projected, "narrow", axis=0, tiled=True)
    blocks = column_rows.reshape(-1, block_size, feat_width)
    group_blocks = blocks.shape[0]
    local_tiles = adj_tiles.reshape(block_rows, per_group, block_size, block_size)
    block_index = pattern.reshape(block_rows * per_group)
    chosen = jnp.take(blocks, block_index, axis=0).reshape(
        block_rows, per_group, block_size, feat_width
    )
    partial_agg = jnp.einsum("rtij,rtjd->rid", local_tiles, chosen, precision=highest)
    partial_agg = partial_agg.reshape(block_rows * block_size, feat_width)
    own_agg = lax.psum_scatter(partial_agg, "wide", scatter_dimension=0, tiled=True)
    preact = own_agg + bias_vec
    own_grads = upstream * silu_slope(preact)
    row_grads = lax.all_gather(own_grads, "wide", axis=0, tiled=True)
    output = preact * jax.nn.sigmoid(preact)
    backward_terms = jnp.einsum(
        "rtij,rid->rtjd",
        local_tiles,
        row_grads.reshape(block_rows, block_size, feat_width),
        precision=highest,
    )
    backward_terms = backward_terms.reshape(block_rows * per_group, block_size * feat_width)
    one_hot = (block_index[:, None] == jnp.arange(group_blocks, dtype=jnp.int32)[None, :]).astype(
        jnp.float32
    )
    spread = lax.dot_general(one_hot, backward_terms, (((0,), (0,)), ((), ())), precision=highest)
    spread = spread.reshape(group_blocks * block_size, feat_width)
    own_grad = lax.psum_scatter(spread, "narrow", scatter_dimension=0, tiled=True)
    input_grad = lax.dot_general(own_grad, weight, (((1,), (1,)), ((), ())), precision=highest)
    weight_term = lax.dot_general(features, own_grad, (((0,), (0,)), ((), ())), precision=highest)
    bias_term = jnp.sum(own_grads, axis=0)
    weight_sum, bias_sum = lax.psum((weight_term, bias_term), ("wide", "narrow"))
    node_total = own_rows * lax.axis_size("wide") * lax.axis_size("narrow")
    grad_scale = 1.0 / math.sqrt(node_total)
    return (output, input_grad, weight_sum * grad_scale, bias_sum * grad_scale)


def solution(mesh):
    in_specs = (
        P(("wide", "narrow"), None),
        P(),
        P(),
        P("narrow", "wide", None, None, None),
        P("narrow", "wide", None),
        P(("narrow", "wide"), None),
    )
    out_specs = (P(("narrow", "wide"), None), P(("wide", "narrow"), None), P(), P())
    return jax.shard_map(body, mesh=mesh, in_specs=in_specs, out_specs=out_specs, check_vma=False)
```

profile of v0, /device:TPU:1, one launch (start us, length us, event | category | flops | bytes accessed | tf_op | source)
XLA Modules:
  0.0 444.5 jit_solution(13083849261026755925)
XLA Ops:
  7.2 0.0 copy-start
  7.2 0.0 all-gather.3.cloned.1.call-start
  7.2 3.9 fusion.12
  11.2 0.0 all-gather.3.cloned.1.call-update
  11.2 0.0 reduce-scatter.3.cloned.1.call-start
  11.2 0.8 copy.15
  12.0 0.7 compare_and_fusion
  12.7 0.1 copy.14
  12.8 0.1 reshape.75
  12.9 44.5 %all-gather.3.cloned.1.call-done = f32[1536,512]{1,0:T(8,128)} async-done(((f32[384,512]{1,0:T(8,128)}), f32[1536,512]{1,0:T(8,128)}) %all-gather.3.cloned.1.call-update) | async-done | bytes 3145744 | tf_op jit(solution)/shard_map/all_gather | solution.py:22
  57.4 9.5 %gather_fusion = f32[48,128,512]{2,1,0:T(8,128)} fusion(f32[12,128,512]{2,1,0:T(8,128)} %bitcast.45, s32[1024]{0:T(1024)S(1)} %pad_clamp_fusion), kind=kCustom, calls=%fused_computation | custom fusion | bytes 25166016 | tf_op jit(solution)/shard_map/jit(_take)/gather | solution.py:27
  66.9 0.0 copy-done
  66.9 12.5 %fusion = f32[24,512,128,1]{1,2,3,0:T(8,128)} fusion(f32[24,2,128,512]{3,2,1,0:T(8,128)} %bitcast.43, pred[24,2]{1,0:T(8,128)(4,1)S(1)} %copy.14, f32[24,1,2,128,128]{4,3,2,1,0:T(8,128)S(1)} %copy-done), kind=kOutput, calls=%fused_computation.1 | convolution fusion | flops 4834983936 | bytes 22020144 | tf_op jit(solution)/shard_map/rtij,rtjd->rid/dot_general | solution.py:30
  79.4 0.0 copy-start.2
  79.4 0.0 reduce-scatter.3.cloned.1.call-update
  79.4 0.0 all-gather.5.cloned.1.call-start
  79.5 67.8 %reduce-scatter.3.cloned.1.call-done = f32[384,512]{1,0:T(8,128)} async-done(((f32[3072,512]{1,0:T(8,128)}), f32[384,512]{1,0:T(8,128)}) %reduce-scatter.3.cloned.1.call-update) | async-done | bytes 786448 | tf_op jit(solution)/shard_map/reduce_scatter | solution.py:32
  147.3 0.0 copy-done.2
  147.3 2.9 fusion.11
  150.1 0.0 all-gather.5.cloned.1.call-update
  150.1 0.2 reduce-scatter.5.cloned.1.call-start
  150.4 0.1 reshape.78
  150.5 65.5 %all-gather.5.cloned.1.call-done = f32[3072,512]{1,0:T(8,128)} async-done(((f32[384,512]{1,0:T(8,128)}), f32[3072,512]{1,0:T(8,128)}) %all-gather.5.cloned.1.call-update) | async-done | bytes 6291472 | tf_op jit(solution)/shard_map/all_gather | solution.py:35
  216.0 14.8 %convolution_bitcast_fusion = f32[24,2,128,512]{2,3,1,0:T(8,128)} fusion(f32[24,128,512,1]{2,1,3,0:T(8,128)} %bitcast.47, f32[24,1,2,128,128]{4,3,2,1,0:T(8,128)S(1)} %copy-done), kind=kOutput, calls=%fused_computation.5 | convolution fusion | flops 4831838208 | bytes 22020096 | tf_op jit(solution)/shard_map/rtij,rid->rtjd/dot_general | solution.py:37
  230.8 12.7 %copy.24 = f32[6,8,128,512]{3,1,2,0:T(8,128)} copy(f32[6,8,128,512]{2,3,1,0:T(8,128)} %bitcast.44) | data formatting | bytes 25165824
  243.5 8.6 %fusion.7 = f32[12,65536]{1,0:T(8,128)} fusion(f32[48,65536]{1,0:T(8,128)} %bitcast.42, s32[48]{0:T(128)S(1)} %reshape.78), kind=kOutput, calls=%fused_computation.14 | convolution fusion | flops 452985408 | bytes 15728832 | tf_op jit(solution)/shard_map/dot_general | solution.py:47
  252.1 3.8 reshape.81
  255.9 0.0 copy-start.1
  255.9 0.0 reduce-scatter.5.cloned.1.call-update
  255.9 0.0 all-reduce.2.cloned.1.call-start
  255.9 42.3 %reduce-scatter.5.cloned.1.call-done = f32[384,512]{1,0:T(8,128)} async-done(((f32[1536,512]{1,0:T(8,128)}), f32[384,512]{1,0:T(8,128)}) %reduce-scatter.5.cloned.1.call-update) | async-done | bytes 786448 | tf_op jit(solution)/shard_map/reduce_scatter | solution.py:49
  298.2 4.2 convolution_bitcast_fusion.1
  302.4 0.0 all-reduce.2.cloned.1.call-update
  302.4 39.0 %psum.15 = f32[512]{0:T(512)S(1)} all-reduce(f32[512]{0:T(512)S(1)} %get-tuple-element.12), channel_id=1, replica_groups=mesh['wide'=8,'narrow'=4] {'wide','narrow'}, use_global_device_ids=true, to_apply=%region_4.5 | all-reduce | flops 512 | bytes 4096 | tf_op jit(solution)/shard_map/psum | solution.py:53
  341.5 0.6 broadcast_multiply_fusion.1
  342.1 3.8 fusion.13
  345.9 87.2 %all-reduce.2.cloned.1.call-done = f32[512,512]{0,1:T(8,128)} async-done(((f32[512,512]{0,1:T(8,128)}), f32[512,512]{0,1:T(8,128)}) %all-reduce.2.cloned.1.call-update) | async-done | bytes 1048592 | tf_op jit(solution)/shard_map/psum | solution.py:53
  433.1 2.3 broadcast_multiply_fusion
  435.4 2.5 copy.19
  438.0 0.0 copy-done.1
  (2 shorter events, 0.0 us)
Async XLA Ops:
  7.2 59.8 %copy-start = (f32[24,1,2,128,128]{4,3,2,1,0:T(8,128)S(1)}, f32[24,1,2,128,128]{4,3,2,1,0:T(8,128)}, u32[]{:S(2)}) copy-start(f32[24,1,2,128,128]{4,3,2,1,0:T(8,128)} %param.9) | copy-start | bytes 9437188
  7.2 50.2 %all-gather.3.cloned.1.call-start = ((), (), s32[]{:S(2)}) async-start(), calls=%async_computation.2 | async-start | bytes 3932160 | tf_op jit(solution)/shard_map/all_gather | solution.py:22
  11.2 136.1 %reduce-scatter.3.cloned.1.call-start = ((), (), s32[]{:S(2)}) async-start(), calls=%async_computation.3 | async-start | bytes 7077888 | tf_op jit(solution)/shard_map/reduce_scatter | solution.py:32
  79.4 67.9 %copy-start.2 = (f32[512]{0:T(512)S(1)}, f32[512]{0:T(512)}, u32[]{:S(2)}) copy-start(f32[512]{0:T(512)} %param.8) | copy-start | bytes 6148
  79.4 136.6 %all-gather.5.cloned.1.call-start = ((), (), s32[]{:S(2)}) async-start(), calls=%async_computation.4 | async-start | bytes 7077888 | tf_op jit(solution)/shard_map/all_gather | solution.py:35
  150.1 148.1 %reduce-scatter.5.cloned.1.call-start = ((), (), s32[]{:S(2)}) async-start(), calls=%async_computation.5 | async-start | bytes 3932160 | tf_op jit(solution)/shard_map/reduce_scatter | solution.py:49
  255.9 182.1 %copy-start.1 = (f32[24,1,2,128,128]{4,3,2,1,0:T(8,128)S(1)}, f32[24,1,2,128,128]{4,3,2,1,0:T(8,128)}, u32[]{:S(2)}) copy-start(f32[24,1,2,128,128]{4,3,2,1,0:T(8,128)} %param.9) | copy-start | bytes 9437188
  255.9 177.2 %all-reduce.2.cloned.1.call-start = ((), (), s32[]{:S(2)}) async-start(), calls=%async_computation.6 | async-start | bytes 2097152 | tf_op jit(solution)/shard_map/psum | solution.py:53
Sparse Core Ops, SparseCore 0:
  11.3 46.0 all-gather.2
  79.5 67.6 reduce-scatter.2
  150.3 65.6 all-gather.4
  256.0 42.1 reduce-scatter.4
  303.8 129.2 all-reduce.1
where the time goes:
time: 446 us; the launch traced here: 445 us
  waiting for transfers between devices  307 us (69%)
  matrix products  47.8 us (11%)
  blocking collectives  39 us (9%)
  local copies, waits for them, and re-layouts  29.6 us (7%)
  between operations  13.8 us (3%)
  other arithmetic  6.48 us (1%)
    psum x1, waiting for transfers between devices, body(): lax.psum((weight_term, bias_term), ('wide', 'narrow'))  87.2 us
    reduce_scatter x1, waiting for transfers between devices, body(): lax.psum_scatter(partial_agg, 'wide', scatter_dimension=0, tiled=True)  67.8 us
    all_gather x1, waiting for transfers between devices, body(): row_grads = lax.all_gather(own_grads, 'wide', axis=0, tiled=True)  65.5 us
    all_gather x1, waiting for transfers between devices, body(): column_rows = lax.all_gather(projected, 'narrow', axis=0, tiled=True)  44.5 us
    reduce_scatter x1, waiting for transfers between devices, body(): lax.psum_scatter(spread, 'narrow', scatter_dimension=0, tiled=True)  42.3 us
    psum x1, blocking collectives, body(): lax.psum((weight_term, bias_term), ('wide', 'narrow'))  39 us
    unnamed x9, local copies, waits for them, and re-layouts  16 us
    dot_general x1, matrix products, body(): jnp.einsum('rtij,rid->rtjd', local_tiles, row_grads.reshape(block_rows, b...  14.8 us
  transfers between devices with their start and end apart: 5, of which 5 were waited for; matrix products, arithmetic and copies ran while one was open for 1% of the time, Pallas kernels for 0%

commit v1 on v0

v1 whole, which is shorter than its diff:
```python
import functools
import math

import jax
import jax.numpy as jnp
from jax import lax
from jax.experimental import pallas as pl
from jax.experimental.pallas import tpu as pltpu
from jax.sharding import PartitionSpec as P

F32 = jnp.float32
BF16 = jnp.bfloat16
HIGH = lax.Precision.HIGH
WIDTHS = (1, 1, 1, 1)
EARLY = 3
WAVES = (False, False, True)
ORDER = ('01201p2x0101x02120x3123013203023101232v3v123v123wvwwvw3wv0bw', 'vbwv3wbvw')
SMALL_VMEM = 12 * 1024 * 1024
VMEM_LIMIT = 40 * 1024 * 1024
STAGE = 16000000000.0


def cost(stages=1.0):
    return pl.CostEstimate(flops=int(STAGE * stages), bytes_accessed=0, transcendentals=0)


def split(x):
    hi = x.astype(BF16)
    return hi, (x - hi.astype(F32)).astype(BF16)


def mm(a, b):
    return jnp.dot(a, b, preferred_element_type=F32)


def bits_of(size):
    return [1 << k for k in range(size.bit_length() - 1)]


def swap(x, dim):
    axis, bit = dim
    size = lax.axis_size(axis)
    return lax.ppermute(x, axis, [(i, i ^ bit) for i in range(size)])


ROWS = 64


def rows_call(fn, out_rows, xs, extra=()):
    width = xs[0].shape[1]
    outs = [jax.ShapeDtypeStruct((rows, width), F32) for rows in out_rows]
    count, every = len(xs), len(xs) + len(extra)

    def kernel(*refs):
        fn(refs[:count], refs[count:every], refs[every:])

    vmem = pl.BlockSpec(memory_space=pltpu.VMEM)
    return pl.pallas_call(
        kernel,
        in_specs=[vmem] * every,
        out_specs=[vmem] * len(outs),
        out_shape=outs,
        compiler_params=pltpu.CompilerParams(vmem_limit_bytes=SMALL_VMEM),
        cost_estimate=cost(),
    )(*xs, *extra)


def blocks_of(rows, step):
    unit = math.gcd(rows, ROWS)

    @pl.loop(0, rows // unit)
    def _(k):
        step(pl.multiple_of(k * unit, unit), unit)


def add_halves(keep, got):
    half = keep.shape[0] // 2

    def fn(ins, _, outs):
        for k, out in enumerate(outs):

            def step(at, unit, k=k, out=out):
                rows = pl.ds(k * half + at, unit)
                out[pl.ds(at, unit), :] = ins[0][rows, :] + ins[1][rows, :]

            blocks_of(half, step)

    return rows_call(fn, [half, half], [keep, got])


def stack(parts):
    def fn(ins, _, outs):
        base = 0
        for ref in ins:

            def step(at, unit, base=base, ref=ref):
                outs[0][pl.ds(base + at, unit), :] = ref[pl.ds(at, unit), :]

            blocks_of(ref.shape[0], step)
            base += ref.shape[0]

    return rows_call(fn, [sum(p.shape[0] for p in parts)], parts)[0]


def add_all(terms):
    def fn(ins, _, outs):
        def step(at, unit):
            rows = pl.ds(at, unit)
            total = ins[0][rows, :]
            for ref in ins[1:]:
                total = total + ref[rows, :]
            outs[0][rows, :] = total

        blocks_of(outs[0].shape[0], step)

    return rows_call(fn, [terms[0].shape[0]], terms)[0]


def activate(keep, got, upstream, bias):
    def fn(ins, extra, outs):
        def step(at, unit):
            rows = pl.ds(at, unit)
            preact = ins[0][rows, :] + ins[1][rows, :] + extra[0][...]
            gate = jax.nn.sigmoid(preact)
            outs[0][rows, :] = preact * gate
            outs[1][rows, :] = ins[2][rows, :] * gate * (1.0 + preact * (1.0 - gate))

        blocks_of(outs[0].shape[0], step)

    rows = keep.shape[0]
    return rows_call(fn, [rows, rows], [keep, got, upstream], [bias.reshape(1, -1)])


class Line:
    def __init__(self):
        self.last = None

    def enter(self, xs):
        if self.last is not None:
            xs, self.last = lax.optimization_barrier((xs, self.last))
        return xs

    def leave(self, xs):
        self.last = xs
        return xs


def gather_stages(line, x, dims, out, waves):
    parts = [x]
    if waves and len(dims) == 2:
        first, second = swap(x, dims[0]), swap(x, dims[1])
        yield
        last = swap(line.leave(stack([line.enter(first)])), dims[1])
        parts = [x, first, second, last]
    else:
        for dim in dims:
            if len(parts) > 1:
                yield
                parts = line.enter(parts)
                parts = [line.leave(stack(parts))]
            parts = parts + [swap(parts[0], dim)]
    yield
    out.extend(line.enter(parts))


def halve_stages(line, keep, send, dims, out):
    for k, dim in enumerate(dims):
        got = swap(send, dim)
        yield
        keep, got = line.enter((keep, got))
        if k + 1 == len(dims):
            out.extend((keep, got))
        else:
            keep, send = line.leave(add_halves(keep, got))


def slot_of(owner, me, labels):
    s = owner ^ me
    last = len(labels) - 1
    return sum(((s // label) & 1) << (last - k) for k, label in enumerate(labels))


def slot_order(labels):
    order = [0]
    for label in reversed(labels):
        order = order + [s ^ label for s in order]
    return order


def prep_kernel(tiles_ref, hi_ref, lo_ref, hit_ref, lot_ref):
    steps, per_group, size, _ = tiles_ref.shape
    for r in range(steps):
        for t in range(per_group):
            tile = tiles_ref[r, t]
            hi, lo = split(tile)
            cols = pl.ds(t * size, size)
            hi_ref[r, :, cols] = hi
            lo_ref[r, :, cols] = lo
            hi, lo = split(tile.T)
            hit_ref[r, cols, :] = hi
            lot_ref[r, cols, :] = lo


def prep(tiles, step):
    rows, per_group, size, _ = tiles.shape
    wide = jax.ShapeDtypeStruct((rows, size, per_group * size), BF16)
    tall = jax.ShapeDtypeStruct((rows, per_group * size, size), BF16)
    return pl.pallas_call(
        prep_kernel,
        grid=(rows // step,),
        in_specs=[pl.BlockSpec((step, per_group, size, size), lambda i: (i, 0, 0, 0))],
        out_specs=[pl.BlockSpec((step,) + s.shape[1:], lambda i: (i, 0, 0)) for s in (wide, wide, tall, tall)],
        out_shape=[wide, wide, tall, tall],
        compiler_params=pltpu.CompilerParams(vmem_limit_bytes=VMEM_LIMIT),
        cost_estimate=cost(0),
    )(tiles)


def load_split(refs, hi, lo):
    base = 0
    for ref in refs:
        rows = ref.shape[0]
        hi[pl.ds(base, rows), :], lo[pl.ds(base, rows), :] = split(ref[...])
        base += rows


def block_rows_at(start, size, unit, own_rows, place):
    at = []
    for q in range(size // unit):
        row = start + q * unit
        w = place(row // own_rows) * own_rows + row % own_rows
        at.append(pl.multiple_of(w, unit))
    return at


def products(a_hi, a_lo, b_hi, b_lo):
    return mm(a_hi, b_hi) + (mm(a_hi, b_lo) + mm(a_lo, b_hi))


def gathered(ref, at, unit):
    return jnp.concatenate([ref[pl.ds(w, unit), :] for w in at], axis=0) if len(at) > 1 else ref[pl.ds(at[0], unit), :]


def forward_kernel(own_rows, wide_labels, narrow_labels, me, pattern, a_hi, a_lo, *rest):
    *p_refs, keep, send, p_hi, p_lo, total = rest
    step = pl.program_id(0)
    rows, size, depth = a_hi.shape
    per_group = depth // size
    unit = math.gcd(own_rows, size)

    @pl.when(step == 0)
    def _():
        load_split(p_refs, p_hi, p_lo)

    for i in range(rows):
        r = step * rows + i
        at = []
        for t in range(per_group):
            start = pattern[r * per_group + t] * size
            at += block_rows_at(start, size, unit, own_rows, lambda o: slot_of(o, me[1], narrow_labels))
        acc = products(a_hi[i], a_lo[i], gathered(p_hi, at, unit), gathered(p_lo, at, unit))
        out_at = block_rows_at(r * size, size, unit, own_rows, lambda o: slot_of(o, me[0], wide_labels))
        for q, w in enumerate(out_at):
            total[pl.ds(w, unit), :] = acc[q * unit : (q + 1) * unit]

    @pl.when(step == pl.num_programs(0) - 1)
    def _():
        half = keep.shape[0]
        keep[...] = total[:half]
        send[...] = total[half:]


def tile_call(kernel, me, pattern, a_hi, a_lo, slots, step, outs, total_rows):
    rows = a_hi.shape[0]
    width = slots[0].shape[1]
    in_rows = sum(s.shape[0] for s in slots)
    whole = lambda s: pl.BlockSpec(s, lambda i, *_: (0, 0))
    tile = pl.BlockSpec((step,) + a_hi.shape[1:], lambda i, *_: (i, 0, 0))
    outs = [jax.ShapeDtypeStruct((n, width), F32) for n in outs]
    return pl.pallas_call(
        kernel,
        grid_spec=pltpu.PrefetchScalarGridSpec(
            num_scalar_prefetch=2,
            grid=(rows // step,),
            in_specs=[tile, tile] + [whole(s.shape) for s in slots],
            out_specs=[whole(o.shape) for o in outs],
            scratch_shapes=[
                pltpu.VMEM((in_rows, width), BF16),
                pltpu.VMEM((in_rows, width), BF16),
                pltpu.VMEM((total_rows, width), F32),
            ],
        ),
        out_shape=outs,
        compiler_params=pltpu.CompilerParams(vmem_limit_bytes=VMEM_LIMIT),
        cost_estimate=cost(),
    )(me, pattern, a_hi, a_lo, *slots)


def backward_kernel(own_rows, wide_labels, narrow_labels, me, pattern, a_hi, a_lo, *rest):
    *g_refs, keep, send, sums, g_hi, g_lo, total = rest
    step = pl.program_id(0)
    rows, depth, size = a_hi.shape
    per_group = depth // size
    unit = math.gcd(own_rows, size)

    @pl.when(step == 0)
    def _():
        load_split(g_refs, g_hi, g_lo)
        total[...] = jnp.zeros_like(total)
        sums[...] = sum(jnp.sum(ref[...].reshape(-1, 8, ref.shape[1]), axis=0) for ref in g_refs)

    for i in range(rows):
        r = step * rows + i
        at = block_rows_at(r * size, size, unit, own_rows, lambda o: slot_of(o, me[0], wide_labels))
        acc = products(a_hi[i], a_lo[i], gathered(g_hi, at, unit), gathered(g_lo, at, unit))
        for t in range(per_group):
            start = pattern[r * per_group + t] * size
            out_at = block_rows_at(start, size, unit, own_rows, lambda o: slot_of(o, me[1], narrow_labels))
            for q, w in enumerate(out_at):
                total[pl.ds(w, unit), :] += acc[t * size + q * unit : t * size + (q + 1) * unit]

    @pl.when(step == pl.num_programs(0) - 1)
    def _():
        half = keep.shape[0]
        keep[...] = total[:half]
        send[...] = total[half:]


def turn_kernel(*refs):
    *x_refs, hi, lo = refs
    base = 0
    for ref in x_refs:
        cols = pl.ds(base, ref.shape[0])
        hi[:, cols], lo[:, cols] = split(ref[...].T)
        base += ref.shape[0]


def turn(slots):
    rows = sum(s.shape[0] for s in slots)
    out = jax.ShapeDtypeStruct((slots[0].shape[1], rows), BF16)
    return pl.pallas_call(
        turn_kernel,
        out_shape=[out, out],
        compiler_params=pltpu.CompilerParams(vmem_limit_bytes=VMEM_LIMIT),
        cost_estimate=cost(),
    )(*slots)


def outer_kernel(labels, orders, me, x_hi, x_lo, *rest):
    *s_refs, keep, send, total = rest
    feats, count = x_hi.shape
    pieces = 1 << len(labels)
    unit = feats // pieces
    base = 0
    for k, order in enumerate(orders):
        refs = s_refs[2 * k : 2 * k + 2]
        width = refs[0].shape[1]
        own = count // len(order)
        half = len(order) // 2
        acc = None
        for j, s in enumerate(order):
            cols = pl.ds(s * own, own)
            rows = refs[j // half][pl.ds((j % half) * own, own), :]
            part = products(x_hi[:, cols], x_lo[:, cols], *split(rows))
            acc = part if acc is None else acc + part
        for q in range(pieces):
            w = slot_of(q, me[2], labels) * unit
            total[pl.ds(pl.multiple_of(w, unit), unit), pl.ds(base, width)] = acc[q * unit : (q + 1) * unit]
        base += width
    half = feats // 2
    keep[...] = total[:half]
    send[...] = total[half:]


def outer(me, x_hi, x_lo, parts, labels, orders):
    feats = x_hi.shape[0]
    width = sum(s.shape[1] for s in parts) // 2
    out = jax.ShapeDtypeStruct((feats // 2, width), F32)
    vmem = pl.BlockSpec(memory_space=pltpu.VMEM)
    return pl.pallas_call(
        functools.partial(outer_kernel, labels, orders),
        in_specs=[pl.BlockSpec(memory_space=pltpu.SMEM)] + [vmem] * (2 + len(parts)),
        out_specs=[vmem, vmem],
        out_shape=[out, out],
        scratch_shapes=[pltpu.VMEM((feats, width), F32)],
        compiler_params=pltpu.CompilerParams(vmem_limit_bytes=VMEM_LIMIT),
        cost_estimate=cost(),
    )(me, x_hi, x_lo, *parts)


def place_kernel(scale, labels, me, *refs):
    *p_refs, out = refs
    order = slot_order(labels)
    unit = out.shape[0] // len(order)
    half = len(order) // 2
    for k, s in enumerate(order):
        part = p_refs[k // half][pl.ds((k % half) * unit, unit), :]
        out[pl.ds(pl.multiple_of((me[2] ^ s) * unit, unit), unit), :] = part * scale


def place(me, parts, labels, scale):
    rows, width = parts[0].shape
    vmem = pl.BlockSpec(memory_space=pltpu.VMEM)
    return pl.pallas_call(
        functools.partial(place_kernel, scale, labels),
        in_specs=[pl.BlockSpec(memory_space=pltpu.SMEM)] + [vmem] * len(parts),
        out_specs=vmem,
        out_shape=jax.ShapeDtypeStruct((rows * len(parts), width), F32),
        compiler_params=pltpu.CompilerParams(vmem_limit_bytes=VMEM_LIMIT),
        cost_estimate=cost(),
    )(me, *parts)


def body(features, weight, bias_vec, adj_tiles, pattern, upstream):
    own_rows, feat_width = features.shape
    block_rows, _, per_group, size, _ = adj_tiles.shape
    n_wide, n_narrow = lax.axis_size("wide"), lax.axis_size("narrow")
    me_wide, me_narrow = lax.axis_index("wide"), lax.axis_index("narrow")
    step = math.gcd(block_rows, 6)
    widths = [w * feat_width // sum(WIDTHS) for w in WIDTHS]
    edges = [sum(widths[:c]) for c in range(len(widths) + 1)]
    count = len(widths)
    grad_scale = 1.0 / math.sqrt(own_rows * n_wide * n_narrow)
    line = Line()

    core = ("wide", 1)
    z_bits = bits_of(n_wide)[1:]
    z_dims = [("wide", b) for b in z_bits]
    narrow_bits = bits_of(n_narrow)
    narrow_dims = [("narrow", b) for b in narrow_bits]
    wide_labels = [1] + z_bits
    sum_labels = [1] + [2 * b for b in narrow_bits]
    me = jnp.stack([me_wide, me_narrow, me_wide % 2 + 2 * me_narrow]).astype(jnp.int32)
    pattern = pattern.reshape(-1)

    tiles = []

    outputs, column_grads, halves, sums = [None] * count, [None] * count, [None] * count, [None] * count
    turned = []

    def chunk_bits(c):
        return narrow_bits if c % 2 == 0 else narrow_bits[::-1]

    def chunk(c):
        cols = slice(edges[c], edges[c + 1])
        n_bits = chunk_bits(c)
        n_dims = [("narrow", b) for b in n_bits]

        own = line.enter(features)
        own = jnp.dot(own, weight[:, cols], precision=HIGH, preferred_element_type=F32)
        inputs = []
        yield from gather_stages(line, line.leave(own), n_dims[::-1], inputs, WAVES[0])
        while not tiles:
            yield
        a_hi, a_lo, at_hi, at_lo = tiles
        kernel = functools.partial(forward_kernel, own_rows, wide_labels, n_bits)
        half = block_rows * size // 2
        keep, send = line.leave(tile_call(kernel, me, pattern, a_hi, a_lo, inputs, step, [half, half], 2 * half))
        got = swap(send, core)
        yield
        keep, got = line.enter((keep, got))
        keep, send = line.leave(add_halves(keep, got))
        found = []
        yield from halve_stages(line, keep, send, z_dims, found)
        outputs[c], grads = activate(*found, upstream[:, cols], bias_vec[cols])
        line.leave(grads)
        rows = []
        yield from gather_stages(line, grads, z_dims[::-1], rows, WAVES[1])
        rows = line.leave(stack(rows))
        got = swap(rows, core)
        yield
        inputs = line.enter([rows, got])
        kernel = functools.partial(backward_kernel, own_rows, wide_labels, n_bits)
        half = own_rows * n_narrow // 2
        keep, send, sums[c] = line.leave(
            tile_call(kernel, me, pattern, at_hi, at_lo, inputs, step, [half, half, 8], 2 * half)
        )
        halves[c] = (keep, send)
        found = []
        yield from halve_stages(line, keep, send, n_dims, found)
        column_grads[c] = line.leave(add_all(found))

    def tile_parts():
        own = line.enter(adj_tiles).reshape(block_rows, per_group, size, size)
        tiles.extend(line.leave(prep(own, step)))
        yield

    def feature_rows():
        slots = []
        yield from gather_stages(line, line.enter(features), narrow_dims[::-1], slots, WAVES[2])
        turned.extend(line.leave(turn(slots)))

    def weight_stages(first, last, out):
        while not turned or None in halves[first:last]:
            yield
        there = slot_order(narrow_bits)
        orders = [[there.index(s) for s in slot_order(chunk_bits(c))] for c in range(first, last)]
        parts = [h for c in range(first, last) for h in halves[c]]
        x_hi, x_lo, *parts = line.enter(list(turned) + parts)
        keep, send = line.leave(outer(me, x_hi, x_lo, parts, sum_labels, orders))
        found = []
        yield from halve_stages(line, keep, send, [core] + narrow_dims, found)
        total = line.leave(add_all(found))
        for dim in z_dims:
            got = swap(total, dim)
            yield
            total, got = line.enter((total, got))
            total = line.leave(add_all([total, got]))
        parts = []
        yield from gather_stages(line, total, narrow_dims[::-1], parts, False)
        parts = line.leave(stack(parts))
        got = swap(parts, core)
        yield
        out.append(line.leave(place(me, line.enter([parts, got]), sum_labels, grad_scale)))

    def bias_stages(out):
        while None in halves:
            yield
        total = line.leave(jnp.concatenate(sums, axis=1))
        for dim in narrow_dims:
            got = swap(total, dim)
            yield
            total, got = line.enter((total, got))
            total = line.leave(total + got)
        out.append(jnp.sum(total, axis=0) * grad_scale)

    early_parts, weight_parts, bias_out = [], [], []
    lines = {"p": tile_parts()}
    lines.update({str(c): chunk(c) for c in range(count)})
    lines["x"] = feature_rows()
    first = EARLY
    if first:
        lines["v"] = weight_stages(0, first, early_parts)
    lines["w"] = weight_stages(first, count, weight_parts)
    lines["b"] = bias_stages(bias_out)
    for k, name in enumerate("".join(ORDER)):
        with jax.named_scope(f"stage_{name}_{k}"):
            next(lines[name] if name in lines else iter(()), None)
    for stages in lines.values():
        for _ in stages:
            pass
    column_grad = jnp.concatenate(column_grads, axis=1)
    input_grad = lax.dot_general(column_grad, weight, (((1,), (1,)), ((), ())), precision=HIGH)
    return (
        jnp.concatenate(outputs, axis=1),
        input_grad,
        jnp.concatenate(early_parts + weight_parts, axis=1),
        bias_out[0],
    )


def solution(mesh):
    in_specs = (
        P(("wide", "narrow"), None),
        P(),
        P(),
        P("narrow", "wide", None, None, None),
        P("narrow", "wide", None),
        P(("narrow", "wide"), None),
    )
    out_specs = (P(("narrow", "wide"), None), P(("wide", "narrow"), None), P(), P())
    return jax.shard_map(body, mesh=mesh, in_specs=in_specs, out_specs=out_specs, check_vma=False)
```

time: 446 us -> 197 us (0.44)
  waiting for transfers between devices: 307 us -> 59.8 us
  starting transfers between devices: 0.39 us -> 78.9 us
  Pallas kernels: 0 us -> 43.4 us
  matrix products: 47.8 us -> 8.4 us
  blocking collectives: 39 us -> 0 us
  local copies, waits for them, and re-layouts: 29.6 us -> 1.65 us
  between operations: 13.8 us -> 1.33 us
    reduce_scatter x2 -> x0, waiting for transfers between devices: 110 us -> none  [the longest x1 67.8 us: body(): lax.psum_scatter(partial_agg, 'wide', scatter_dimension=0, tiled=True)]
    all_gather x2 -> x0, waiting for transfers between devices: 110 us -> none  [the longest x1 65.5 us: body(): row_grads = lax.all_gather(own_grads, 'wide', axis=0, tiled=True)]
    psum x1 -> x0, waiting for transfers between devices: 87.2 us -> none  [body(): lax.psum((weight_term, bias_term), ('wide', 'narrow'))]
    ppermute x0 -> x61, starting transfers between devices: none -> 78.9 us  [swap(): return lax.ppermute(x, axis, [(i, i ^ bit) for i in range(size)])]
    ppermute x0 -> x61, waiting for transfers between devices: none -> 59.8 us  [swap(): return lax.ppermute(x, axis, [(i, i ^ bit) for i in range(size)])]
    pallas_call x0 -> x61, Pallas kernels: none -> 43.4 us  [the longest x8 27.4 us: tile_call(): pl.pallas_call(kernel, grid_spec=pltpu.PrefetchScalarGridSpec(num_scalar_...]
    dot_general x6 -> x5, matrix products: 47.8 us -> 8.4 us  [the longest x4 6.66 us: chunk(): jnp.dot(own, weight[:, cols], precision=HIGH, preferred_element_type=F32)]
    psum x1 -> x0, blocking collectives: 39 us -> none  [body(): lax.psum((weight_term, bias_term), ('wide', 'narrow'))]
  transfers between devices with their start and end apart: 5 -> 61, of which waited for: 5 -> 22; matrix products, arithmetic and copies ran while one was open for 1% -> 4% of each run, Pallas kernels for 0% -> 22%
where the time goes in v1:
time: 197 us; the launch traced here: 196 us
  starting transfers between devices  78.9 us (40%)
  waiting for transfers between devices  59.8 us (30%)
  Pallas kernels  43.4 us (22%)
  matrix products  8.4 us (4%)
  other arithmetic  2.71 us (1%)
    ppermute x61, starting transfers between devices, swap(): return lax.ppermute(x, axis, [(i, i ^ bit) for i in range(size)])  78.9 us
    ppermute x61, waiting for transfers between devices, swap(): return lax.ppermute(x, axis, [(i, i ^ bit) for i in range(size)])  59.8 us
    pallas_call x8, Pallas kernels, tile_call(): pl.pallas_call(kernel, grid_spec=pltpu.PrefetchScalarGridSpec(num_scalar_...  27.4 us
    pallas_call x2, Pallas kernels, outer(): pl.pallas_call(functools.partial(outer_kernel, labels, orders), in_specs=...  6.74 us
    dot_general x4, matrix products, chunk(): jnp.dot(own, weight[:, cols], precision=HIGH, preferred_element_type=F32)  6.66 us
    pallas_call x47, Pallas kernels, rows_call(): pl.pallas_call(kernel, in_specs=[vmem] * every, out_specs=[vmem] * len(ou...  4.68 us
  transfers between devices with their start and end apart: 61, of which 22 were waited for; matrix products, arithmetic and copies ran while one was open for 4% of the time, Pallas kernels for 22%

profile of v1, /device:TPU:1, one launch (start us, length us, event | category | flops | bytes accessed | tf_op | source)
XLA Modules:
  0.0 196.3 jit_solution(810386803384980955)
XLA Ops:
  0.6 1.7 fusion.14.refs_0_
  2.3 2.1 %collective-permute-start.1 = (f32[384,128]{1,0:T(8,128)S(1)}, f32[384,128]{1,0:T(8,128)S(1)}, u32[]{:S(2)}, u32[]{:S(2)}) collective-permute-start(f32[384,128]{1,0:T(8,128)S(1)} %fusion.14.refs_0_), channel_id=1, source_target_pairs={{0,2},{1,3},{2,0},{3,1},{4,6},{5,7},{6,4},{7,5},{8,10},{9,11},{10,... | collective-permute-start | bytes 589832 | tf_op jit(solution)/shard_map/stage_0_0/ppermute | solution.py:43
  4.5 1.7 fusion.12.refs_0_
  7.4 1.7 fusion.10.refs_0_
  12.2 1.4 copy-done
  16.7 3.3 %collective-permute-done.2.rest_1_ = f32[768,128]{1,0:T(8,128)S(1)} collective-permute-done((f32[768,128]{1,0:T(8,128)S(1)}, f32[768,128]{1,0:T(8,128)S(1)}, u32[]{:S(2)}, u32[]{:S(2)}) %collective-permute-start.2) | collective-permute-done | bytes 393248 | tf_op jit(solution)/shard_map/stage_0_3/ppermute | solution.py:43
  20.1 3.1 %stage_0_8.1 = (f32[1536,128]{1,0:T(8,128)S(1)}, f32[1536,128]{1,0:T(8,128)S(1)}) custom-call(s32[3]{0:T(128)S(1)} %pad_add_fusion.me, s32[48]{0:T(128)S(1)} %reshape.26.pattern, bf16[24,128,256]{2,1,0:T(8,128)(2,1)S(1)} %get-tuple-element.219.a_hi, bf16[24,128,256]{2,1,0:T(8,128)(2,1)S(1)} %get-tuple-element.220.a_lo, f32[768,128]{1,0:T(8,128)S(1)} %stage_0_3.1.rest_0_, ...), custom_call_target="tpu_custom_call" | custom-call | flops 16000000000 | tf_op jit(solution)/shard_map/stage_0_8/pallas_call | solution.py:280
  23.2 3.5 %collective-permute-start.3 = (f32[1536,128]{1,0:T(8,128)S(1)}, f32[1536,128]{1,0:T(8,128)S(1)}, u32[]{:S(2)}, u32[]{:S(2)}) collective-permute-start(f32[1536,128]{1,0:T(8,128)S(1)} %get-tuple-element.224), channel_id=1, source_target_pairs={{0,4},{4,0},{8,12},{12,8},{16,20},{20,16},{24,28},{28,24},{1,5},{5... | collective-permute-start | bytes 2359304 | tf_op jit(solution)/shard_map/stage_0_8/ppermute | solution.py:43
  26.7 3.1 %stage_1_9.1 = (f32[1536,128]{1,0:T(8,128)S(1)}, f32[1536,128]{1,0:T(8,128)S(1)}) custom-call(s32[3]{0:T(128)S(1)} %pad_add_fusion.me, s32[48]{0:T(128)S(1)} %reshape.26.pattern, bf16[24,128,256]{2,1,0:T(8,128)(2,1)S(1)} %get-tuple-element.219.a_hi, bf16[24,128,256]{2,1,0:T(8,128)(2,1)S(1)} %get-tuple-element.220.a_lo, f32[768,128]{1,0:T(8,128)S(1)} %stage_1_4.1.rest_0_, ...), custom_call_target="tpu_custom_call" | custom-call | flops 16000000000 | tf_op jit(solution)/shard_map/stage_1_9/pallas_call | solution.py:280
  33.7 6.2 %collective-permute-done.7.refs_0_.refs_1_ = f32[384,512]{1,0:T(8,128)S(1)} collective-permute-done((f32[384,512]{1,0:T(8,128)}, f32[384,512]{1,0:T(8,128)S(1)}, u32[]{:S(2)}, u32[]{:S(2)}) %collective-permute-start.7) | collective-permute-done | bytes 786464 | tf_op jit(solution)/shard_map/stage_x_7/ppermute | solution.py:43
  40.5 2.4 %collective-permute-start.9 = (f32[384,128]{1,0:T(8,128)S(1)}, f32[384,128]{1,0:T(8,128)S(1)}, u32[]{:S(2)}, u32[]{:S(2)}) collective-permute-start(f32[384,128]{1,0:T(8,128)S(1)} %get-tuple-element.246), channel_id=1, source_target_pairs={{0,16},{4,20},{8,24},{12,28},{16,0},{20,4},{24,8},{28,12},{1,17},{... | collective-permute-start | bytes 589832 | tf_op jit(solution)/shard_map/stage_0_13/ppermute | solution.py:43
  42.9 3.1 %stage_2_14.1 = (f32[1536,128]{1,0:T(8,128)S(1)}, f32[1536,128]{1,0:T(8,128)S(1)}) custom-call(s32[3]{0:T(128)S(1)} %pad_add_fusion.me, s32[48]{0:T(128)S(1)} %reshape.26.pattern, bf16[24,128,256]{2,1,0:T(8,128)(2,1)S(1)} %get-tuple-element.219.a_hi, bf16[24,128,256]{2,1,0:T(8,128)(2,1)S(1)} %get-tuple-element.220.a_lo, f32[768,128]{1,0:T(8,128)S(1)} %stage_2_6.1.rest_0_, ...), custom_call_target="tpu_custom_call" | custom-call | flops 16000000000 | tf_op jit(solution)/shard_map/stage_2_14/pallas_call | solution.py:280
  46.0 2.5 %collective-permute-start.11 = (f32[1536,128]{1,0:T(8,128)S(1)}, f32[1536,128]{1,0:T(8,128)S(1)}, u32[]{:S(2)}, u32[]{:S(2)}) collective-permute-start(f32[1536,128]{1,0:T(8,128)S(1)} %get-tuple-element.250), channel_id=1, source_target_pairs={{0,4},{4,0},{8,12},{12,8},{16,20},{20,16},{24,28},{28,24},{1,5},{5... | collective-permute-start | bytes 2359304 | tf_op jit(solution)/shard_map/stage_2_14/ppermute | solution.py:43
  48.5 4.4 %collective-permute-done.12.refs_1_ = f32[768,128]{1,0:T(8,128)S(1)} collective-permute-done((f32[768,128]{1,0:T(8,128)S(1)}, f32[768,128]{1,0:T(8,128)S(1)}, u32[]{:S(2)}, u32[]{:S(2)}) %collective-permute-start.12) | collective-permute-done | bytes 393248 | tf_op jit(solution)/shard_map/stage_1_11/ppermute | solution.py:43
  53.0 1.5 collective-permute-start.13
  54.7 2.3 %collective-permute-start.16 = (f32[768,128]{1,0:T(8,128)S(1)}, f32[768,128]{1,0:T(8,128)S(1)}, u32[]{:S(2)}, u32[]{:S(2)}) collective-permute-start(f32[768,128]{1,0:T(8,128)S(1)} %get-tuple-element.258), channel_id=1, source_target_pairs={{0,8},{4,12},{8,0},{12,4},{16,24},{20,28},{24,16},{28,20},{1,9},{5... | collective-permute-start | bytes 1179656 | tf_op jit(solution)/shard_map/stage_2_16/ppermute | solution.py:43
  57.2 5.0 %collective-permute-done.15.refs_3_ = f32[384,512]{1,0:T(8,128)S(1)} collective-permute-done((f32[384,512]{1,0:T(8,128)S(1)}, f32[384,512]{1,0:T(8,128)S(1)}, u32[]{:S(2)}, u32[]{:S(2)}) %collective-permute-start.15) | collective-permute-done | bytes 786464 | tf_op jit(solution)/shard_map/stage_x_12/ppermute | solution.py:43
  62.2 2.2 %stage_x_18.1 = (bf16[512,1536]{1,0:T(8,128)(2,1)S(1)}, bf16[512,1536]{1,0:T(8,128)(2,1)S(1)}) custom-call(f32[384,512]{1,0:T(8,128)} %refs_0_, f32[384,512]{1,0:T(8,128)S(1)} %collective-permute-done.7.refs_0_.refs_1_, f32[384,512]{1,0:T(8,128)} %collective-permute-done.14.refs_2_, f32[384,512]{1,0:T(8,128)S(1)} %collective-permute-done.15.refs_3_), custom_call_target="tpu_custom_call" | custom-call | flops 16000000000 | tf_op jit(solution)/shard_map/stage_x_18/pallas_call | solution.py:341
  64.4 1.7 fusion.8.refs_0_
  66.1 1.5 collective-permute-start.18
  67.8 2.4 %collective-permute-start.20 = (f32[384,128]{1,0:T(8,128)S(1)}, f32[384,128]{1,0:T(8,128)S(1)}, u32[]{:S(2)}, u32[]{:S(2)}) collective-permute-start(f32[384,128]{1,0:T(8,128)S(1)} %get-tuple-element.282.refs_0_), channel_id=1, source_target_pairs={{0,16},{4,20},{8,24},{12,28},{16,0},{20,4},{24,8},{28,12},{1,17},{... | collective-permute-start | bytes 589832 | tf_op jit(solution)/shard_map/stage_1_20/ppermute | solution.py:43
  70.2 2.2 %collective-permute-done.16.refs_1_ = f32[768,128]{1,0:T(8,128)S(1)} collective-permute-done((f32[768,128]{1,0:T(8,128)S(1)}, f32[768,128]{1,0:T(8,128)S(1)}, u32[]{:S(2)}, u32[]{:S(2)}) %collective-permute-start.16) | collective-permute-done | bytes 393248 | tf_op jit(solution)/shard_map/stage_2_16/ppermute | solution.py:43
  72.8 2.0 collective-permute-start.19
  74.8 1.7 collective-permute-start.23
  76.5 10.3 %collective-permute-done.20.refs_1_ = f32[384,128]{1,0:T(8,128)S(1)} collective-permute-done((f32[384,128]{1,0:T(8,128)S(1)}, f32[384,128]{1,0:T(8,128)S(1)}, u32[]{:S(2)}, u32[]{:S(2)}) %collective-permute-start.20) | collective-permute-done | bytes 196640 | tf_op jit(solution)/shard_map/stage_1_20/ppermute | solution.py:43
  86.9 3.1 %stage_3_25.1 = (f32[1536,128]{1,0:T(8,128)S(1)}, f32[1536,128]{1,0:T(8,128)S(1)}) custom-call(s32[3]{0:T(128)S(1)} %pad_add_fusion.me, s32[48]{0:T(128)S(1)} %reshape.26.pattern, bf16[24,128,256]{2,1,0:T(8,128)(2,1)S(1)} %get-tuple-element.219.a_hi, bf16[24,128,256]{2,1,0:T(8,128)(2,1)S(1)} %get-tuple-element.220.a_lo, f32[768,128]{1,0:T(8,128)S(1)} %stage_3_22.1.rest_0_, ...), custom_call_target="tpu_custom_call" | custom-call | flops 16000000000 | tf_op jit(solution)/shard_map/stage_3_25/pallas_call | solution.py:280
  91.3 1.9 collective-permute-start.25
  93.3 8.6 %collective-permute-start.26 = (f32[1536,128]{1,0:T(8,128)S(1)}, f32[1536,128]{1,0:T(8,128)S(1)}, u32[]{:S(2)}, u32[]{:S(2)}) collective-permute-start(f32[1536,128]{1,0:T(8,128)S(1)} %stage_0_27.1.rest_0_), channel_id=1, source_target_pairs={{0,4},{4,0},{8,12},{12,8},{16,20},{20,16},{24,28},{28,24},{1,5},{5... | collective-permute-start | bytes 2359304 | tf_op jit(solution)/shard_map/stage_0_27/ppermute | solution.py:43
  102.2 1.7 collective-permute-done.26.rest_1_
  103.9 3.7 %stage_0_29.1 = (f32[768,128]{1,0:T(8,128)S(1)}, f32[768,128]{1,0:T(8,128)S(1)}, f32[8,128]{1,0:T(8,128)S(1)}) custom-call(s32[3]{0:T(128)S(1)} %pad_add_fusion.me, s32[48]{0:T(128)S(1)} %reshape.26.pattern, bf16[24,256,128]{2,1,0:T(8,128)(2,1)S(1)} %get-tuple-element.233.a_hi, bf16[24,256,128]{2,1,0:T(8,128)(2,1)S(1)} %get-tuple-element.234.a_lo, ...), custom_call_target="tpu_custom_call" | custom-call | flops 16000000000 | tf_op jit(solution)/shard_map/stage_0_29/pallas_call | solution.py:280
  107.8 5.6 %collective-permute-done.24.refs_1_ = f32[768,128]{1,0:T(8,128)S(1)} collective-permute-done((f32[768,128]{1,0:T(8,128)S(1)}, f32[768,128]{1,0:T(8,128)S(1)}, u32[]{:S(2)}, u32[]{:S(2)}) %collective-permute-start.24) | collective-permute-done | bytes 393248 | tf_op jit(solution)/shard_map/stage_3_28/ppermute | solution.py:43
  114.5 5.6 %collective-permute-start.30 = (f32[1536,128]{1,0:T(8,128)S(1)}, f32[1536,128]{1,0:T(8,128)S(1)}, u32[]{:S(2)}, u32[]{:S(2)}) collective-permute-start(f32[1536,128]{1,0:T(8,128)S(1)} %stage_1_32.1.rest_0_), channel_id=1, source_target_pairs={{0,4},{4,0},{8,12},{12,8},{16,20},{20,16},{24,28},{28,24},{1,5},{5... | collective-permute-start | bytes 2359304 | tf_op jit(solution)/shard_map/stage_1_32/ppermute | solution.py:43
  122.1 3.7 %stage_1_34.1 = (f32[768,128]{1,0:T(8,128)S(1)}, f32[768,128]{1,0:T(8,128)S(1)}, f32[8,128]{1,0:T(8,128)S(1)}) custom-call(s32[3]{0:T(128)S(1)} %pad_add_fusion.me, s32[48]{0:T(128)S(1)} %reshape.26.pattern, bf16[24,256,128]{2,1,0:T(8,128)(2,1)S(1)} %get-tuple-element.233.a_hi, bf16[24,256,128]{2,1,0:T(8,128)(2,1)S(1)} %get-tuple-element.234.a_lo, ...), custom_call_target="tpu_custom_call" | custom-call | flops 16000000000 | tf_op jit(solution)/shard_map/stage_1_34/pallas_call | solution.py:280
  127.1 2.7 %collective-permute-start.35 = (f32[384,128]{1,0:T(8,128)S(1)}, f32[384,128]{1,0:T(8,128)S(1)}, u32[]{:S(2)}, u32[]{:S(2)}) collective-permute-start(f32[384,128]{1,0:T(8,128)S(1)} %get-tuple-element.341.refs_0_), channel_id=1, source_target_pairs={{0,16},{4,20},{8,24},{12,28},{16,0},{20,4},{24,8},{28,12},{1,17},{... | collective-permute-start | bytes 589832 | tf_op jit(solution)/shard_map/stage_3_36/ppermute | solution.py:43
  130.7 3.9 %stage_2_37.1 = (f32[768,128]{1,0:T(8,128)S(1)}, f32[768,128]{1,0:T(8,128)S(1)}, f32[8,128]{1,0:T(8,128)S(1)}) custom-call(s32[3]{0:T(128)S(1)} %pad_add_fusion.me, s32[48]{0:T(128)S(1)} %reshape.26.pattern, bf16[24,256,128]{2,1,0:T(8,128)(2,1)S(1)} %get-tuple-element.233.a_hi, bf16[24,256,128]{2,1,0:T(8,128)(2,1)S(1)} %get-tuple-element.234.a_lo, ...), custom_call_target="tpu_custom_call" | custom-call | flops 16000000000 | tf_op jit(solution)/shard_map/stage_2_37/pallas_call | solution.py:280
  134.6 2.4 %collective-permute-start.38 = (f32[768,128]{1,0:T(8,128)S(1)}, f32[768,128]{1,0:T(8,128)S(1)}, u32[]{:S(2)}, u32[]{:S(2)}) collective-permute-start(f32[768,128]{1,0:T(8,128)S(1)} %get-tuple-element.338.rest_5_), channel_id=1, source_target_pairs={{0,1},{1,0},{2,3},{3,2},{4,5},{5,4},{6,7},{7,6},{8,9},{9,8},{10,11... | collective-permute-start | bytes 1179656 | tf_op jit(solution)/shard_map/stage_2_37/ppermute | solution.py:43
  137.0 4.7 %stage_v_38.1 = (f32[256,384]{1,0:T(8,128)S(1)}, f32[256,384]{1,0:T(8,128)S(1)}) custom-call(s32[3]{0:T(128)S(1)} %pad_add_fusion.me, bf16[512,1536]{1,0:T(8,128)(2,1)S(1)} %get-tuple-element.370.x_hi, bf16[512,1536]{1,0:T(8,128)(2,1)S(1)} %get-tuple-element.371.x_lo, f32[768,128]{1,0:T(8,128)S(1)} %get-tuple-element.333.refs_0_.rest_0_, ...), custom_call_target="tpu_custom_call" | custom-call | flops 16000000000 | tf_op jit(solution)/shard_map/stage_v_38/pallas_call | solution.py:380
  143.9 1.5 collective-permute-start.43
  146.6 6.6 %collective-permute-done.37.refs_1_ = f32[768,128]{1,0:T(8,128)S(1)} collective-permute-done((f32[768,128]{1,0:T(8,128)S(1)}, f32[768,128]{1,0:T(8,128)S(1)}, u32[]{:S(2)}, u32[]{:S(2)}) %collective-permute-start.37) | collective-permute-done | bytes 393248 | tf_op jit(solution)/shard_map/stage_3_39/ppermute | solution.py:43
  156.1 3.7 %stage_3_47.1 = (f32[768,128]{1,0:T(8,128)S(1)}, f32[768,128]{1,0:T(8,128)S(1)}, f32[8,128]{1,0:T(8,128)S(1)}) custom-call(s32[3]{0:T(128)S(1)} %pad_add_fusion.me, s32[48]{0:T(128)S(1)} %reshape.26.pattern, bf16[24,256,128]{2,1,0:T(8,128)(2,1)S(1)} %get-tuple-element.233.a_hi, bf16[24,256,128]{2,1,0:T(8,128)(2,1)S(1)} %get-tuple-element.234.a_lo, ...), custom_call_target="tpu_custom_call" | custom-call | flops 16000000000 | tf_op jit(solution)/shard_map/stage_3_47/pallas_call | solution.py:280
  160.8 2.0 %stage_w_48.1 = (f32[256,128]{1,0:T(8,128)S(1)}, f32[256,128]{1,0:T(8,128)S(1)}) custom-call(s32[3]{0:T(128)S(1)} %pad_add_fusion.me, bf16[512,1536]{1,0:T(8,128)(2,1)S(1)} %get-tuple-element.370.x_hi, bf16[512,1536]{1,0:T(8,128)(2,1)S(1)} %get-tuple-element.371.x_lo, f32[768,128]{1,0:T(8,128)S(1)} %get-tuple-element.390.rest_0_.refs_0_, ...), custom_call_target="tpu_custom_call" | custom-call | flops 16000000000 | tf_op jit(solution)/shard_map/stage_w_48/pallas_call | solution.py:380
  166.1 1.9 collective-permute-done.46.refs_1_
  168.7 2.1 %collective-permute-start.47 = (f32[64,384]{1,0:T(8,128)S(1)}, f32[64,384]{1,0:T(8,128)S(1)}, u32[]{:S(2)}, u32[]{:S(2)}) collective-permute-start(f32[64,384]{1,0:T(8,128)S(1)} %stage_v_52.1.refs_0_), channel_id=1, source_target_pairs={{0,16},{4,20},{8,24},{12,28},{16,0},{20,4},{24,8},{28,12},{1,17},{... | collective-permute-start | bytes 294920 | tf_op jit(solution)/shard_map/stage_v_52/ppermute | solution.py:43
  172.5 2.6 %collective-permute-done.49.refs_1_ = f32[64,128]{1,0:T(8,128)S(1)} collective-permute-done((f32[64,128]{1,0:T(8,128)S(1)}, f32[64,128]{1,0:T(8,128)S(1)}, u32[]{:S(2)}, u32[]{:S(2)}) %collective-permute-start.49) | collective-permute-done | bytes 32800 | tf_op jit(solution)/shard_map/stage_w_53/ppermute | solution.py:43
  175.1 1.4 collective-permute-start.53
  182.6 2.2 %collective-permute-done.54.refs_1_ = f32[128,384]{1,0:T(8,128)S(1)} collective-permute-done((f32[128,384]{1,0:T(8,128)S(1)}, f32[128,384]{1,0:T(8,128)S(1)}, u32[]{:S(2)}, u32[]{:S(2)}) %collective-permute-start.54) | collective-permute-done | bytes 196640 | tf_op jit(solution)/shard_map/stage_v_60/ppermute | solution.py:43
  184.8 6.2 %collective-permute-start.57 = (f32[256,384]{1,0:T(8,128)S(1)}, f32[256,384]{1,0:T(8,128)S(1)}, u32[]{:S(2)}, u32[]{:S(2)}) collective-permute-start(f32[256,384]{1,0:T(8,128)S(1)} %stage_v_63.1.refs_0_), channel_id=1, source_target_pairs={{0,4},{4,0},{8,12},{12,8},{16,20},{20,16},{24,28},{28,24},{1,5},{5... | collective-permute-start | bytes 1179656 | tf_op jit(solution)/shard_map/stage_v_63/ppermute | solution.py:43
  192.3 1.7 fusion
  (168 shorter events, 42.5 us)
Async XLA Ops:
  2.3 7.4 %collective-permute-start.1 = (f32[384,128]{1,0:T(8,128)S(1)}, f32[384,128]{1,0:T(8,128)S(1)}, u32[]{:S(2)}, u32[]{:S(2)}) collective-permute-start(f32[384,128]{1,0:T(8,128)S(1)} %fusion.14.refs_0_), channel_id=1, source_target_pairs={{0,2},{1,3},{2,0},{3,1},{4,6},{5,7},{6,4},{7,5},{8,10},{9,11},{10,... | collective-permute-start | bytes 589832 | tf_op jit(solution)/shard_map/stage_0_0/ppermute | solution.py:43
  6.1 5.5 %collective-permute-start = (f32[384,128]{1,0:T(8,128)S(1)}, f32[384,128]{1,0:T(8,128)S(1)}, u32[]{:S(2)}, u32[]{:S(2)}) collective-permute-start(f32[384,128]{1,0:T(8,128)S(1)} %fusion.12.refs_0_), channel_id=1, source_target_pairs={{0,1},{1,0},{2,3},{3,2},{4,5},{5,4},{6,7},{7,6},{8,9},{9,8},{10,11... | collective-permute-start | bytes 589832 | tf_op jit(solution)/shard_map/stage_1_1/ppermute | solution.py:43
  9.1 5.6 %collective-permute-start.6 = (f32[384,128]{1,0:T(8,128)S(1)}, f32[384,128]{1,0:T(8,128)S(1)}, u32[]{:S(2)}, u32[]{:S(2)}) collective-permute-start(f32[384,128]{1,0:T(8,128)S(1)} %fusion.10.refs_0_), channel_id=1, source_target_pairs={{0,2},{1,3},{2,0},{3,1},{4,6},{5,7},{6,4},{7,5},{8,10},{9,11},{10,... | collective-permute-start | bytes 589832 | tf_op jit(solution)/shard_map/stage_2_2/ppermute | solution.py:43
  9.8 10.2 %collective-permute-start.2 = (f32[768,128]{1,0:T(8,128)S(1)}, f32[768,128]{1,0:T(8,128)S(1)}, u32[]{:S(2)}, u32[]{:S(2)}) collective-permute-start(f32[768,128]{1,0:T(8,128)S(1)} %stage_0_3.1.rest_0_), channel_id=1, source_target_pairs={{0,1},{1,0},{2,3},{3,2},{4,5},{5,4},{6,7},{7,6},{8,9},{9,8},{10,11... | collective-permute-start | bytes 1179656 | tf_op jit(solution)/shard_map/stage_0_3/ppermute | solution.py:43
  11.7 14.9 %collective-permute-start.4 = (f32[768,128]{1,0:T(8,128)S(1)}, f32[768,128]{1,0:T(8,128)S(1)}, u32[]{:S(2)}, u32[]{:S(2)}) collective-permute-start(f32[768,128]{1,0:T(8,128)S(1)} %stage_1_4.1.rest_0_), channel_id=1, source_target_pairs={{0,2},{1,3},{2,0},{3,1},{4,6},{5,7},{6,4},{7,5},{8,10},{9,11},{10,... | collective-permute-start | bytes 1179656 | tf_op jit(solution)/shard_map/stage_1_4/ppermute | solution.py:43
  14.8 28.1 %collective-permute-start.10 = (f32[768,128]{1,0:T(8,128)S(1)}, f32[768,128]{1,0:T(8,128)S(1)}, u32[]{:S(2)}, u32[]{:S(2)}) collective-permute-start(f32[768,128]{1,0:T(8,128)S(1)} %stage_2_6.1.rest_0_), channel_id=1, source_target_pairs={{0,1},{1,0},{2,3},{3,2},{4,5},{5,4},{6,7},{7,6},{8,9},{9,8},{10,11... | collective-permute-start | bytes 1179656 | tf_op jit(solution)/shard_map/stage_2_6/ppermute | solution.py:43
  16.1 23.8 %collective-permute-start.7 = (f32[384,512]{1,0:T(8,128)}, f32[384,512]{1,0:T(8,128)S(1)}, u32[]{:S(2)}, u32[]{:S(2)}) collective-permute-start(f32[384,512]{1,0:T(8,128)} %refs_0_), channel_id=1, source_target_pairs={{0,2},{1,3},{2,0},{3,1},{4,6},{5,7},{6,4},{7,5},{8,10},{9,11},{10,... | collective-permute-start | bytes 2359304 | tf_op jit(solution)/shard_map/stage_x_7/ppermute | solution.py:43
  16.3 40.8 %collective-permute-start.14 = (f32[384,512]{1,0:T(8,128)}, f32[384,512]{1,0:T(8,128)}, u32[]{:S(2)}, u32[]{:S(2)}) collective-permute-start(f32[384,512]{1,0:T(8,128)} %refs_0_), channel_id=1, source_target_pairs={{0,1},{1,0},{2,3},{3,2},{4,5},{5,4},{6,7},{7,6},{8,9},{9,8},{10,11... | collective-permute-start | bytes 2359304 | tf_op jit(solution)/shard_map/stage_x_7/ppermute | solution.py:43
  23.2 6.7 %collective-permute-start.3 = (f32[1536,128]{1,0:T(8,128)S(1)}, f32[1536,128]{1,0:T(8,128)S(1)}, u32[]{:S(2)}, u32[]{:S(2)}) collective-permute-start(f32[1536,128]{1,0:T(8,128)S(1)} %get-tuple-element.224), channel_id=1, source_target_pairs={{0,4},{4,0},{8,12},{12,8},{16,20},{20,16},{24,28},{28,24},{1,5},{5... | collective-permute-start | bytes 2359304 | tf_op jit(solution)/shard_map/stage_0_8/ppermute | solution.py:43
  30.0 10.4 %collective-permute-start.5 = (f32[768,128]{1,0:T(8,128)S(1)}, f32[768,128]{1,0:T(8,128)S(1)}, u32[]{:S(2)}, u32[]{:S(2)}) collective-permute-start(f32[768,128]{1,0:T(8,128)S(1)} %get-tuple-element.232), channel_id=1, source_target_pairs={{0,8},{4,12},{8,0},{12,4},{16,24},{20,28},{24,16},{28,20},{1,9},{5... | collective-permute-start | bytes 1179656 | tf_op jit(solution)/shard_map/stage_0_10/ppermute | solution.py:43
  32.3 20.7 %collective-permute-start.12 = (f32[768,128]{1,0:T(8,128)S(1)}, f32[768,128]{1,0:T(8,128)S(1)}, u32[]{:S(2)}, u32[]{:S(2)}) collective-permute-start(f32[768,128]{1,0:T(8,128)S(1)} %get-tuple-element.241), channel_id=1, source_target_pairs={{0,8},{4,12},{8,0},{12,4},{16,24},{20,28},{24,16},{28,20},{1,9},{5... | collective-permute-start | bytes 1179656 | tf_op jit(solution)/shard_map/stage_1_11/ppermute | solution.py:43
  39.9 22.2 %collective-permute-start.15 = (f32[384,512]{1,0:T(8,128)S(1)}, f32[384,512]{1,0:T(8,128)S(1)}, u32[]{:S(2)}, u32[]{:S(2)}) collective-permute-start(f32[384,512]{1,0:T(8,128)S(1)} %stage_x_12.1), channel_id=1, source_target_pairs={{0,1},{1,0},{2,3},{3,2},{4,5},{5,4},{6,7},{7,6},{8,9},{9,8},{10,11... | collective-permute-start | bytes 2359304 | tf_op jit(solution)/shard_map/stage_x_12/ppermute | solution.py:43
  40.5 16.4 %collective-permute-start.9 = (f32[384,128]{1,0:T(8,128)S(1)}, f32[384,128]{1,0:T(8,128)S(1)}, u32[]{:S(2)}, u32[]{:S(2)}) collective-permute-start(f32[384,128]{1,0:T(8,128)S(1)} %get-tuple-element.246), channel_id=1, source_target_pairs={{0,16},{4,20},{8,24},{12,28},{16,0},{20,4},{24,8},{28,12},{1,17},{... | collective-permute-start | bytes 589832 | tf_op jit(solution)/shard_map/stage_0_13/ppermute | solution.py:43
  46.0 8.5 %collective-permute-start.11 = (f32[1536,128]{1,0:T(8,128)S(1)}, f32[1536,128]{1,0:T(8,128)S(1)}, u32[]{:S(2)}, u32[]{:S(2)}) collective-permute-start(f32[1536,128]{1,0:T(8,128)S(1)} %get-tuple-element.250), channel_id=1, source_target_pairs={{0,4},{4,0},{8,12},{12,8},{16,20},{20,16},{24,28},{28,24},{1,5},{5... | collective-permute-start | bytes 2359304 | tf_op jit(solution)/shard_map/stage_2_14/ppermute | solution.py:43
  53.0 14.6 %collective-permute-start.13 = (f32[384,128]{1,0:T(8,128)S(1)}, f32[384,128]{1,0:T(8,128)S(1)}, u32[]{:S(2)}, u32[]{:S(2)}) collective-permute-start(f32[384,128]{1,0:T(8,128)S(1)} %get-tuple-element.254), channel_id=1, source_target_pairs={{0,16},{4,20},{8,24},{12,28},{16,0},{20,4},{24,8},{28,12},{1,17},{... | collective-permute-start | bytes 589832 | tf_op jit(solution)/shard_map/stage_1_15/ppermute | solution.py:43
  54.7 17.8 %collective-permute-start.16 = (f32[768,128]{1,0:T(8,128)S(1)}, f32[768,128]{1,0:T(8,128)S(1)}, u32[]{:S(2)}, u32[]{:S(2)}) collective-permute-start(f32[768,128]{1,0:T(8,128)S(1)} %get-tuple-element.258), channel_id=1, source_target_pairs={{0,8},{4,12},{8,0},{12,4},{16,24},{20,28},{24,16},{28,20},{1,9},{5... | collective-permute-start | bytes 1179656 | tf_op jit(solution)/shard_map/stage_2_16/ppermute | solution.py:43
  57.1 17.7 %collective-permute-start.21 = (f32[384,128]{1,0:T(8,128)S(1)}, f32[384,128]{1,0:T(8,128)S(1)}, u32[]{:S(2)}, u32[]{:S(2)}) collective-permute-start(f32[384,128]{1,0:T(8,128)S(1)} %get-tuple-element.280.refs_0_), channel_id=1, source_target_pairs={{0,16},{4,20},{8,24},{12,28},{16,0},{20,4},{24,8},{28,12},{1,17},{... | collective-permute-start | bytes 589832 | tf_op jit(solution)/shard_map/stage_0_17/ppermute | solution.py:43
  66.1 6.6 %collective-permute-start.18 = (f32[384,128]{1,0:T(8,128)S(1)}, f32[384,128]{1,0:T(8,128)S(1)}, u32[]{:S(2)}, u32[]{:S(2)}) collective-permute-start(f32[384,128]{1,0:T(8,128)S(1)} %fusion.8.refs_0_), channel_id=1, source_target_pairs={{0,1},{1,0},{2,3},{3,2},{4,5},{5,4},{6,7},{7,6},{8,9},{9,8},{10,11... | collective-permute-start | bytes 589832 | tf_op jit(solution)/shard_map/stage_3_19/ppermute | solution.py:43
  67.8 18.9 %collective-permute-start.20 = (f32[384,128]{1,0:T(8,128)S(1)}, f32[384,128]{1,0:T(8,128)S(1)}, u32[]{:S(2)}, u32[]{:S(2)}) collective-permute-start(f32[384,128]{1,0:T(8,128)S(1)} %get-tuple-element.282.refs_0_), channel_id=1, source_target_pairs={{0,16},{4,20},{8,24},{12,28},{16,0},{20,4},{24,8},{28,12},{1,17},{... | collective-permute-start | bytes 589832 | tf_op jit(solution)/shard_map/stage_1_20/ppermute | solution.py:43
  72.5 18.7 %collective-permute-start.17 = (f32[384,128]{1,0:T(8,128)S(1)}, f32[384,128]{1,0:T(8,128)S(1)}, u32[]{:S(2)}, u32[]{:S(2)}) collective-permute-start(f32[384,128]{1,0:T(8,128)S(1)} %get-tuple-element.277), channel_id=1, source_target_pairs={{0,16},{4,20},{8,24},{12,28},{16,0},{20,4},{24,8},{28,12},{1,17},{... | collective-permute-start | bytes 589832 | tf_op jit(solution)/shard_map/stage_2_21/ppermute | solution.py:43
  72.8 14.1 %collective-permute-start.19 = (f32[768,128]{1,0:T(8,128)S(1)}, f32[768,128]{1,0:T(8,128)S(1)}, u32[]{:S(2)}, u32[]{:S(2)}) collective-permute-start(f32[768,128]{1,0:T(8,128)S(1)} %stage_3_22.1.rest_0_), channel_id=1, source_target_pairs={{0,2},{1,3},{2,0},{3,1},{4,6},{5,7},{6,4},{7,5},{8,10},{9,11},{10,... | collective-permute-start | bytes 1179656 | tf_op jit(solution)/shard_map/stage_3_22/ppermute | solution.py:43
  74.8 18.4 %collective-permute-start.23 = (f32[768,128]{1,0:T(8,128)S(1)}, f32[768,128]{1,0:T(8,128)S(1)}, u32[]{:S(2)}, u32[]{:S(2)}) collective-permute-start(f32[768,128]{1,0:T(8,128)S(1)} %stage_0_23.1.refs_0_), channel_id=1, source_target_pairs={{0,8},{4,12},{8,0},{12,4},{16,24},{20,28},{24,16},{28,20},{1,9},{5... | collective-permute-start | bytes 1179656 | tf_op jit(solution)/shard_map/stage_0_23/ppermute | solution.py:43
  86.8 27.6 %collective-permute-start.29 = (f32[768,128]{1,0:T(8,128)S(1)}, f32[768,128]{1,0:T(8,128)S(1)}, u32[]{:S(2)}, u32[]{:S(2)}) collective-permute-start(f32[768,128]{1,0:T(8,128)S(1)} %stage_1_24.1.refs_0_), channel_id=1, source_target_pairs={{0,8},{4,12},{8,0},{12,4},{16,24},{20,28},{24,16},{28,20},{1,9},{5... | collective-permute-start | bytes 1179656 | tf_op jit(solution)/shard_map/stage_1_24/ppermute | solution.py:43
  90.0 11.9 %collective-permute-start.22 = (f32[1536,128]{1,0:T(8,128)S(1)}, f32[1536,128]{1,0:T(8,128)S(1)}, u32[]{:S(2)}, u32[]{:S(2)}) collective-permute-start(f32[1536,128]{1,0:T(8,128)S(1)} %get-tuple-element.287), channel_id=1, source_target_pairs={{0,4},{4,0},{8,12},{12,8},{16,20},{20,16},{24,28},{28,24},{1,5},{5... | collective-permute-start | bytes 2359304 | tf_op jit(solution)/shard_map/stage_3_25/ppermute | solution.py:43
  91.3 16.3 %collective-permute-start.25 = (f32[384,128]{1,0:T(8,128)S(1)}, f32[384,128]{1,0:T(8,128)S(1)}, u32[]{:S(2)}, u32[]{:S(2)}) collective-permute-start(f32[384,128]{1,0:T(8,128)S(1)} %get-tuple-element.303.refs_0_), channel_id=1, source_target_pairs={{0,16},{4,20},{8,24},{12,28},{16,0},{20,4},{24,8},{28,12},{1,17},{... | collective-permute-start | bytes 589832 | tf_op jit(solution)/shard_map/stage_2_26/ppermute | solution.py:43
  93.3 10.5 %collective-permute-start.26 = (f32[1536,128]{1,0:T(8,128)S(1)}, f32[1536,128]{1,0:T(8,128)S(1)}, u32[]{:S(2)}, u32[]{:S(2)}) collective-permute-start(f32[1536,128]{1,0:T(8,128)S(1)} %stage_0_27.1.rest_0_), channel_id=1, source_target_pairs={{0,4},{4,0},{8,12},{12,8},{16,20},{20,16},{24,28},{28,24},{1,5},{5... | collective-permute-start | bytes 2359304 | tf_op jit(solution)/shard_map/stage_0_27/ppermute | solution.py:43
  102.1 11.3 %collective-permute-start.24 = (f32[768,128]{1,0:T(8,128)S(1)}, f32[768,128]{1,0:T(8,128)S(1)}, u32[]{:S(2)}, u32[]{:S(2)}) collective-permute-start(f32[768,128]{1,0:T(8,128)S(1)} %get-tuple-element.297), channel_id=1, source_target_pairs={{0,8},{4,12},{8,0},{12,4},{16,24},{20,28},{24,16},{28,20},{1,9},{5... | collective-permute-start | bytes 1179656 | tf_op jit(solution)/shard_map/stage_3_28/ppermute | solution.py:43
  107.6 12.6 %collective-permute-start.31 = (f32[768,128]{1,0:T(8,128)S(1)}, f32[768,128]{1,0:T(8,128)S(1)}, u32[]{:S(2)}, u32[]{:S(2)}) collective-permute-start(f32[768,128]{1,0:T(8,128)S(1)} %get-tuple-element.334.rest_1_), channel_id=1, source_target_pairs={{0,1},{1,0},{2,3},{3,2},{4,5},{5,4},{6,7},{7,6},{8,9},{9,8},{10,11... | collective-permute-start | bytes 1179656 | tf_op jit(solution)/shard_map/stage_0_29/ppermute | solution.py:43
  107.7 18.4 %collective-permute-start.28 = (f32[768,128]{1,0:T(8,128)S(1)}, f32[768,128]{1,0:T(8,128)S(1)}, u32[]{:S(2)}, u32[]{:S(2)}) collective-permute-start(f32[768,128]{1,0:T(8,128)S(1)} %stage_2_30.1.refs_0_), channel_id=1, source_target_pairs={{0,8},{4,12},{8,0},{12,4},{16,24},{20,28},{24,16},{28,20},{1,9},{5... | collective-permute-start | bytes 1179656 | tf_op jit(solution)/shard_map/stage_2_30/ppermute | solution.py:43
  113.4 13.5 %collective-permute-start.27 = (f32[384,128]{1,0:T(8,128)S(1)}, f32[384,128]{1,0:T(8,128)S(1)}, u32[]{:S(2)}, u32[]{:S(2)}) collective-permute-start(f32[384,128]{1,0:T(8,128)S(1)} %get-tuple-element.308), channel_id=1, source_target_pairs={{0,16},{4,20},{8,24},{12,28},{16,0},{20,4},{24,8},{28,12},{1,17},{... | collective-permute-start | bytes 589832 | tf_op jit(solution)/shard_map/stage_3_31/ppermute | solution.py:43
  114.5 7.5 %collective-permute-start.30 = (f32[1536,128]{1,0:T(8,128)S(1)}, f32[1536,128]{1,0:T(8,128)S(1)}, u32[]{:S(2)}, u32[]{:S(2)}) collective-permute-start(f32[1536,128]{1,0:T(8,128)S(1)} %stage_1_32.1.rest_0_), channel_id=1, source_target_pairs={{0,4},{4,0},{8,12},{12,8},{16,20},{20,16},{24,28},{28,24},{1,5},{5... | collective-permute-start | bytes 2359304 | tf_op jit(solution)/shard_map/stage_1_32/ppermute | solution.py:43
  120.9 56.5 %collective-permute-start.32 = (f32[384,128]{1,0:T(8,128)}, f32[384,128]{1,0:T(8,128)}, u32[]{:S(2)}, u32[]{:S(2)}) collective-permute-start(f32[384,128]{1,0:T(8,128)} %get-tuple-element.314), channel_id=1, source_target_pairs={{0,2},{1,3},{2,0},{3,1},{4,6},{5,7},{6,4},{7,5},{8,10},{9,11},{10,... | collective-permute-start | bytes 589832 | tf_op jit(solution)/shard_map/stage_0_33/ppermute | solution.py:43
  125.8 18.1 %collective-permute-start.39 = (f32[768,128]{1,0:T(8,128)S(1)}, f32[768,128]{1,0:T(8,128)S(1)}, u32[]{:S(2)}, u32[]{:S(2)}) collective-permute-start(f32[768,128]{1,0:T(8,128)S(1)} %get-tuple-element.336.rest_3_), channel_id=1, source_target_pairs={{0,2},{1,3},{2,0},{3,1},{4,6},{5,7},{6,4},{7,5},{8,10},{9,11},{10,... | collective-permute-start | bytes 1179656 | tf_op jit(solution)/shard_map/stage_1_34/ppermute | solution.py:43
  127.1 15.3 %collective-permute-start.35 = (f32[384,128]{1,0:T(8,128)S(1)}, f32[384,128]{1,0:T(8,128)S(1)}, u32[]{:S(2)}, u32[]{:S(2)}) collective-permute-start(f32[384,128]{1,0:T(8,128)S(1)} %get-tuple-element.341.refs_0_), channel_id=1, source_target_pairs={{0,16},{4,20},{8,24},{12,28},{16,0},{20,4},{24,8},{28,12},{1,17},{... | collective-permute-start | bytes 589832 | tf_op jit(solution)/shard_map/stage_3_36/ppermute | solution.py:43
  134.6 11.7 %collective-permute-start.38 = (f32[768,128]{1,0:T(8,128)S(1)}, f32[768,128]{1,0:T(8,128)S(1)}, u32[]{:S(2)}, u32[]{:S(2)}) collective-permute-start(f32[768,128]{1,0:T(8,128)S(1)} %get-tuple-element.338.rest_5_), channel_id=1, source_target_pairs={{0,1},{1,0},{2,3},{3,2},{4,5},{5,4},{6,7},{7,6},{8,9},{9,8},{10,11... | collective-permute-start | bytes 1179656 | tf_op jit(solution)/shard_map/stage_2_37/ppermute | solution.py:43
  142.4 10.8 %collective-permute-start.37 = (f32[768,128]{1,0:T(8,128)S(1)}, f32[768,128]{1,0:T(8,128)S(1)}, u32[]{:S(2)}, u32[]{:S(2)}) collective-permute-start(f32[768,128]{1,0:T(8,128)S(1)} %stage_3_39.1.refs_0_), channel_id=1, source_target_pairs={{0,8},{4,12},{8,0},{12,4},{16,24},{20,28},{24,16},{28,20},{1,9},{5... | collective-permute-start | bytes 1179656 | tf_op jit(solution)/shard_map/stage_3_39/ppermute | solution.py:43
  143.8 10.5 %collective-permute-start.36 = (f32[128,384]{1,0:T(8,128)S(1)}, f32[128,384]{1,0:T(8,128)S(1)}, u32[]{:S(2)}, u32[]{:S(2)}) collective-permute-start(f32[128,384]{1,0:T(8,128)S(1)} %get-tuple-element.346), channel_id=1, source_target_pairs={{0,1},{1,0},{2,3},{3,2},{4,5},{5,4},{6,7},{7,6},{8,9},{9,8},{10,11... | collective-permute-start | bytes 589832 | tf_op jit(solution)/shard_map/stage_v_40/ppermute | solution.py:43
  143.9 11.3 %collective-permute-start.43 = (f32[384,128]{1,0:T(8,128)S(1)}, f32[384,128]{1,0:T(8,128)S(1)}, u32[]{:S(2)}, u32[]{:S(2)}) collective-permute-start(f32[384,128]{1,0:T(8,128)S(1)} %get-tuple-element.350), channel_id=1, source_target_pairs={{0,1},{1,0},{2,3},{3,2},{4,5},{5,4},{6,7},{7,6},{8,9},{9,8},{10,11... | collective-permute-start | bytes 589832 | tf_op jit(solution)/shard_map/stage_1_41/ppermute | solution.py:43
  146.3 8.9 %collective-permute-start.42 = (f32[384,128]{1,0:T(8,128)S(1)}, f32[384,128]{1,0:T(8,128)S(1)}, u32[]{:S(2)}, u32[]{:S(2)}) collective-permute-start(f32[384,128]{1,0:T(8,128)S(1)} %get-tuple-element.354), channel_id=1, source_target_pairs={{0,2},{1,3},{2,0},{3,1},{4,6},{5,7},{6,4},{7,5},{8,10},{9,11},{10,... | collective-permute-start | bytes 589832 | tf_op jit(solution)/shard_map/stage_2_42/ppermute | solution.py:43
  154.3 9.3 %collective-permute-start.40 = (f32[64,384]{1,0:T(8,128)S(1)}, f32[64,384]{1,0:T(8,128)S(1)}, u32[]{:S(2)}, u32[]{:S(2)}) collective-permute-start(f32[64,384]{1,0:T(8,128)S(1)} %get-tuple-element.360), channel_id=1, source_target_pairs={{0,2},{1,3},{2,0},{3,1},{4,6},{5,7},{6,4},{7,5},{8,10},{9,11},{10,... | collective-permute-start | bytes 294920 | tf_op jit(solution)/shard_map/stage_v_44/ppermute | solution.py:43
  159.8 11.9 %collective-permute-start.50 = (f32[768,128]{1,0:T(8,128)S(1)}, f32[768,128]{1,0:T(8,128)S(1)}, u32[]{:S(2)}, u32[]{:S(2)}) collective-permute-start(f32[768,128]{1,0:T(8,128)S(1)} %get-tuple-element.373.rest_1_), channel_id=1, source_target_pairs={{0,2},{1,3},{2,0},{3,1},{4,6},{5,7},{6,4},{7,5},{8,10},{9,11},{10,... | collective-permute-start | bytes 1179656 | tf_op jit(solution)/shard_map/stage_3_47/ppermute | solution.py:43
  163.6 5.1 %collective-permute-start.44 = (f32[64,384]{1,0:T(8,128)S(1)}, f32[64,384]{1,0:T(8,128)S(1)}, u32[]{:S(2)}, u32[]{:S(2)}) collective-permute-start(f32[64,384]{1,0:T(8,128)S(1)} %stage_v_49.1.refs_0_), channel_id=1, source_target_pairs={{0,8},{4,12},{8,0},{12,4},{16,24},{20,28},{24,16},{28,20},{1,9},{5... | collective-permute-start | bytes 294920 | tf_op jit(solution)/shard_map/stage_v_49/ppermute | solution.py:43
  165.2 15.5 %collective-permute-start.56 = (f32[8,512]{1,0:T(8,128)S(1)}, f32[8,512]{1,0:T(8,128)S(1)}, u32[]{:S(2)}, u32[]{:S(2)}) collective-permute-start(f32[8,512]{1,0:T(8,128)S(1)} %constant_dynamic-update-slice_fusion), channel_id=1, source_target_pairs={{0,1},{1,0},{2,3},{3,2},{4,5},{5,4},{6,7},{7,6},{8,9},{9,8},{10,11... | collective-permute-start | bytes 49160 | tf_op jit(solution)/shard_map/stage_b_58/ppermute | solution.py:43
  168.7 7.9 %collective-permute-start.47 = (f32[64,384]{1,0:T(8,128)S(1)}, f32[64,384]{1,0:T(8,128)S(1)}, u32[]{:S(2)}, u32[]{:S(2)}) collective-permute-start(f32[64,384]{1,0:T(8,128)S(1)} %stage_v_52.1.refs_0_), channel_id=1, source_target_pairs={{0,16},{4,20},{8,24},{12,28},{16,0},{20,4},{24,8},{28,12},{1,17},{... | collective-permute-start | bytes 294920 | tf_op jit(solution)/shard_map/stage_v_52/ppermute | solution.py:43
  171.9 19.1 %collective-permute-start.51 = (f32[384,128]{1,0:T(8,128)S(1)}, f32[384,128]{1,0:T(8,128)S(1)}, u32[]{:S(2)}, u32[]{:S(2)}) collective-permute-start(f32[384,128]{1,0:T(8,128)S(1)} %get-tuple-element.393), channel_id=1, source_target_pairs={{0,1},{1,0},{2,3},{3,2},{4,5},{5,4},{6,7},{7,6},{8,9},{9,8},{10,11... | collective-permute-start | bytes 589832 | tf_op jit(solution)/shard_map/stage_3_54/ppermute | solution.py:43
  180.7 11.0 %collective-permute-start.58 = (f32[8,512]{1,0:T(8,128)S(1)}, f32[8,512]{1,0:T(8,128)S(1)}, u32[]{:S(2)}, u32[]{:S(2)}) collective-permute-start(f32[8,512]{1,0:T(8,128)S(1)} %add.15), channel_id=1, source_target_pairs={{0,2},{1,3},{2,0},{3,1},{4,6},{5,7},{6,4},{7,5},{8,10},{9,11},{10,... | collective-permute-start | bytes 49160 | tf_op jit(solution)/shard_map/stage_b_61/ppermute | solution.py:43
  182.0 9.1 %collective-permute-start.59 = (f32[128,128]{1,0:T(8,128)S(1)}, f32[128,128]{1,0:T(8,128)S(1)}, u32[]{:S(2)}, u32[]{:S(2)}) collective-permute-start(f32[128,128]{1,0:T(8,128)S(1)} %stage_w_62.1.refs_0_), channel_id=1, source_target_pairs={{0,1},{1,0},{2,3},{3,2},{4,5},{5,4},{6,7},{7,6},{8,9},{9,8},{10,11... | collective-permute-start | bytes 196616 | tf_op jit(solution)/shard_map/stage_w_62/ppermute | solution.py:43
  184.8 9.2 %collective-permute-start.57 = (f32[256,384]{1,0:T(8,128)S(1)}, f32[256,384]{1,0:T(8,128)S(1)}, u32[]{:S(2)}, u32[]{:S(2)}) collective-permute-start(f32[256,384]{1,0:T(8,128)S(1)} %stage_v_63.1.refs_0_), channel_id=1, source_target_pairs={{0,4},{4,0},{8,12},{12,8},{16,20},{20,16},{24,28},{28,24},{1,5},{5... | collective-permute-start | bytes 1179656 | tf_op jit(solution)/shard_map/stage_v_63/ppermute | solution.py:43
  (20 other events, 67.7 us)

commit v2 on v1

--- a/solution.py
+++ b/solution.py
@@ -12,12 +12,13 @@
 BF16 = jnp.bfloat16
 HIGH = lax.Precision.HIGH
 WIDTHS = (1, 1, 1, 1)
-EARLY = 3
-WAVES = (False, False, True)
-ORDER = ('01201p2x0101x02120x3123013203023101232v3v123v123wvwwvw3wv0bw', 'vbwv3wbvw')
+EARLY = 2
+WAVES = (False, False, False)
+ORDER = ('01201p32010132x021303x123120131x20302v230v30wvw21wv3wv2wvbwv', 'wbvw3vb1w')
 SMALL_VMEM = 12 * 1024 * 1024
 VMEM_LIMIT = 40 * 1024 * 1024
 STAGE = 16000000000.0
+TAIL = 0.3
 
 
 def cost(stages=1.0):
@@ -46,7 +47,7 @@
 ROWS = 64
 
 
-def rows_call(fn, out_rows, xs, extra=()):
+def rows_call(fn, out_rows, xs, extra=(), stages=1.0):
     width = xs[0].shape[1]
     outs = [jax.ShapeDtypeStruct((rows, width), F32) for rows in out_rows]
     count, every = len(xs), len(xs) + len(extra)
@@ -61,7 +62,7 @@
         out_specs=[vmem] * len(outs),
         out_shape=outs,
         compiler_params=pltpu.CompilerParams(vmem_limit_bytes=SMALL_VMEM),
-        cost_estimate=cost(),
+        cost_estimate=cost(stages),
     )(*xs, *extra)
 
 
@@ -73,7 +74,7 @@
         step(pl.multiple_of(k * unit, unit), unit)
 
 
-def add_halves(keep, got):
+def add_halves(keep, got, stages=1.0):
     half = keep.shape[0] // 2
 
     def fn(ins, _, outs):
@@ -85,10 +86,10 @@
 
             blocks_of(half, step)
 
-    return rows_call(fn, [half, half], [keep, got])
-
-
-def stack(parts):
+    return rows_call(fn, [half, half], [keep, got], stages=stages)
+
+
+def stack(parts, stages=1.0):
     def fn(ins, _, outs):
         base = 0
         for ref in ins:
@@ -99,10 +100,10 @@
             blocks_of(ref.shape[0], step)
             base += ref.shape[0]
 
-    return rows_call(fn, [sum(p.shape[0] for p in parts)], parts)[0]
-
-
-def add_all(terms):
+    return rows_call(fn, [sum(p.shape[0] for p in parts)], parts, stages=stages)[0]
+
+
+def add_all(terms, stages=1.0):
     def fn(ins, _, outs):
         def step(at, unit):
             rows = pl.ds(at, unit)
@@ -113,7 +114,7 @@
 
         blocks_of(outs[0].shape[0], step)
 
-    return rows_call(fn, [terms[0].shape[0]], terms)[0]
+    return rows_call(fn, [terms[0].shape[0]], terms, stages=stages)[0]
 
 
 def activate(keep, got, upstream, bias):
@@ -145,7 +146,7 @@
         return xs
 
 
-def gather_stages(line, x, dims, out, waves):
+def gather_stages(line, x, dims, out, waves, stages=1.0):
     parts = [x]
     if waves and len(dims) == 2:
         first, second = swap(x, dims[0]), swap(x, dims[1])
@@ -157,13 +158,13 @@
             if len(parts) > 1:
                 yield
                 parts = line.enter(parts)
-                parts = [line.leave(stack(parts))]
+                parts = [line.leave(stack(parts, stages))]
             parts = parts + [swap(parts[0], dim)]
     yield
     out.extend(line.enter(parts))
 
 
-def halve_stages(line, keep, send, dims, out):
+def halve_stages(line, keep, send, dims, out, stages=1.0):
     for k, dim in enumerate(dims):
         got = swap(send, dim)
         yield
@@ -171,7 +172,7 @@
         if k + 1 == len(dims):
             out.extend((keep, got))
         else:
-            keep, send = line.leave(add_halves(keep, got))
+            keep, send = line.leave(add_halves(keep, got, stages))
 
 
 def slot_of(owner, me, labels):
@@ -393,19 +394,23 @@
     order = slot_order(labels)
     unit = out.shape[0] // len(order)
     half = len(order) // 2
-    for k, s in enumerate(order):
-        part = p_refs[k // half][pl.ds((k % half) * unit, unit), :]
-        out[pl.ds(pl.multiple_of((me[2] ^ s) * unit, unit), unit), :] = part * scale
+    base = 0
+    for g in range(0, len(p_refs), 2):
+        width = p_refs[g].shape[1]
+        for k, s in enumerate(order):
+            part = p_refs[g + k // half][pl.ds((k % half) * unit, unit), :]
+            out[pl.ds(pl.multiple_of((me[2] ^ s) * unit, unit), unit), pl.ds(base, width)] = part * scale
+        base += width
 
 
 def place(me, parts, labels, scale):
-    rows, width = parts[0].shape
+    rows = 2 * parts[0].shape[0]
     vmem = pl.BlockSpec(memory_space=pltpu.VMEM)
     return pl.pallas_call(
         functools.partial(place_kernel, scale, labels),
         in_specs=[pl.BlockSpec(memory_space=pltpu.SMEM)] + [vmem] * len(parts),
         out_specs=vmem,
-        out_shape=jax.ShapeDtypeStruct((rows * len(parts), width), F32),
+        out_shape=jax.ShapeDtypeStruct((rows, sum(p.shape[1] for p in parts[::2])), F32),
         compiler_params=pltpu.CompilerParams(vmem_limit_bytes=VMEM_LIMIT),
         cost_estimate=cost(),
     )(me, *parts)
@@ -435,8 +440,8 @@
 
     tiles = []
 
-    outputs, column_grads, halves, sums = [None] * count, [None] * count, [None] * count, [None] * count
-    turned = []
+    outputs, halves, sums = [None] * count, [None] * count, [None] * count
+    input_grads, turned = [], []
 
     def chunk_bits(c):
         return narrow_bits if c % 2 == 0 else narrow_bits[::-1]
@@ -478,7 +483,9 @@
         halves[c] = (keep, send)
         found = []
         yield from halve_stages(line, keep, send, n_dims, found)
-        column_grads[c] = line.leave(add_all(found))
+        column_grad = line.leave(add_all(found))
+        term = lax.dot_general(column_grad, weight[:, cols], (((1,), (1,)), ((), ())), precision=HIGH)
+        input_grads[:] = [sum(input_grads, term)]
 
     def tile_parts():
         own = line.enter(adj_tiles).reshape(block_rows, per_group, size, size)
@@ -499,19 +506,19 @@
         x_hi, x_lo, *parts = line.enter(list(turned) + parts)
         keep, send = line.leave(outer(me, x_hi, x_lo, parts, sum_labels, orders))
         found = []
-        yield from halve_stages(line, keep, send, [core] + narrow_dims, found)
-        total = line.leave(add_all(found))
+        yield from halve_stages(line, keep, send, [core] + narrow_dims, found, TAIL)
+        total = line.leave(add_all(found, TAIL))
         for dim in z_dims:
             got = swap(total, dim)
             yield
             total, got = line.enter((total, got))
-            total = line.leave(add_all([total, got]))
+            total = line.leave(add_all([total, got], TAIL))
         parts = []
-        yield from gather_stages(line, total, narrow_dims[::-1], parts, False)
-        parts = line.leave(stack(parts))
+        yield from gather_stages(line, total, narrow_dims[::-1], parts, False, TAIL)
+        parts = line.leave(stack(parts, TAIL))
         got = swap(parts, core)
         yield
-        out.append(line.leave(place(me, line.enter([parts, got]), sum_labels, grad_scale)))
+        out.extend(line.leave(line.enter([parts, got])))
 
     def bias_stages(out):
         while None in halves:
@@ -539,12 +546,10 @@
     for stages in lines.values():
         for _ in stages:
             pass
-    column_grad = jnp.concatenate(column_grads, axis=1)
-    input_grad = lax.dot_general(column_grad, weight, (((1,), (1,)), ((), ())), precision=HIGH)
     return (
         jnp.concatenate(outputs, axis=1),
-        input_grad,
-        jnp.concatenate(early_parts + weight_parts, axis=1),
+        input_grads[0],
+        place(me, early_parts + weight_parts, sum_labels, grad_scale),
         bias_out[0],
     )
 

time: 197 us -> 195 us (0.990)
    ppermute x61 -> x60, starting transfers between devices: 78.9 us -> 78.1 us  [swap(): return lax.ppermute(x, axis, [(i, i ^ bit) for i in range(size)])]
    ppermute x61 -> x60, waiting for transfers between devices: 59.8 us -> 59.6 us  [swap(): return lax.ppermute(x, axis, [(i, i ^ bit) for i in range(size)])]
  transfers between devices with their start and end apart: 61 -> 60, of which waited for: 22 -> 22; matrix products, arithmetic and copies ran while one was open for 4% -> 5% of each run, Pallas kernels for 22% -> 21%
where the time goes in v2:
time: 195 us; the launch traced here: 194 us
  starting transfers between devices  78.1 us (40%)
  waiting for transfers between devices  59.6 us (31%)
  Pallas kernels  43.1 us (22%)
  matrix products  8.96 us (5%)
    ppermute x60, starting transfers between devices, swap(): return lax.ppermute(x, axis, [(i, i ^ bit) for i in range(size)])  78.1 us
    ppermute x60, waiting for transfers between devices, swap(): return lax.ppermute(x, axis, [(i, i ^ bit) for i in range(size)])  59.6 us
    pallas_call x8, Pallas kernels, tile_call(): pl.pallas_call(kernel, grid_spec=pltpu.PrefetchScalarGridSpec(num_scalar_...  28 us
    pallas_call x2, Pallas kernels, outer(): pl.pallas_call(functools.partial(outer_kernel, labels, orders), in_specs=...  7.17 us
    dot_general x4, matrix products, chunk(): jnp.dot(own, weight[:, cols], precision=HIGH, preferred_element_type=F32)  6.03 us
    pallas_call x47, Pallas kernels, rows_call(): pl.pallas_call(kernel, in_specs=[vmem] * every, out_specs=[vmem] * len(ou...  4.28 us
  transfers between devices with their start and end apart: 60, of which 22 were waited for; matrix products, arithmetic and copies ran while one was open for 5% of the time, Pallas kernels for 21%

profile of v2, /device:TPU:1, one launch (start us, length us, event | category | flops | bytes accessed | tf_op | source)
XLA Modules:
  0.0 194.3 jit_solution(73010682995234360)
XLA Ops:
  0.7 1.7 fusion.11.refs_0_
  2.4 2.1 %collective-permute-start.1 = (f32[384,128]{1,0:T(8,128)S(1)}, f32[384,128]{1,0:T(8,128)S(1)}, u32[]{:S(2)}, u32[]{:S(2)}) collective-permute-start(f32[384,128]{1,0:T(8,128)S(1)} %fusion.11.refs_0_), channel_id=1, source_target_pairs={{0,2},{1,3},{2,0},{3,1},{4,6},{5,7},{6,4},{7,5},{8,10},{9,11},{10,... | collective-permute-start | bytes 589832 | tf_op jit(solution)/shard_map/stage_0_0/ppermute | solution.py:44
  4.5 1.4 fusion.7.refs_0_
  7.3 1.4 fusion.4.refs_0_
  14.6 1.4 fusion.1.refs_0_
  17.7 2.4 %collective-permute-done.2.rest_1_ = f32[768,128]{1,0:T(8,128)S(1)} collective-permute-done((f32[768,128]{1,0:T(8,128)S(1)}, f32[768,128]{1,0:T(8,128)S(1)}, u32[]{:S(2)}, u32[]{:S(2)}) %collective-permute-start.2) | collective-permute-done | bytes 393248 | tf_op jit(solution)/shard_map/stage_0_3/ppermute | solution.py:44
  20.1 3.1 %stage_0_8.1 = (f32[1536,128]{1,0:T(8,128)S(1)}, f32[1536,128]{1,0:T(8,128)S(1)}) custom-call(s32[3]{0:T(128)S(1)} %pad_add_fusion.me, s32[48]{0:T(128)S(1)} %reshape.26.pattern, bf16[24,128,256]{2,1,0:T(8,128)(2,1)S(1)} %get-tuple-element.218.a_hi, bf16[24,128,256]{2,1,0:T(8,128)(2,1)S(1)} %get-tuple-element.219.a_lo, f32[768,128]{1,0:T(8,128)S(1)} %stage_0_3.1.rest_0_, ...), custom_call_target="tpu_custom_call" | custom-call | flops 16000000000 | tf_op jit(solution)/shard_map/stage_0_8/pallas_call | solution.py:281
  23.3 3.0 %collective-permute-start.4 = (f32[1536,128]{1,0:T(8,128)S(1)}, f32[1536,128]{1,0:T(8,128)S(1)}, u32[]{:S(2)}, u32[]{:S(2)}) collective-permute-start(f32[1536,128]{1,0:T(8,128)S(1)} %get-tuple-element.228), channel_id=1, source_target_pairs={{0,4},{4,0},{8,12},{12,8},{16,20},{20,16},{24,28},{28,24},{1,5},{5... | collective-permute-start | bytes 2359304 | tf_op jit(solution)/shard_map/stage_0_8/ppermute | solution.py:44
  26.3 3.1 %stage_1_9.1 = (f32[1536,128]{1,0:T(8,128)S(1)}, f32[1536,128]{1,0:T(8,128)S(1)}) custom-call(s32[3]{0:T(128)S(1)} %pad_add_fusion.me, s32[48]{0:T(128)S(1)} %reshape.26.pattern, bf16[24,128,256]{2,1,0:T(8,128)(2,1)S(1)} %get-tuple-element.218.a_hi, bf16[24,128,256]{2,1,0:T(8,128)(2,1)S(1)} %get-tuple-element.219.a_lo, f32[768,128]{1,0:T(8,128)S(1)} %stage_1_4.1.rest_0_, ...), custom_call_target="tpu_custom_call" | custom-call | flops 16000000000 | tf_op jit(solution)/shard_map/stage_1_9/pallas_call | solution.py:281
  29.6 1.4 collective-permute-start.6
  31.9 1.4 collective-permute-start.11
  34.6 3.1 %stage_2_13.1 = (f32[1536,128]{1,0:T(8,128)S(1)}, f32[1536,128]{1,0:T(8,128)S(1)}) custom-call(s32[3]{0:T(128)S(1)} %pad_add_fusion.me, s32[48]{0:T(128)S(1)} %reshape.26.pattern, bf16[24,128,256]{2,1,0:T(8,128)(2,1)S(1)} %get-tuple-element.218.a_hi, bf16[24,128,256]{2,1,0:T(8,128)(2,1)S(1)} %get-tuple-element.219.a_lo, f32[768,128]{1,0:T(8,128)S(1)} %stage_2_7.1.rest_0_, ...), custom_call_target="tpu_custom_call" | custom-call | flops 16000000000 | tf_op jit(solution)/shard_map/stage_2_13/pallas_call | solution.py:281
  40.0 2.4 %collective-permute-start.7 = (f32[384,128]{1,0:T(8,128)S(1)}, f32[384,128]{1,0:T(8,128)S(1)}, u32[]{:S(2)}, u32[]{:S(2)}) collective-permute-start(f32[384,128]{1,0:T(8,128)S(1)} %get-tuple-element.240), channel_id=1, source_target_pairs={{0,16},{4,20},{8,24},{12,28},{16,0},{20,4},{24,8},{28,12},{1,17},{... | collective-permute-start | bytes 589832 | tf_op jit(solution)/shard_map/stage_0_15/ppermute | solution.py:44
  42.5 1.4 collective-permute-start.17
  43.9 8.7 %collective-permute-done.11.refs_1_ = f32[768,128]{1,0:T(8,128)S(1)} collective-permute-done((f32[768,128]{1,0:T(8,128)S(1)}, f32[768,128]{1,0:T(8,128)S(1)}, u32[]{:S(2)}, u32[]{:S(2)}) %collective-permute-start.11) | collective-permute-done | bytes 393248 | tf_op jit(solution)/shard_map/stage_1_11/ppermute | solution.py:44
  52.6 1.5 collective-permute-start.14
  54.1 3.1 %stage_3_18.1 = (f32[1536,128]{1,0:T(8,128)S(1)}, f32[1536,128]{1,0:T(8,128)S(1)}) custom-call(s32[3]{0:T(128)S(1)} %pad_add_fusion.me, s32[48]{0:T(128)S(1)} %reshape.26.pattern, bf16[24,128,256]{2,1,0:T(8,128)(2,1)S(1)} %get-tuple-element.218.a_hi, bf16[24,128,256]{2,1,0:T(8,128)(2,1)S(1)} %get-tuple-element.219.a_lo, f32[768,128]{1,0:T(8,128)S(1)} %stage_3_12.1.rest_0_, ...), custom_call_target="tpu_custom_call" | custom-call | flops 16000000000 | tf_op jit(solution)/shard_map/stage_3_18/pallas_call | solution.py:281
  57.2 2.6 %collective-permute-start.16 = (f32[1536,128]{1,0:T(8,128)S(1)}, f32[1536,128]{1,0:T(8,128)S(1)}, u32[]{:S(2)}, u32[]{:S(2)}) collective-permute-start(f32[1536,128]{1,0:T(8,128)S(1)} %get-tuple-element.262), channel_id=1, source_target_pairs={{0,4},{4,0},{8,12},{12,8},{16,20},{20,16},{24,28},{28,24},{1,5},{5... | collective-permute-start | bytes 2359304 | tf_op jit(solution)/shard_map/stage_3_18/ppermute | solution.py:44
  61.9 2.3 %collective-permute-start.20 = (f32[768,128]{1,0:T(8,128)S(1)}, f32[768,128]{1,0:T(8,128)S(1)}, u32[]{:S(2)}, u32[]{:S(2)}) collective-permute-start(f32[768,128]{1,0:T(8,128)S(1)} %get-tuple-element.271), channel_id=1, source_target_pairs={{0,8},{4,12},{8,0},{12,4},{16,24},{20,28},{24,16},{28,20},{1,9},{5... | collective-permute-start | bytes 1179656 | tf_op jit(solution)/shard_map/stage_3_20/ppermute | solution.py:44
  65.4 2.2 %collective-permute-start.19 = (f32[384,128]{1,0:T(8,128)S(1)}, f32[384,128]{1,0:T(8,128)S(1)}, u32[]{:S(2)}, u32[]{:S(2)}) collective-permute-start(f32[384,128]{1,0:T(8,128)S(1)} %get-tuple-element.286.refs_0_), channel_id=1, source_target_pairs={{0,16},{4,20},{8,24},{12,28},{16,0},{20,4},{24,8},{28,12},{1,17},{... | collective-permute-start | bytes 589832 | tf_op jit(solution)/shard_map/stage_1_22/ppermute | solution.py:44
  68.0 14.8 %collective-permute-done.20.refs_1_ = f32[768,128]{1,0:T(8,128)S(1)} collective-permute-done((f32[768,128]{1,0:T(8,128)S(1)}, f32[768,128]{1,0:T(8,128)S(1)}, u32[]{:S(2)}, u32[]{:S(2)}) %collective-permute-start.20) | collective-permute-done | bytes 393248 | tf_op jit(solution)/shard_map/stage_3_20/ppermute | solution.py:44
  84.0 2.3 %collective-permute-start.22 = (f32[768,128]{1,0:T(8,128)S(1)}, f32[768,128]{1,0:T(8,128)S(1)}, u32[]{:S(2)}, u32[]{:S(2)}) collective-permute-start(f32[768,128]{1,0:T(8,128)S(1)} %stage_1_25.1.refs_0_), channel_id=1, source_target_pairs={{0,8},{4,12},{8,0},{12,4},{16,24},{20,28},{24,16},{28,20},{1,9},{5... | collective-permute-start | bytes 1179656 | tf_op jit(solution)/shard_map/stage_1_25/ppermute | solution.py:44
  86.2 10.6 %collective-permute-done.18.refs_1_ = f32[384,128]{1,0:T(8,128)S(1)} collective-permute-done((f32[384,128]{1,0:T(8,128)S(1)}, f32[384,128]{1,0:T(8,128)S(1)}, u32[]{:S(2)}, u32[]{:S(2)}) %collective-permute-start.18) | collective-permute-done | bytes 196640 | tf_op jit(solution)/shard_map/stage_2_23/ppermute | solution.py:44
  97.2 1.9 %collective-permute-start.29 = (f32[768,128]{1,0:T(8,128)S(1)}, f32[768,128]{1,0:T(8,128)S(1)}, u32[]{:S(2)}, u32[]{:S(2)}) collective-permute-start(f32[768,128]{1,0:T(8,128)S(1)} %stage_0_27.1.refs_0_), channel_id=1, source_target_pairs={{0,8},{4,12},{8,0},{12,4},{16,24},{20,28},{24,16},{28,20},{1,9},{5... | collective-permute-start | bytes 1179656 | tf_op jit(solution)/shard_map/stage_0_27/ppermute | solution.py:44
  99.1 2.7 %collective-permute-done.22.refs_1_ = f32[768,128]{1,0:T(8,128)S(1)} collective-permute-done((f32[768,128]{1,0:T(8,128)S(1)}, f32[768,128]{1,0:T(8,128)S(1)}, u32[]{:S(2)}, u32[]{:S(2)}) %collective-permute-start.22) | collective-permute-done | bytes 393248 | tf_op jit(solution)/shard_map/stage_1_25/ppermute | solution.py:44
  102.0 5.6 %collective-permute-start.24 = (f32[1536,128]{1,0:T(8,128)S(1)}, f32[1536,128]{1,0:T(8,128)S(1)}, u32[]{:S(2)}, u32[]{:S(2)}) collective-permute-start(f32[1536,128]{1,0:T(8,128)S(1)} %stage_1_28.1.rest_0_), channel_id=1, source_target_pairs={{0,4},{4,0},{8,12},{12,8},{16,20},{20,16},{24,28},{28,24},{1,5},{5... | collective-permute-start | bytes 2359304 | tf_op jit(solution)/shard_map/stage_1_28/ppermute | solution.py:44
  109.5 4.4 %stage_1_30.1 = (f32[768,128]{1,0:T(8,128)S(1)}, f32[768,128]{1,0:T(8,128)}, f32[8,128]{1,0:T(8,128)S(1)}) custom-call(s32[3]{0:T(128)S(1)} %pad_add_fusion.me, s32[48]{0:T(128)S(1)} %reshape.26.pattern, bf16[24,256,128]{2,1,0:T(8,128)(2,1)S(1)} %get-tuple-element.220.a_hi, bf16[24,256,128]{2,1,0:T(8,128)(2,1)S(1)} %get-tuple-element.221.a_lo, ...), custom_call_target="tpu_custom_call" | custom-call | flops 16000000000 | tf_op jit(solution)/shard_map/stage_1_30/pallas_call | solution.py:281
  118.0 3.7 %collective-permute-start.30 = (f32[1536,128]{1,0:T(8,128)S(1)}, f32[1536,128]{1,0:T(8,128)S(1)}, u32[]{:S(2)}, u32[]{:S(2)}) collective-permute-start(f32[1536,128]{1,0:T(8,128)S(1)} %stage_0_33.1.rest_0_), channel_id=1, source_target_pairs={{0,4},{4,0},{8,12},{12,8},{16,20},{20,16},{24,28},{28,24},{1,5},{5... | collective-permute-start | bytes 2359304 | tf_op jit(solution)/shard_map/stage_0_33/ppermute | solution.py:44
  121.8 1.8 collective-permute-done.30.rest_1_
  123.6 3.7 %stage_0_35.1 = (f32[768,128]{1,0:T(8,128)S(1)}, f32[768,128]{1,0:T(8,128)S(1)}, f32[8,128]{1,0:T(8,128)S(1)}) custom-call(s32[3]{0:T(128)S(1)} %pad_add_fusion.me, s32[48]{0:T(128)S(1)} %reshape.26.pattern, bf16[24,256,128]{2,1,0:T(8,128)(2,1)S(1)} %get-tuple-element.220.a_hi, bf16[24,256,128]{2,1,0:T(8,128)(2,1)S(1)} %get-tuple-element.221.a_lo, ...), custom_call_target="tpu_custom_call" | custom-call | flops 16000000000 | tf_op jit(solution)/shard_map/stage_0_35/pallas_call | solution.py:281
  128.6 1.7 collective-permute-start.32
  131.1 3.8 %stage_v_37.1 = (f32[256,256]{1,0:T(8,128)S(1)}, f32[256,256]{1,0:T(8,128)S(1)}) custom-call(s32[3]{0:T(128)S(1)} %pad_add_fusion.me, bf16[512,1536]{1,0:T(8,128)(2,1)S(1)} %get-tuple-element.352.x_hi, bf16[512,1536]{1,0:T(8,128)(2,1)S(1)} %get-tuple-element.353.x_lo, f32[768,128]{1,0:T(8,128)S(1)} %get-tuple-element.337.rest_0_.refs_0_, ...), custom_call_target="tpu_custom_call" | custom-call | flops 16000000000 | tf_op jit(solution)/shard_map/stage_v_37/pallas_call | solution.py:381
  135.3 3.7 %stage_2_38.1 = (f32[768,128]{1,0:T(8,128)S(1)}, f32[768,128]{1,0:T(8,128)S(1)}, f32[8,128]{1,0:T(8,128)S(1)}) custom-call(s32[3]{0:T(128)S(1)} %pad_add_fusion.me, s32[48]{0:T(128)S(1)} %reshape.26.pattern, bf16[24,256,128]{2,1,0:T(8,128)(2,1)S(1)} %get-tuple-element.220.a_hi, bf16[24,256,128]{2,1,0:T(8,128)(2,1)S(1)} %get-tuple-element.221.a_lo, ...), custom_call_target="tpu_custom_call" | custom-call | flops 16000000000 | tf_op jit(solution)/shard_map/stage_2_38/pallas_call | solution.py:281
  141.0 2.7 %collective-permute-start.38 = (f32[384,128]{1,0:T(8,128)S(1)}, f32[384,128]{1,0:T(8,128)S(1)}, u32[]{:S(2)}, u32[]{:S(2)}) collective-permute-start(f32[384,128]{1,0:T(8,128)S(1)} %get-tuple-element.340), channel_id=1, source_target_pairs={{0,2},{1,3},{2,0},{3,1},{4,6},{5,7},{6,4},{7,5},{8,10},{9,11},{10,... | collective-permute-start | bytes 589832 | tf_op jit(solution)/shard_map/stage_0_40/ppermute | solution.py:44
  143.8 1.4 collective-permute-start.40
  145.2 3.7 %stage_3_42.1 = (f32[768,128]{1,0:T(8,128)S(1)}, f32[768,128]{1,0:T(8,128)S(1)}, f32[8,128]{1,0:T(8,128)S(1)}) custom-call(s32[3]{0:T(128)S(1)} %pad_add_fusion.me, s32[48]{0:T(128)S(1)} %reshape.26.pattern, bf16[24,256,128]{2,1,0:T(8,128)(2,1)S(1)} %get-tuple-element.220.a_hi, bf16[24,256,128]{2,1,0:T(8,128)(2,1)S(1)} %get-tuple-element.221.a_lo, ...), custom_call_target="tpu_custom_call" | custom-call | flops 16000000000 | tf_op jit(solution)/shard_map/stage_3_42/pallas_call | solution.py:281
  149.0 3.3 %stage_w_44.1 = (f32[256,256]{1,0:T(8,128)S(1)}, f32[256,256]{1,0:T(8,128)S(1)}) custom-call(s32[3]{0:T(128)S(1)} %pad_add_fusion.me, bf16[512,1536]{1,0:T(8,128)(2,1)S(1)} %get-tuple-element.352.x_hi, bf16[512,1536]{1,0:T(8,128)(2,1)S(1)} %get-tuple-element.353.x_lo, f32[768,128]{1,0:T(8,128)S(1)} %get-tuple-element.368.rest_0_.refs_0_, ...), custom_call_target="tpu_custom_call" | custom-call | flops 16000000000 | tf_op jit(solution)/shard_map/stage_w_44/pallas_call | solution.py:381
  152.4 1.8 collective-permute-start.39
  154.2 1.8 collective-permute-start.46
  162.2 1.5 collective-permute-start.44
  163.9 2.5 %collective-permute-done.44.refs_1_ = f32[64,256]{1,0:T(8,128)S(1)} collective-permute-done((f32[64,256]{1,0:T(8,128)S(1)}, f32[64,256]{1,0:T(8,128)S(1)}, u32[]{:S(2)}, u32[]{:S(2)}) %collective-permute-start.44) | collective-permute-done | bytes 65568 | tf_op jit(solution)/shard_map/stage_w_49/ppermute | solution.py:44
  167.2 2.0 %collective-permute-start.52 = (f32[64,256]{1,0:T(8,128)S(1)}, f32[64,256]{1,0:T(8,128)S(1)}, u32[]{:S(2)}, u32[]{:S(2)}) collective-permute-start(f32[64,256]{1,0:T(8,128)S(1)} %stage_v_53.1.refs_0_), channel_id=1, source_target_pairs={{0,16},{4,20},{8,24},{12,28},{16,0},{20,4},{24,8},{28,12},{1,17},{... | collective-permute-start | bytes 196616 | tf_op jit(solution)/shard_map/stage_v_53/ppermute | solution.py:44
  171.8 4.0 %collective-permute-done.50.refs_1_ = f32[64,256]{1,0:T(8,128)S(1)} collective-permute-done((f32[64,256]{1,0:T(8,128)S(1)}, f32[64,256]{1,0:T(8,128)S(1)}, u32[]{:S(2)}, u32[]{:S(2)}) %collective-permute-start.50) | collective-permute-done | bytes 65568 | tf_op jit(solution)/shard_map/stage_w_55/ppermute | solution.py:44
  177.1 2.2 %collective-permute-done.51.refs_1_ = f32[64,256]{1,0:T(8,128)S(1)} collective-permute-done((f32[64,256]{1,0:T(8,128)S(1)}, f32[64,256]{1,0:T(8,128)S(1)}, u32[]{:S(2)}, u32[]{:S(2)}) %collective-permute-start.51) | collective-permute-done | bytes 65568 | tf_op jit(solution)/shard_map/stage_w_58/ppermute | solution.py:44
  180.9 6.4 %collective-permute-start.56 = (f32[256,256]{1,0:T(8,128)S(1)}, f32[256,256]{1,0:T(8,128)S(1)}, u32[]{:S(2)}, u32[]{:S(2)}) collective-permute-start(f32[256,256]{1,0:T(8,128)S(1)} %stage_v_62.1.refs_0_), channel_id=1, source_target_pairs={{0,4},{4,0},{8,12},{12,8},{16,20},{20,16},{24,28},{28,24},{1,5},{5... | collective-permute-start | bytes 786440 | tf_op jit(solution)/shard_map/stage_v_62/ppermute | solution.py:44
  187.3 2.7 %collective-permute-start.59 = (f32[256,256]{1,0:T(8,128)S(1)}, f32[256,256]{1,0:T(8,128)S(1)}, u32[]{:S(2)}, u32[]{:S(2)}) collective-permute-start(f32[256,256]{1,0:T(8,128)S(1)} %stage_w_63.1.refs_2_), channel_id=1, source_target_pairs={{0,4},{4,0},{8,12},{12,8},{16,20},{20,16},{24,28},{28,24},{1,5},{5... | collective-permute-start | bytes 786440 | tf_op jit(solution)/shard_map/stage_w_63/ppermute | solution.py:44
  191.3 1.4 convolution_add_fusion.2
  192.7 1.6 shard_map.93
  (165 shorter events, 43.5 us)
Async XLA Ops:
  2.4 6.9 %collective-permute-start.1 = (f32[384,128]{1,0:T(8,128)S(1)}, f32[384,128]{1,0:T(8,128)S(1)}, u32[]{:S(2)}, u32[]{:S(2)}) collective-permute-start(f32[384,128]{1,0:T(8,128)S(1)} %fusion.11.refs_0_), channel_id=1, source_target_pairs={{0,2},{1,3},{2,0},{3,1},{4,6},{5,7},{6,4},{7,5},{8,10},{9,11},{10,... | collective-permute-start | bytes 589832 | tf_op jit(solution)/shard_map/stage_0_0/ppermute | solution.py:44
  6.0 5.5 %collective-permute-start = (f32[384,128]{1,0:T(8,128)S(1)}, f32[384,128]{1,0:T(8,128)S(1)}, u32[]{:S(2)}, u32[]{:S(2)}) collective-permute-start(f32[384,128]{1,0:T(8,128)S(1)} %fusion.7.refs_0_), channel_id=1, source_target_pairs={{0,1},{1,0},{2,3},{3,2},{4,5},{5,4},{6,7},{7,6},{8,9},{9,8},{10,11... | collective-permute-start | bytes 589832 | tf_op jit(solution)/shard_map/stage_1_1/ppermute | solution.py:44
  8.7 8.6 %collective-permute-start.3 = (f32[384,128]{1,0:T(8,128)S(1)}, f32[384,128]{1,0:T(8,128)S(1)}, u32[]{:S(2)}, u32[]{:S(2)}) collective-permute-start(f32[384,128]{1,0:T(8,128)S(1)} %fusion.4.refs_0_), channel_id=1, source_target_pairs={{0,2},{1,3},{2,0},{3,1},{4,6},{5,7},{6,4},{7,5},{8,10},{9,11},{10,... | collective-permute-start | bytes 589832 | tf_op jit(solution)/shard_map/stage_2_2/ppermute | solution.py:44
  9.4 10.7 %collective-permute-start.2 = (f32[768,128]{1,0:T(8,128)S(1)}, f32[768,128]{1,0:T(8,128)S(1)}, u32[]{:S(2)}, u32[]{:S(2)}) collective-permute-start(f32[768,128]{1,0:T(8,128)S(1)} %stage_0_3.1.rest_0_), channel_id=1, source_target_pairs={{0,1},{1,0},{2,3},{3,2},{4,5},{5,4},{6,7},{7,6},{8,9},{9,8},{10,11... | collective-permute-start | bytes 1179656 | tf_op jit(solution)/shard_map/stage_0_3/ppermute | solution.py:44
  11.6 14.7 %collective-permute-start.5 = (f32[768,128]{1,0:T(8,128)S(1)}, f32[768,128]{1,0:T(8,128)S(1)}, u32[]{:S(2)}, u32[]{:S(2)}) collective-permute-start(f32[768,128]{1,0:T(8,128)S(1)} %stage_1_4.1.rest_0_), channel_id=1, source_target_pairs={{0,2},{1,3},{2,0},{3,1},{4,6},{5,7},{6,4},{7,5},{8,10},{9,11},{10,... | collective-permute-start | bytes 1179656 | tf_op jit(solution)/shard_map/stage_1_4/ppermute | solution.py:44
  16.0 17.2 %collective-permute-start.8 = (f32[384,128]{1,0:T(8,128)S(1)}, f32[384,128]{1,0:T(8,128)S(1)}, u32[]{:S(2)}, u32[]{:S(2)}) collective-permute-start(f32[384,128]{1,0:T(8,128)S(1)} %fusion.1.refs_0_), channel_id=1, source_target_pairs={{0,1},{1,0},{2,3},{3,2},{4,5},{5,4},{6,7},{7,6},{8,9},{9,8},{10,11... | collective-permute-start | bytes 589832 | tf_op jit(solution)/shard_map/stage_3_6/ppermute | solution.py:44
  17.4 17.3 %collective-permute-start.12 = (f32[768,128]{1,0:T(8,128)S(1)}, f32[768,128]{1,0:T(8,128)S(1)}, u32[]{:S(2)}, u32[]{:S(2)}) collective-permute-start(f32[768,128]{1,0:T(8,128)S(1)} %stage_2_7.1.rest_0_), channel_id=1, source_target_pairs={{0,1},{1,0},{2,3},{3,2},{4,5},{5,4},{6,7},{7,6},{8,9},{9,8},{10,11... | collective-permute-start | bytes 1179656 | tf_op jit(solution)/shard_map/stage_2_7/ppermute | solution.py:44
  23.3 6.2 %collective-permute-start.4 = (f32[1536,128]{1,0:T(8,128)S(1)}, f32[1536,128]{1,0:T(8,128)S(1)}, u32[]{:S(2)}, u32[]{:S(2)}) collective-permute-start(f32[1536,128]{1,0:T(8,128)S(1)} %get-tuple-element.228), channel_id=1, source_target_pairs={{0,4},{4,0},{8,12},{12,8},{16,20},{20,16},{24,28},{28,24},{1,5},{5... | collective-permute-start | bytes 2359304 | tf_op jit(solution)/shard_map/stage_0_8/ppermute | solution.py:44
  29.6 10.3 %collective-permute-start.6 = (f32[768,128]{1,0:T(8,128)S(1)}, f32[768,128]{1,0:T(8,128)S(1)}, u32[]{:S(2)}, u32[]{:S(2)}) collective-permute-start(f32[768,128]{1,0:T(8,128)S(1)} %get-tuple-element.236), channel_id=1, source_target_pairs={{0,8},{4,12},{8,0},{12,4},{16,24},{20,28},{24,16},{28,20},{1,9},{5... | collective-permute-start | bytes 1179656 | tf_op jit(solution)/shard_map/stage_0_10/ppermute | solution.py:44
  31.9 20.7 %collective-permute-start.11 = (f32[768,128]{1,0:T(8,128)S(1)}, f32[768,128]{1,0:T(8,128)S(1)}, u32[]{:S(2)}, u32[]{:S(2)}) collective-permute-start(f32[768,128]{1,0:T(8,128)S(1)} %get-tuple-element.244), channel_id=1, source_target_pairs={{0,8},{4,12},{8,0},{12,4},{16,24},{20,28},{24,16},{28,20},{1,9},{5... | collective-permute-start | bytes 1179656 | tf_op jit(solution)/shard_map/stage_1_11/ppermute | solution.py:44
  33.3 20.8 %collective-permute-start.10 = (f32[768,128]{1,0:T(8,128)S(1)}, f32[768,128]{1,0:T(8,128)S(1)}, u32[]{:S(2)}, u32[]{:S(2)}) collective-permute-start(f32[768,128]{1,0:T(8,128)S(1)} %stage_3_12.1.rest_0_), channel_id=1, source_target_pairs={{0,2},{1,3},{2,0},{3,1},{4,6},{5,7},{6,4},{7,5},{8,10},{9,11},{10,... | collective-permute-start | bytes 1179656 | tf_op jit(solution)/shard_map/stage_3_12/ppermute | solution.py:44
  38.6 25.6 %collective-permute-start.15 = (f32[384,512]{1,0:T(8,128)S(1)}, f32[384,512]{1,0:T(8,128)S(1)}, u32[]{:S(2)}, u32[]{:S(2)}) collective-permute-start(f32[384,512]{1,0:T(8,128)S(1)} %copy-done), channel_id=1, source_target_pairs={{0,2},{1,3},{2,0},{3,1},{4,6},{5,7},{6,4},{7,5},{8,10},{9,11},{10,... | collective-permute-start | bytes 2359304 | tf_op jit(solution)/shard_map/stage_x_14/ppermute | solution.py:44
  40.0 19.8 %collective-permute-start.7 = (f32[384,128]{1,0:T(8,128)S(1)}, f32[384,128]{1,0:T(8,128)S(1)}, u32[]{:S(2)}, u32[]{:S(2)}) collective-permute-start(f32[384,128]{1,0:T(8,128)S(1)} %get-tuple-element.240), channel_id=1, source_target_pairs={{0,16},{4,20},{8,24},{12,28},{16,0},{20,4},{24,8},{28,12},{1,17},{... | collective-permute-start | bytes 589832 | tf_op jit(solution)/shard_map/stage_0_15/ppermute | solution.py:44
  42.5 25.1 %collective-permute-start.17 = (f32[768,128]{1,0:T(8,128)S(1)}, f32[768,128]{1,0:T(8,128)S(1)}, u32[]{:S(2)}, u32[]{:S(2)}) collective-permute-start(f32[768,128]{1,0:T(8,128)S(1)} %get-tuple-element.254), channel_id=1, source_target_pairs={{0,8},{4,12},{8,0},{12,4},{16,24},{20,28},{24,16},{28,20},{1,9},{5... | collective-permute-start | bytes 1179656 | tf_op jit(solution)/shard_map/stage_2_16/ppermute | solution.py:44
  52.6 12.7 %collective-permute-start.14 = (f32[384,128]{1,0:T(8,128)S(1)}, f32[384,128]{1,0:T(8,128)S(1)}, u32[]{:S(2)}, u32[]{:S(2)}) collective-permute-start(f32[384,128]{1,0:T(8,128)S(1)} %get-tuple-element.258), channel_id=1, source_target_pairs={{0,16},{4,20},{8,24},{12,28},{16,0},{20,4},{24,8},{28,12},{1,17},{... | collective-permute-start | bytes 589832 | tf_op jit(solution)/shard_map/stage_1_17/ppermute | solution.py:44
  60.0 37.1 %collective-permute-start.23 = (f32[384,128]{1,0:T(8,128)S(1)}, f32[384,128]{1,0:T(8,128)S(1)}, u32[]{:S(2)}, u32[]{:S(2)}) collective-permute-start(f32[384,128]{1,0:T(8,128)S(1)} %get-tuple-element.292.refs_0_), channel_id=1, source_target_pairs={{0,16},{4,20},{8,24},{12,28},{16,0},{20,4},{24,8},{28,12},{1,17},{... | collective-permute-start | bytes 589832 | tf_op jit(solution)/shard_map/stage_0_19/ppermute | solution.py:44
  61.9 20.9 %collective-permute-start.20 = (f32[768,128]{1,0:T(8,128)S(1)}, f32[768,128]{1,0:T(8,128)S(1)}, u32[]{:S(2)}, u32[]{:S(2)}) collective-permute-start(f32[768,128]{1,0:T(8,128)S(1)} %get-tuple-element.271), channel_id=1, source_target_pairs={{0,8},{4,12},{8,0},{12,4},{16,24},{20,28},{24,16},{28,20},{1,9},{5... | collective-permute-start | bytes 1179656 | tf_op jit(solution)/shard_map/stage_3_20/ppermute | solution.py:44
  64.3 50.8 %collective-permute-start.27 = (f32[768,512]{1,0:T(8,128)S(1)}, f32[768,512]{1,0:T(8,128)S(1)}, u32[]{:S(2)}, u32[]{:S(2)}) collective-permute-start(f32[768,512]{1,0:T(8,128)S(1)} %stage_x_21.1.refs_0_), channel_id=1, source_target_pairs={{0,1},{1,0},{2,3},{3,2},{4,5},{5,4},{6,7},{7,6},{8,9},{9,8},{10,11... | collective-permute-start | bytes 4718600 | tf_op jit(solution)/shard_map/stage_x_21/ppermute | solution.py:44
  65.4 18.5 %collective-permute-start.19 = (f32[384,128]{1,0:T(8,128)S(1)}, f32[384,128]{1,0:T(8,128)S(1)}, u32[]{:S(2)}, u32[]{:S(2)}) collective-permute-start(f32[384,128]{1,0:T(8,128)S(1)} %get-tuple-element.286.refs_0_), channel_id=1, source_target_pairs={{0,16},{4,20},{8,24},{12,28},{16,0},{20,4},{24,8},{28,12},{1,17},{... | collective-permute-start | bytes 589832 | tf_op jit(solution)/shard_map/stage_1_22/ppermute | solution.py:44
  67.7 29.2 %collective-permute-start.18 = (f32[384,128]{1,0:T(8,128)S(1)}, f32[384,128]{1,0:T(8,128)S(1)}, u32[]{:S(2)}, u32[]{:S(2)}) collective-permute-start(f32[384,128]{1,0:T(8,128)S(1)} %get-tuple-element.281), channel_id=1, source_target_pairs={{0,16},{4,20},{8,24},{12,28},{16,0},{20,4},{24,8},{28,12},{1,17},{... | collective-permute-start | bytes 589832 | tf_op jit(solution)/shard_map/stage_2_23/ppermute | solution.py:44
  82.8 24.7 %collective-permute-start.21 = (f32[384,128]{1,0:T(8,128)S(1)}, f32[384,128]{1,0:T(8,128)S(1)}, u32[]{:S(2)}, u32[]{:S(2)}) collective-permute-start(f32[384,128]{1,0:T(8,128)S(1)} %get-tuple-element.285), channel_id=1, source_target_pairs={{0,16},{4,20},{8,24},{12,28},{16,0},{20,4},{24,8},{28,12},{1,17},{... | collective-permute-start | bytes 589832 | tf_op jit(solution)/shard_map/stage_3_24/ppermute | solution.py:44
  84.0 17.9 %collective-permute-start.22 = (f32[768,128]{1,0:T(8,128)S(1)}, f32[768,128]{1,0:T(8,128)S(1)}, u32[]{:S(2)}, u32[]{:S(2)}) collective-permute-start(f32[768,128]{1,0:T(8,128)S(1)} %stage_1_25.1.refs_0_), channel_id=1, source_target_pairs={{0,8},{4,12},{8,0},{12,4},{16,24},{20,28},{24,16},{28,20},{1,9},{5... | collective-permute-start | bytes 1179656 | tf_op jit(solution)/shard_map/stage_1_25/ppermute | solution.py:44
  97.0 19.0 %collective-permute-start.26 = (f32[384,128]{1,0:T(8,128)S(1)}, f32[384,128]{1,0:T(8,128)S(1)}, u32[]{:S(2)}, u32[]{:S(2)}) collective-permute-start(f32[384,128]{1,0:T(8,128)S(1)} %get-tuple-element.309.refs_0_), channel_id=1, source_target_pairs={{0,16},{4,20},{8,24},{12,28},{16,0},{20,4},{24,8},{28,12},{1,17},{... | collective-permute-start | bytes 589832 | tf_op jit(solution)/shard_map/stage_2_26/ppermute | solution.py:44
  97.2 20.7 %collective-permute-start.29 = (f32[768,128]{1,0:T(8,128)S(1)}, f32[768,128]{1,0:T(8,128)S(1)}, u32[]{:S(2)}, u32[]{:S(2)}) collective-permute-start(f32[768,128]{1,0:T(8,128)S(1)} %stage_0_27.1.refs_0_), channel_id=1, source_target_pairs={{0,8},{4,12},{8,0},{12,4},{16,24},{20,28},{24,16},{28,20},{1,9},{5... | collective-permute-start | bytes 1179656 | tf_op jit(solution)/shard_map/stage_0_27/ppermute | solution.py:44
  102.0 7.5 %collective-permute-start.24 = (f32[1536,128]{1,0:T(8,128)S(1)}, f32[1536,128]{1,0:T(8,128)S(1)}, u32[]{:S(2)}, u32[]{:S(2)}) collective-permute-start(f32[1536,128]{1,0:T(8,128)S(1)} %stage_1_28.1.rest_0_), channel_id=1, source_target_pairs={{0,4},{4,0},{8,12},{12,8},{16,20},{20,16},{24,28},{28,24},{1,5},{5... | collective-permute-start | bytes 2359304 | tf_op jit(solution)/shard_map/stage_1_28/ppermute | solution.py:44
  107.7 14.0 %collective-permute-start.31 = (f32[384,128]{1,0:T(8,128)S(1)}, f32[384,128]{1,0:T(8,128)S(1)}, u32[]{:S(2)}, u32[]{:S(2)}) collective-permute-start(f32[384,128]{1,0:T(8,128)S(1)} %get-tuple-element.313.refs_0_), channel_id=1, source_target_pairs={{0,16},{4,20},{8,24},{12,28},{16,0},{20,4},{24,8},{28,12},{1,17},{... | collective-permute-start | bytes 589832 | tf_op jit(solution)/shard_map/stage_3_29/ppermute | solution.py:44
  113.9 44.3 %collective-permute-start.25 = (f32[768,128]{1,0:T(8,128)}, f32[768,128]{1,0:T(8,128)}, u32[]{:S(2)}, u32[]{:S(2)}) collective-permute-start(f32[768,128]{1,0:T(8,128)} %get-tuple-element.327.rest_3_), channel_id=1, source_target_pairs={{0,2},{1,3},{2,0},{3,1},{4,6},{5,7},{6,4},{7,5},{8,10},{9,11},{10,... | collective-permute-start | bytes 1179656 | tf_op jit(solution)/shard_map/stage_1_30/ppermute | solution.py:44
  116.1 12.2 %collective-permute-start.28 = (f32[768,128]{1,0:T(8,128)S(1)}, f32[768,128]{1,0:T(8,128)S(1)}, u32[]{:S(2)}, u32[]{:S(2)}) collective-permute-start(f32[768,128]{1,0:T(8,128)S(1)} %stage_2_32.1.refs_0_), channel_id=1, source_target_pairs={{0,8},{4,12},{8,0},{12,4},{16,24},{20,28},{24,16},{28,20},{1,9},{5... | collective-permute-start | bytes 1179656 | tf_op jit(solution)/shard_map/stage_2_32/ppermute | solution.py:44
  118.0 5.6 %collective-permute-start.30 = (f32[1536,128]{1,0:T(8,128)S(1)}, f32[1536,128]{1,0:T(8,128)S(1)}, u32[]{:S(2)}, u32[]{:S(2)}) collective-permute-start(f32[1536,128]{1,0:T(8,128)S(1)} %stage_0_33.1.rest_0_), channel_id=1, source_target_pairs={{0,4},{4,0},{8,12},{12,8},{16,20},{20,16},{24,28},{28,24},{1,5},{5... | collective-permute-start | bytes 2359304 | tf_op jit(solution)/shard_map/stage_0_33/ppermute | solution.py:44
  121.7 18.0 %collective-permute-start.34 = (f32[768,128]{1,0:T(8,128)S(1)}, f32[768,128]{1,0:T(8,128)S(1)}, u32[]{:S(2)}, u32[]{:S(2)}) collective-permute-start(f32[768,128]{1,0:T(8,128)S(1)} %stage_3_34.1.refs_0_), channel_id=1, source_target_pairs={{0,8},{4,12},{8,0},{12,4},{16,24},{20,28},{24,16},{28,20},{1,9},{5... | collective-permute-start | bytes 1179656 | tf_op jit(solution)/shard_map/stage_3_34/ppermute | solution.py:44
  128.6 6.7 %collective-permute-start.32 = (f32[1536,128]{1,0:T(8,128)S(1)}, f32[1536,128]{1,0:T(8,128)S(1)}, u32[]{:S(2)}, u32[]{:S(2)}) collective-permute-start(f32[1536,128]{1,0:T(8,128)S(1)} %stage_2_36.1.rest_0_), channel_id=1, source_target_pairs={{0,4},{4,0},{8,12},{12,8},{16,20},{20,16},{24,28},{28,24},{1,5},{5... | collective-permute-start | bytes 2359304 | tf_op jit(solution)/shard_map/stage_2_36/ppermute | solution.py:44
  130.3 10.7 %collective-permute-start.37 = (f32[768,128]{1,0:T(8,128)S(1)}, f32[768,128]{1,0:T(8,128)S(1)}, u32[]{:S(2)}, u32[]{:S(2)}) collective-permute-start(f32[768,128]{1,0:T(8,128)S(1)} %get-tuple-element.325.rest_1_), channel_id=1, source_target_pairs={{0,1},{1,0},{2,3},{3,2},{4,5},{5,4},{6,7},{7,6},{8,9},{9,8},{10,11... | collective-permute-start | bytes 1179656 | tf_op jit(solution)/shard_map/stage_0_35/ppermute | solution.py:44
  134.9 8.9 %collective-permute-start.36 = (f32[256,256]{1,0:T(8,128)S(1)}, f32[256,256]{1,0:T(8,128)S(1)}, u32[]{:S(2)}, u32[]{:S(2)}) collective-permute-start(f32[256,256]{1,0:T(8,128)S(1)} %get-tuple-element.329), channel_id=1, source_target_pairs={{0,4},{4,0},{8,12},{12,8},{16,20},{20,16},{24,28},{28,24},{1,5},{5... | collective-permute-start | bytes 786440 | tf_op jit(solution)/shard_map/stage_v_37/ppermute | solution.py:44
  139.0 17.9 %collective-permute-start.33 = (f32[768,128]{1,0:T(8,128)S(1)}, f32[768,128]{1,0:T(8,128)S(1)}, u32[]{:S(2)}, u32[]{:S(2)}) collective-permute-start(f32[768,128]{1,0:T(8,128)S(1)} %get-tuple-element.355.rest_1_), channel_id=1, source_target_pairs={{0,1},{1,0},{2,3},{3,2},{4,5},{5,4},{6,7},{7,6},{8,9},{9,8},{10,11... | collective-permute-start | bytes 1179656 | tf_op jit(solution)/shard_map/stage_2_38/ppermute | solution.py:44
  141.0 7.9 %collective-permute-start.38 = (f32[384,128]{1,0:T(8,128)S(1)}, f32[384,128]{1,0:T(8,128)S(1)}, u32[]{:S(2)}, u32[]{:S(2)}) collective-permute-start(f32[384,128]{1,0:T(8,128)S(1)} %get-tuple-element.340), channel_id=1, source_target_pairs={{0,2},{1,3},{2,0},{3,1},{4,6},{5,7},{6,4},{7,5},{8,10},{9,11},{10,... | collective-permute-start | bytes 589832 | tf_op jit(solution)/shard_map/stage_0_40/ppermute | solution.py:44
  143.8 10.4 %collective-permute-start.40 = (f32[128,256]{1,0:T(8,128)S(1)}, f32[128,256]{1,0:T(8,128)S(1)}, u32[]{:S(2)}, u32[]{:S(2)}) collective-permute-start(f32[128,256]{1,0:T(8,128)S(1)} %get-tuple-element.344), channel_id=1, source_target_pairs={{0,1},{1,0},{2,3},{3,2},{4,5},{5,4},{6,7},{7,6},{8,9},{9,8},{10,11... | collective-permute-start | bytes 393224 | tf_op jit(solution)/shard_map/stage_v_41/ppermute | solution.py:44
  148.9 14.8 %collective-permute-start.45 = (f32[768,128]{1,0:T(8,128)S(1)}, f32[768,128]{1,0:T(8,128)S(1)}, u32[]{:S(2)}, u32[]{:S(2)}) collective-permute-start(f32[768,128]{1,0:T(8,128)S(1)} %get-tuple-element.357.rest_3_), channel_id=1, source_target_pairs={{0,2},{1,3},{2,0},{3,1},{4,6},{5,7},{6,4},{7,5},{8,10},{9,11},{10,... | collective-permute-start | bytes 1179656 | tf_op jit(solution)/shard_map/stage_3_42/ppermute | solution.py:44
  154.2 7.9 %collective-permute-start.46 = (f32[64,256]{1,0:T(8,128)S(1)}, f32[64,256]{1,0:T(8,128)S(1)}, u32[]{:S(2)}, u32[]{:S(2)}) collective-permute-start(f32[64,256]{1,0:T(8,128)S(1)} %get-tuple-element.363), channel_id=1, source_target_pairs={{0,2},{1,3},{2,0},{3,1},{4,6},{5,7},{6,4},{7,5},{8,10},{9,11},{10,... | collective-permute-start | bytes 196616 | tf_op jit(solution)/shard_map/stage_v_45/ppermute | solution.py:44
  156.5 23.6 %collective-permute-start.42 = (f32[8,512]{1,0:T(8,128)S(1)}, f32[8,512]{1,0:T(8,128)S(1)}, u32[]{:S(2)}, u32[]{:S(2)}) collective-permute-start(f32[8,512]{1,0:T(8,128)S(1)} %constant_dynamic-update-slice_fusion), channel_id=1, source_target_pairs={{0,1},{1,0},{2,3},{3,2},{4,5},{5,4},{6,7},{7,6},{8,9},{9,8},{10,11... | collective-permute-start | bytes 49160 | tf_op jit(solution)/shard_map/stage_b_57/ppermute | solution.py:44
  158.2 9.0 %collective-permute-start.48 = (f32[384,128]{1,0:T(8,128)S(1)}, f32[384,128]{1,0:T(8,128)S(1)}, u32[]{:S(2)}, u32[]{:S(2)}) collective-permute-start(f32[384,128]{1,0:T(8,128)S(1)} %get-tuple-element.371), channel_id=1, source_target_pairs={{0,2},{1,3},{2,0},{3,1},{4,6},{5,7},{6,4},{7,5},{8,10},{9,11},{10,... | collective-permute-start | bytes 589832 | tf_op jit(solution)/shard_map/stage_2_47/ppermute | solution.py:44
  161.3 29.4 %collective-permute-start.41 = (f32[384,128]{1,0:T(8,128)S(1)}, f32[384,128]{1,0:T(8,128)S(1)}, u32[]{:S(2)}, u32[]{:S(2)}) collective-permute-start(f32[384,128]{1,0:T(8,128)S(1)} %get-tuple-element.375), channel_id=1, source_target_pairs={{0,1},{1,0},{2,3},{3,2},{4,5},{5,4},{6,7},{7,6},{8,9},{9,8},{10,11... | collective-permute-start | bytes 589832 | tf_op jit(solution)/shard_map/stage_1_48/ppermute | solution.py:44
  166.4 23.7 %collective-permute-start.57 = (f32[384,128]{1,0:T(8,128)S(1)}, f32[384,128]{1,0:T(8,128)S(1)}, u32[]{:S(2)}, u32[]{:S(2)}) collective-permute-start(f32[384,128]{1,0:T(8,128)S(1)} %get-tuple-element.385), channel_id=1, source_target_pairs={{0,1},{1,0},{2,3},{3,2},{4,5},{5,4},{6,7},{7,6},{8,9},{9,8},{10,11... | collective-permute-start | bytes 589832 | tf_op jit(solution)/shard_map/stage_3_51/ppermute | solution.py:44
  170.4 5.4 %collective-permute-start.50 = (f32[64,256]{1,0:T(8,128)S(1)}, f32[64,256]{1,0:T(8,128)S(1)}, u32[]{:S(2)}, u32[]{:S(2)}) collective-permute-start(f32[64,256]{1,0:T(8,128)S(1)} %stage_w_55.1.refs_0_), channel_id=1, source_target_pairs={{0,16},{4,20},{8,24},{12,28},{16,0},{20,4},{24,8},{28,12},{1,17},{... | collective-permute-start | bytes 196616 | tf_op jit(solution)/shard_map/stage_w_55/ppermute | solution.py:44
  171.3 5.7 %collective-permute-start.53 = (f32[64,256]{1,0:T(8,128)S(1)}, f32[64,256]{1,0:T(8,128)S(1)}, u32[]{:S(2)}, u32[]{:S(2)}) collective-permute-start(f32[64,256]{1,0:T(8,128)S(1)} %stage_v_56.1.refs_0_), channel_id=1, source_target_pairs={{0,2},{1,3},{2,0},{3,1},{4,6},{5,7},{6,4},{7,5},{8,10},{9,11},{10,... | collective-permute-start | bytes 196616 | tf_op jit(solution)/shard_map/stage_v_56/ppermute | solution.py:44
  179.2 8.1 %collective-permute-start.58 = (f32[128,256]{1,0:T(8,128)S(1)}, f32[128,256]{1,0:T(8,128)S(1)}, u32[]{:S(2)}, u32[]{:S(2)}) collective-permute-start(f32[128,256]{1,0:T(8,128)S(1)} %stage_w_60.1.refs_0_), channel_id=1, source_target_pairs={{0,1},{1,0},{2,3},{3,2},{4,5},{5,4},{6,7},{7,6},{8,9},{9,8},{10,11... | collective-permute-start | bytes 393224 | tf_op jit(solution)/shard_map/stage_w_60/ppermute | solution.py:44
  180.1 10.5 %collective-permute-start.54 = (f32[8,512]{1,0:T(8,128)S(1)}, f32[8,512]{1,0:T(8,128)S(1)}, u32[]{:S(2)}, u32[]{:S(2)}) collective-permute-start(f32[8,512]{1,0:T(8,128)S(1)} %add.24), channel_id=1, source_target_pairs={{0,2},{1,3},{2,0},{3,1},{4,6},{5,7},{6,4},{7,5},{8,10},{9,11},{10,... | collective-permute-start | bytes 49160 | tf_op jit(solution)/shard_map/stage_b_61/ppermute | solution.py:44
  180.9 9.8 %collective-permute-start.56 = (f32[256,256]{1,0:T(8,128)S(1)}, f32[256,256]{1,0:T(8,128)S(1)}, u32[]{:S(2)}, u32[]{:S(2)}) collective-permute-start(f32[256,256]{1,0:T(8,128)S(1)} %stage_v_62.1.refs_0_), channel_id=1, source_target_pairs={{0,4},{4,0},{8,12},{12,8},{16,20},{20,16},{24,28},{28,24},{1,5},{5... | collective-permute-start | bytes 786440 | tf_op jit(solution)/shard_map/stage_v_62/ppermute | solution.py:44
  187.3 5.4 %collective-permute-start.59 = (f32[256,256]{1,0:T(8,128)S(1)}, f32[256,256]{1,0:T(8,128)S(1)}, u32[]{:S(2)}, u32[]{:S(2)}) collective-permute-start(f32[256,256]{1,0:T(8,128)S(1)} %stage_w_63.1.refs_2_), channel_id=1, source_target_pairs={{0,4},{4,0},{8,12},{12,8},{16,20},{20,16},{24,28},{28,24},{1,5},{5... | collective-permute-start | bytes 786440 | tf_op jit(solution)/shard_map/stage_w_63/ppermute | solution.py:44
  (18 other events, 73.6 us)

commit v3 on v2

--- a/solution.py
+++ b/solution.py
@@ -14,7 +14,7 @@
 WIDTHS = (1, 1, 1, 1)
 EARLY = 2
 WAVES = (False, False, False)
-ORDER = ('01201p32010132x021303x123120131x20302v230v30wvw21wv3wv2wvbwv', 'wbvw3vb1w')
+ORDER = ('01201p32010132x021303x123120131x20302v230v30wvw21wv3wv2wvbwv', '1wbvw3vbw')
 SMALL_VMEM = 12 * 1024 * 1024
 VMEM_LIMIT = 40 * 1024 * 1024
 STAGE = 16000000000.0

time: 195 us -> 194 us (level)
  no operation moved by 1% of the time
where the time goes in v3:
time: 194 us
  starting transfers between devices  78.1 us (40%)
  waiting for transfers between devices  59.1 us (30%)
  Pallas kernels  43.1 us (22%)
  matrix products  8.83 us (5%)
    ppermute x60, starting transfers between devices, swap(): return lax.ppermute(x, axis, [(i, i ^ bit) for i in range(size)])  78.1 us
    ppermute x60, waiting for transfers between devices, swap(): return lax.ppermute(x, axis, [(i, i ^ bit) for i in range(size)])  59.1 us
    pallas_call x8, Pallas kernels, tile_call(): pl.pallas_call(kernel, grid_spec=pltpu.PrefetchScalarGridSpec(num_scalar_...  28 us
    pallas_call x2, Pallas kernels, outer(): pl.pallas_call(functools.partial(outer_kernel, labels, orders), in_specs=...  7.17 us
    dot_general x4, matrix products, chunk(): jnp.dot(own, weight[:, cols], precision=HIGH, preferred_element_type=F32)  6.03 us
    pallas_call x47, Pallas kernels, rows_call(): pl.pallas_call(kernel, in_specs=[vmem] * every, out_specs=[vmem] * len(ou...  4.29 us
  transfers between devices with their start and end apart: 60, of which 22 were waited for; matrix products, arithmetic and copies ran while one was open for 5% of the time, Pallas kernels for 21%

profile of v3, /device:TPU:1, one launch (start us, length us, event | category | flops | bytes accessed | tf_op | source)
XLA Modules:
  0.0 193.7 jit_solution(4385066910326476305)
XLA Ops:
  0.7 1.7 fusion.11.refs_0_
  2.4 2.1 %collective-permute-start.1 = (f32[384,128]{1,0:T(8,128)S(1)}, f32[384,128]{1,0:T(8,128)S(1)}, u32[]{:S(2)}, u32[]{:S(2)}) collective-permute-start(f32[384,128]{1,0:T(8,128)S(1)} %fusion.11.refs_0_), channel_id=1, source_target_pairs={{0,2},{1,3},{2,0},{3,1},{4,6},{5,7},{6,4},{7,5},{8,10},{9,11},{10,... | collective-permute-start | bytes 589832 | tf_op jit(solution)/shard_map/stage_0_0/ppermute | solution.py:44
  4.5 1.4 fusion.7.refs_0_
  7.3 1.4 fusion.4.refs_0_
  14.6 1.4 fusion.1.refs_0_
  17.7 2.4 %collective-permute-done.2.rest_1_ = f32[768,128]{1,0:T(8,128)S(1)} collective-permute-done((f32[768,128]{1,0:T(8,128)S(1)}, f32[768,128]{1,0:T(8,128)S(1)}, u32[]{:S(2)}, u32[]{:S(2)}) %collective-permute-start.2) | collective-permute-done | bytes 393248 | tf_op jit(solution)/shard_map/stage_0_3/ppermute | solution.py:44
  20.1 3.1 %stage_0_8.1 = (f32[1536,128]{1,0:T(8,128)S(1)}, f32[1536,128]{1,0:T(8,128)S(1)}) custom-call(s32[3]{0:T(128)S(1)} %pad_add_fusion.me, s32[48]{0:T(128)S(1)} %reshape.26.pattern, bf16[24,128,256]{2,1,0:T(8,128)(2,1)S(1)} %get-tuple-element.218.a_hi, bf16[24,128,256]{2,1,0:T(8,128)(2,1)S(1)} %get-tuple-element.219.a_lo, f32[768,128]{1,0:T(8,128)S(1)} %stage_0_3.1.rest_0_, ...), custom_call_target="tpu_custom_call" | custom-call | flops 16000000000 | tf_op jit(solution)/shard_map/stage_0_8/pallas_call | solution.py:281
  23.3 3.0 %collective-permute-start.4 = (f32[1536,128]{1,0:T(8,128)S(1)}, f32[1536,128]{1,0:T(8,128)S(1)}, u32[]{:S(2)}, u32[]{:S(2)}) collective-permute-start(f32[1536,128]{1,0:T(8,128)S(1)} %get-tuple-element.228), channel_id=1, source_target_pairs={{0,4},{4,0},{8,12},{12,8},{16,20},{20,16},{24,28},{28,24},{1,5},{5... | collective-permute-start | bytes 2359304 | tf_op jit(solution)/shard_map/stage_0_8/ppermute | solution.py:44
  26.3 3.1 %stage_1_9.1 = (f32[1536,128]{1,0:T(8,128)S(1)}, f32[1536,128]{1,0:T(8,128)S(1)}) custom-call(s32[3]{0:T(128)S(1)} %pad_add_fusion.me, s32[48]{0:T(128)S(1)} %reshape.26.pattern, bf16[24,128,256]{2,1,0:T(8,128)(2,1)S(1)} %get-tuple-element.218.a_hi, bf16[24,128,256]{2,1,0:T(8,128)(2,1)S(1)} %get-tuple-element.219.a_lo, f32[768,128]{1,0:T(8,128)S(1)} %stage_1_4.1.rest_0_, ...), custom_call_target="tpu_custom_call" | custom-call | flops 16000000000 | tf_op jit(solution)/shard_map/stage_1_9/pallas_call | solution.py:281
  29.6 1.4 collective-permute-start.6
  31.9 1.4 collective-permute-start.11
  34.6 3.1 %stage_2_13.1 = (f32[1536,128]{1,0:T(8,128)S(1)}, f32[1536,128]{1,0:T(8,128)S(1)}) custom-call(s32[3]{0:T(128)S(1)} %pad_add_fusion.me, s32[48]{0:T(128)S(1)} %reshape.26.pattern, bf16[24,128,256]{2,1,0:T(8,128)(2,1)S(1)} %get-tuple-element.218.a_hi, bf16[24,128,256]{2,1,0:T(8,128)(2,1)S(1)} %get-tuple-element.219.a_lo, f32[768,128]{1,0:T(8,128)S(1)} %stage_2_7.1.rest_0_, ...), custom_call_target="tpu_custom_call" | custom-call | flops 16000000000 | tf_op jit(solution)/shard_map/stage_2_13/pallas_call | solution.py:281
  40.0 2.4 %collective-permute-start.7 = (f32[384,128]{1,0:T(8,128)S(1)}, f32[384,128]{1,0:T(8,128)S(1)}, u32[]{:S(2)}, u32[]{:S(2)}) collective-permute-start(f32[384,128]{1,0:T(8,128)S(1)} %get-tuple-element.240), channel_id=1, source_target_pairs={{0,16},{4,20},{8,24},{12,28},{16,0},{20,4},{24,8},{28,12},{1,17},{... | collective-permute-start | bytes 589832 | tf_op jit(solution)/shard_map/stage_0_15/ppermute | solution.py:44
  42.5 1.4 collective-permute-start.17
  43.9 8.7 %collective-permute-done.11.refs_1_ = f32[768,128]{1,0:T(8,128)S(1)} collective-permute-done((f32[768,128]{1,0:T(8,128)S(1)}, f32[768,128]{1,0:T(8,128)S(1)}, u32[]{:S(2)}, u32[]{:S(2)}) %collective-permute-start.11) | collective-permute-done | bytes 393248 | tf_op jit(solution)/shard_map/stage_1_11/ppermute | solution.py:44
  52.6 1.5 collective-permute-start.14
  54.1 3.1 %stage_3_18.1 = (f32[1536,128]{1,0:T(8,128)S(1)}, f32[1536,128]{1,0:T(8,128)S(1)}) custom-call(s32[3]{0:T(128)S(1)} %pad_add_fusion.me, s32[48]{0:T(128)S(1)} %reshape.26.pattern, bf16[24,128,256]{2,1,0:T(8,128)(2,1)S(1)} %get-tuple-element.218.a_hi, bf16[24,128,256]{2,1,0:T(8,128)(2,1)S(1)} %get-tuple-element.219.a_lo, f32[768,128]{1,0:T(8,128)S(1)} %stage_3_12.1.rest_0_, ...), custom_call_target="tpu_custom_call" | custom-call | flops 16000000000 | tf_op jit(solution)/shard_map/stage_3_18/pallas_call | solution.py:281
  57.2 2.6 %collective-permute-start.16 = (f32[1536,128]{1,0:T(8,128)S(1)}, f32[1536,128]{1,0:T(8,128)S(1)}, u32[]{:S(2)}, u32[]{:S(2)}) collective-permute-start(f32[1536,128]{1,0:T(8,128)S(1)} %get-tuple-element.262), channel_id=1, source_target_pairs={{0,4},{4,0},{8,12},{12,8},{16,20},{20,16},{24,28},{28,24},{1,5},{5... | collective-permute-start | bytes 2359304 | tf_op jit(solution)/shard_map/stage_3_18/ppermute | solution.py:44
  61.9 2.3 %collective-permute-start.20 = (f32[768,128]{1,0:T(8,128)S(1)}, f32[768,128]{1,0:T(8,128)S(1)}, u32[]{:S(2)}, u32[]{:S(2)}) collective-permute-start(f32[768,128]{1,0:T(8,128)S(1)} %get-tuple-element.271), channel_id=1, source_target_pairs={{0,8},{4,12},{8,0},{12,4},{16,24},{20,28},{24,16},{28,20},{1,9},{5... | collective-permute-start | bytes 1179656 | tf_op jit(solution)/shard_map/stage_3_20/ppermute | solution.py:44
  65.4 2.2 %collective-permute-start.19 = (f32[384,128]{1,0:T(8,128)S(1)}, f32[384,128]{1,0:T(8,128)S(1)}, u32[]{:S(2)}, u32[]{:S(2)}) collective-permute-start(f32[384,128]{1,0:T(8,128)S(1)} %get-tuple-element.286.refs_0_), channel_id=1, source_target_pairs={{0,16},{4,20},{8,24},{12,28},{16,0},{20,4},{24,8},{28,12},{1,17},{... | collective-permute-start | bytes 589832 | tf_op jit(solution)/shard_map/stage_1_22/ppermute | solution.py:44
  68.0 14.8 %collective-permute-done.20.refs_1_ = f32[768,128]{1,0:T(8,128)S(1)} collective-permute-done((f32[768,128]{1,0:T(8,128)S(1)}, f32[768,128]{1,0:T(8,128)S(1)}, u32[]{:S(2)}, u32[]{:S(2)}) %collective-permute-start.20) | collective-permute-done | bytes 393248 | tf_op jit(solution)/shard_map/stage_3_20/ppermute | solution.py:44
  84.0 2.3 %collective-permute-start.22 = (f32[768,128]{1,0:T(8,128)S(1)}, f32[768,128]{1,0:T(8,128)S(1)}, u32[]{:S(2)}, u32[]{:S(2)}) collective-permute-start(f32[768,128]{1,0:T(8,128)S(1)} %stage_1_25.1.refs_0_), channel_id=1, source_target_pairs={{0,8},{4,12},{8,0},{12,4},{16,24},{20,28},{24,16},{28,20},{1,9},{5... | collective-permute-start | bytes 1179656 | tf_op jit(solution)/shard_map/stage_1_25/ppermute | solution.py:44
  86.2 10.6 %collective-permute-done.18.refs_1_ = f32[384,128]{1,0:T(8,128)S(1)} collective-permute-done((f32[384,128]{1,0:T(8,128)S(1)}, f32[384,128]{1,0:T(8,128)S(1)}, u32[]{:S(2)}, u32[]{:S(2)}) %collective-permute-start.18) | collective-permute-done | bytes 196640 | tf_op jit(solution)/shard_map/stage_2_23/ppermute | solution.py:44
  97.2 1.9 %collective-permute-start.25 = (f32[768,128]{1,0:T(8,128)S(1)}, f32[768,128]{1,0:T(8,128)S(1)}, u32[]{:S(2)}, u32[]{:S(2)}) collective-permute-start(f32[768,128]{1,0:T(8,128)S(1)} %stage_0_27.1.refs_0_), channel_id=1, source_target_pairs={{0,8},{4,12},{8,0},{12,4},{16,24},{20,28},{24,16},{28,20},{1,9},{5... | collective-permute-start | bytes 1179656 | tf_op jit(solution)/shard_map/stage_0_27/ppermute | solution.py:44
  99.1 2.7 %collective-permute-done.22.refs_1_ = f32[768,128]{1,0:T(8,128)S(1)} collective-permute-done((f32[768,128]{1,0:T(8,128)S(1)}, f32[768,128]{1,0:T(8,128)S(1)}, u32[]{:S(2)}, u32[]{:S(2)}) %collective-permute-start.22) | collective-permute-done | bytes 393248 | tf_op jit(solution)/shard_map/stage_1_25/ppermute | solution.py:44
  102.0 5.6 %collective-permute-start.28 = (f32[1536,128]{1,0:T(8,128)S(1)}, f32[1536,128]{1,0:T(8,128)S(1)}, u32[]{:S(2)}, u32[]{:S(2)}) collective-permute-start(f32[1536,128]{1,0:T(8,128)S(1)} %stage_1_28.1.rest_0_), channel_id=1, source_target_pairs={{0,4},{4,0},{8,12},{12,8},{16,20},{20,16},{24,28},{28,24},{1,5},{5... | collective-permute-start | bytes 2359304 | tf_op jit(solution)/shard_map/stage_1_28/ppermute | solution.py:44
  109.5 4.4 %stage_1_30.1 = (f32[768,128]{1,0:T(8,128)S(1)}, f32[768,128]{1,0:T(8,128)}, f32[8,128]{1,0:T(8,128)S(1)}) custom-call(s32[3]{0:T(128)S(1)} %pad_add_fusion.me, s32[48]{0:T(128)S(1)} %reshape.26.pattern, bf16[24,256,128]{2,1,0:T(8,128)(2,1)S(1)} %get-tuple-element.220.a_hi, bf16[24,256,128]{2,1,0:T(8,128)(2,1)S(1)} %get-tuple-element.221.a_lo, ...), custom_call_target="tpu_custom_call" | custom-call | flops 16000000000 | tf_op jit(solution)/shard_map/stage_1_30/pallas_call | solution.py:281
  118.0 3.7 %collective-permute-start.31 = (f32[1536,128]{1,0:T(8,128)S(1)}, f32[1536,128]{1,0:T(8,128)S(1)}, u32[]{:S(2)}, u32[]{:S(2)}) collective-permute-start(f32[1536,128]{1,0:T(8,128)S(1)} %stage_0_33.1.rest_0_), channel_id=1, source_target_pairs={{0,4},{4,0},{8,12},{12,8},{16,20},{20,16},{24,28},{28,24},{1,5},{5... | collective-permute-start | bytes 2359304 | tf_op jit(solution)/shard_map/stage_0_33/ppermute | solution.py:44
  121.8 1.8 collective-permute-done.31.rest_1_
  123.6 3.7 %stage_0_35.1 = (f32[768,128]{1,0:T(8,128)S(1)}, f32[768,128]{1,0:T(8,128)S(1)}, f32[8,128]{1,0:T(8,128)S(1)}) custom-call(s32[3]{0:T(128)S(1)} %pad_add_fusion.me, s32[48]{0:T(128)S(1)} %reshape.26.pattern, bf16[24,256,128]{2,1,0:T(8,128)(2,1)S(1)} %get-tuple-element.220.a_hi, bf16[24,256,128]{2,1,0:T(8,128)(2,1)S(1)} %get-tuple-element.221.a_lo, ...), custom_call_target="tpu_custom_call" | custom-call | flops 16000000000 | tf_op jit(solution)/shard_map/stage_0_35/pallas_call | solution.py:281
  128.6 1.7 collective-permute-start.32
  131.1 3.8 %stage_v_37.1 = (f32[256,256]{1,0:T(8,128)S(1)}, f32[256,256]{1,0:T(8,128)S(1)}) custom-call(s32[3]{0:T(128)S(1)} %pad_add_fusion.me, bf16[512,1536]{1,0:T(8,128)(2,1)S(1)} %get-tuple-element.352.x_hi, bf16[512,1536]{1,0:T(8,128)(2,1)S(1)} %get-tuple-element.353.x_lo, f32[768,128]{1,0:T(8,128)S(1)} %get-tuple-element.337.rest_0_.refs_0_, ...), custom_call_target="tpu_custom_call" | custom-call | flops 16000000000 | tf_op jit(solution)/shard_map/stage_v_37/pallas_call | solution.py:381
  135.3 3.7 %stage_2_38.1 = (f32[768,128]{1,0:T(8,128)S(1)}, f32[768,128]{1,0:T(8,128)S(1)}, f32[8,128]{1,0:T(8,128)S(1)}) custom-call(s32[3]{0:T(128)S(1)} %pad_add_fusion.me, s32[48]{0:T(128)S(1)} %reshape.26.pattern, bf16[24,256,128]{2,1,0:T(8,128)(2,1)S(1)} %get-tuple-element.220.a_hi, bf16[24,256,128]{2,1,0:T(8,128)(2,1)S(1)} %get-tuple-element.221.a_lo, ...), custom_call_target="tpu_custom_call" | custom-call | flops 16000000000 | tf_op jit(solution)/shard_map/stage_2_38/pallas_call | solution.py:281
  141.0 2.7 %collective-permute-start.38 = (f32[384,128]{1,0:T(8,128)S(1)}, f32[384,128]{1,0:T(8,128)S(1)}, u32[]{:S(2)}, u32[]{:S(2)}) collective-permute-start(f32[384,128]{1,0:T(8,128)S(1)} %get-tuple-element.340), channel_id=1, source_target_pairs={{0,2},{1,3},{2,0},{3,1},{4,6},{5,7},{6,4},{7,5},{8,10},{9,11},{10,... | collective-permute-start | bytes 589832 | tf_op jit(solution)/shard_map/stage_0_40/ppermute | solution.py:44
  143.8 1.4 collective-permute-start.37
  145.2 3.7 %stage_3_42.1 = (f32[768,128]{1,0:T(8,128)S(1)}, f32[768,128]{1,0:T(8,128)S(1)}, f32[8,128]{1,0:T(8,128)S(1)}) custom-call(s32[3]{0:T(128)S(1)} %pad_add_fusion.me, s32[48]{0:T(128)S(1)} %reshape.26.pattern, bf16[24,256,128]{2,1,0:T(8,128)(2,1)S(1)} %get-tuple-element.220.a_hi, bf16[24,256,128]{2,1,0:T(8,128)(2,1)S(1)} %get-tuple-element.221.a_lo, ...), custom_call_target="tpu_custom_call" | custom-call | flops 16000000000 | tf_op jit(solution)/shard_map/stage_3_42/pallas_call | solution.py:281
  149.0 3.3 %stage_w_44.1 = (f32[256,256]{1,0:T(8,128)S(1)}, f32[256,256]{1,0:T(8,128)S(1)}) custom-call(s32[3]{0:T(128)S(1)} %pad_add_fusion.me, bf16[512,1536]{1,0:T(8,128)(2,1)S(1)} %get-tuple-element.352.x_hi, bf16[512,1536]{1,0:T(8,128)(2,1)S(1)} %get-tuple-element.353.x_lo, f32[768,128]{1,0:T(8,128)S(1)} %get-tuple-element.368.rest_0_.refs_0_, ...), custom_call_target="tpu_custom_call" | custom-call | flops 16000000000 | tf_op jit(solution)/shard_map/stage_w_44/pallas_call | solution.py:381
  152.4 1.8 collective-permute-start.40
  154.2 1.8 collective-permute-start.39
  162.2 1.5 collective-permute-start.45
  163.9 2.5 %collective-permute-done.45.refs_1_ = f32[64,256]{1,0:T(8,128)S(1)} collective-permute-done((f32[64,256]{1,0:T(8,128)S(1)}, f32[64,256]{1,0:T(8,128)S(1)}, u32[]{:S(2)}, u32[]{:S(2)}) %collective-permute-start.45) | collective-permute-done | bytes 65568 | tf_op jit(solution)/shard_map/stage_w_49/ppermute | solution.py:44
  167.2 2.0 %collective-permute-start.52 = (f32[64,256]{1,0:T(8,128)S(1)}, f32[64,256]{1,0:T(8,128)S(1)}, u32[]{:S(2)}, u32[]{:S(2)}) collective-permute-start(f32[64,256]{1,0:T(8,128)S(1)} %stage_v_53.1.refs_0_), channel_id=1, source_target_pairs={{0,16},{4,20},{8,24},{12,28},{16,0},{20,4},{24,8},{28,12},{1,17},{... | collective-permute-start | bytes 196616 | tf_op jit(solution)/shard_map/stage_v_53/ppermute | solution.py:44
  171.8 4.0 %collective-permute-done.49.refs_1_ = f32[64,256]{1,0:T(8,128)S(1)} collective-permute-done((f32[64,256]{1,0:T(8,128)S(1)}, f32[64,256]{1,0:T(8,128)S(1)}, u32[]{:S(2)}, u32[]{:S(2)}) %collective-permute-start.49) | collective-permute-done | bytes 65568 | tf_op jit(solution)/shard_map/stage_w_55/ppermute | solution.py:44
  177.6 1.6 collective-permute-done.50.refs_1_
  180.9 6.4 %collective-permute-start.57 = (f32[256,256]{1,0:T(8,128)S(1)}, f32[256,256]{1,0:T(8,128)S(1)}, u32[]{:S(2)}, u32[]{:S(2)}) collective-permute-start(f32[256,256]{1,0:T(8,128)S(1)} %stage_v_63.1.refs_0_), channel_id=1, source_target_pairs={{0,4},{4,0},{8,12},{12,8},{16,20},{20,16},{24,28},{28,24},{1,5},{5... | collective-permute-start | bytes 786440 | tf_op jit(solution)/shard_map/stage_v_63/ppermute | solution.py:44
  187.3 2.7 %collective-permute-start.58 = (f32[256,256]{1,0:T(8,128)S(1)}, f32[256,256]{1,0:T(8,128)S(1)}, u32[]{:S(2)}, u32[]{:S(2)}) collective-permute-start(f32[256,256]{1,0:T(8,128)S(1)} %stage_w_64.1.refs_2_), channel_id=1, source_target_pairs={{0,4},{4,0},{8,12},{12,8},{16,20},{20,16},{24,28},{28,24},{1,5},{5... | collective-permute-start | bytes 786440 | tf_op jit(solution)/shard_map/stage_w_64/ppermute | solution.py:44
  190.1 1.4 convolution_add_fusion.2
  192.1 1.6 shard_map.93
  (165 shorter events, 43.4 us)
Async XLA Ops:
  2.4 6.9 %collective-permute-start.1 = (f32[384,128]{1,0:T(8,128)S(1)}, f32[384,128]{1,0:T(8,128)S(1)}, u32[]{:S(2)}, u32[]{:S(2)}) collective-permute-start(f32[384,128]{1,0:T(8,128)S(1)} %fusion.11.refs_0_), channel_id=1, source_target_pairs={{0,2},{1,3},{2,0},{3,1},{4,6},{5,7},{6,4},{7,5},{8,10},{9,11},{10,... | collective-permute-start | bytes 589832 | tf_op jit(solution)/shard_map/stage_0_0/ppermute | solution.py:44
  6.0 5.5 %collective-permute-start = (f32[384,128]{1,0:T(8,128)S(1)}, f32[384,128]{1,0:T(8,128)S(1)}, u32[]{:S(2)}, u32[]{:S(2)}) collective-permute-start(f32[384,128]{1,0:T(8,128)S(1)} %fusion.7.refs_0_), channel_id=1, source_target_pairs={{0,1},{1,0},{2,3},{3,2},{4,5},{5,4},{6,7},{7,6},{8,9},{9,8},{10,11... | collective-permute-start | bytes 589832 | tf_op jit(solution)/shard_map/stage_1_1/ppermute | solution.py:44
  8.7 8.6 %collective-permute-start.3 = (f32[384,128]{1,0:T(8,128)S(1)}, f32[384,128]{1,0:T(8,128)S(1)}, u32[]{:S(2)}, u32[]{:S(2)}) collective-permute-start(f32[384,128]{1,0:T(8,128)S(1)} %fusion.4.refs_0_), channel_id=1, source_target_pairs={{0,2},{1,3},{2,0},{3,1},{4,6},{5,7},{6,4},{7,5},{8,10},{9,11},{10,... | collective-permute-start | bytes 589832 | tf_op jit(solution)/shard_map/stage_2_2/ppermute | solution.py:44
  9.4 10.7 %collective-permute-start.2 = (f32[768,128]{1,0:T(8,128)S(1)}, f32[768,128]{1,0:T(8,128)S(1)}, u32[]{:S(2)}, u32[]{:S(2)}) collective-permute-start(f32[768,128]{1,0:T(8,128)S(1)} %stage_0_3.1.rest_0_), channel_id=1, source_target_pairs={{0,1},{1,0},{2,3},{3,2},{4,5},{5,4},{6,7},{7,6},{8,9},{9,8},{10,11... | collective-permute-start | bytes 1179656 | tf_op jit(solution)/shard_map/stage_0_3/ppermute | solution.py:44
  11.6 14.7 %collective-permute-start.5 = (f32[768,128]{1,0:T(8,128)S(1)}, f32[768,128]{1,0:T(8,128)S(1)}, u32[]{:S(2)}, u32[]{:S(2)}) collective-permute-start(f32[768,128]{1,0:T(8,128)S(1)} %stage_1_4.1.rest_0_), channel_id=1, source_target_pairs={{0,2},{1,3},{2,0},{3,1},{4,6},{5,7},{6,4},{7,5},{8,10},{9,11},{10,... | collective-permute-start | bytes 1179656 | tf_op jit(solution)/shard_map/stage_1_4/ppermute | solution.py:44
  16.0 17.2 %collective-permute-start.8 = (f32[384,128]{1,0:T(8,128)S(1)}, f32[384,128]{1,0:T(8,128)S(1)}, u32[]{:S(2)}, u32[]{:S(2)}) collective-permute-start(f32[384,128]{1,0:T(8,128)S(1)} %fusion.1.refs_0_), channel_id=1, source_target_pairs={{0,1},{1,0},{2,3},{3,2},{4,5},{5,4},{6,7},{7,6},{8,9},{9,8},{10,11... | collective-permute-start | bytes 589832 | tf_op jit(solution)/shard_map/stage_3_6/ppermute | solution.py:44
  17.4 17.3 %collective-permute-start.12 = (f32[768,128]{1,0:T(8,128)S(1)}, f32[768,128]{1,0:T(8,128)S(1)}, u32[]{:S(2)}, u32[]{:S(2)}) collective-permute-start(f32[768,128]{1,0:T(8,128)S(1)} %stage_2_7.1.rest_0_), channel_id=1, source_target_pairs={{0,1},{1,0},{2,3},{3,2},{4,5},{5,4},{6,7},{7,6},{8,9},{9,8},{10,11... | collective-permute-start | bytes 1179656 | tf_op jit(solution)/shard_map/stage_2_7/ppermute | solution.py:44
  23.3 6.2 %collective-permute-start.4 = (f32[1536,128]{1,0:T(8,128)S(1)}, f32[1536,128]{1,0:T(8,128)S(1)}, u32[]{:S(2)}, u32[]{:S(2)}) collective-permute-start(f32[1536,128]{1,0:T(8,128)S(1)} %get-tuple-element.228), channel_id=1, source_target_pairs={{0,4},{4,0},{8,12},{12,8},{16,20},{20,16},{24,28},{28,24},{1,5},{5... | collective-permute-start | bytes 2359304 | tf_op jit(solution)/shard_map/stage_0_8/ppermute | solution.py:44
  29.6 10.3 %collective-permute-start.6 = (f32[768,128]{1,0:T(8,128)S(1)}, f32[768,128]{1,0:T(8,128)S(1)}, u32[]{:S(2)}, u32[]{:S(2)}) collective-permute-start(f32[768,128]{1,0:T(8,128)S(1)} %get-tuple-element.236), channel_id=1, source_target_pairs={{0,8},{4,12},{8,0},{12,4},{16,24},{20,28},{24,16},{28,20},{1,9},{5... | collective-permute-start | bytes 1179656 | tf_op jit(solution)/shard_map/stage_0_10/ppermute | solution.py:44
  31.9 20.7 %collective-permute-start.11 = (f32[768,128]{1,0:T(8,128)S(1)}, f32[768,128]{1,0:T(8,128)S(1)}, u32[]{:S(2)}, u32[]{:S(2)}) collective-permute-start(f32[768,128]{1,0:T(8,128)S(1)} %get-tuple-element.244), channel_id=1, source_target_pairs={{0,8},{4,12},{8,0},{12,4},{16,24},{20,28},{24,16},{28,20},{1,9},{5... | collective-permute-start | bytes 1179656 | tf_op jit(solution)/shard_map/stage_1_11/ppermute | solution.py:44
  33.3 20.8 %collective-permute-start.10 = (f32[768,128]{1,0:T(8,128)S(1)}, f32[768,128]{1,0:T(8,128)S(1)}, u32[]{:S(2)}, u32[]{:S(2)}) collective-permute-start(f32[768,128]{1,0:T(8,128)S(1)} %stage_3_12.1.rest_0_), channel_id=1, source_target_pairs={{0,2},{1,3},{2,0},{3,1},{4,6},{5,7},{6,4},{7,5},{8,10},{9,11},{10,... | collective-permute-start | bytes 1179656 | tf_op jit(solution)/shard_map/stage_3_12/ppermute | solution.py:44
  38.6 25.6 %collective-permute-start.15 = (f32[384,512]{1,0:T(8,128)S(1)}, f32[384,512]{1,0:T(8,128)S(1)}, u32[]{:S(2)}, u32[]{:S(2)}) collective-permute-start(f32[384,512]{1,0:T(8,128)S(1)} %copy-done), channel_id=1, source_target_pairs={{0,2},{1,3},{2,0},{3,1},{4,6},{5,7},{6,4},{7,5},{8,10},{9,11},{10,... | collective-permute-start | bytes 2359304 | tf_op jit(solution)/shard_map/stage_x_14/ppermute | solution.py:44
  40.0 19.8 %collective-permute-start.7 = (f32[384,128]{1,0:T(8,128)S(1)}, f32[384,128]{1,0:T(8,128)S(1)}, u32[]{:S(2)}, u32[]{:S(2)}) collective-permute-start(f32[384,128]{1,0:T(8,128)S(1)} %get-tuple-element.240), channel_id=1, source_target_pairs={{0,16},{4,20},{8,24},{12,28},{16,0},{20,4},{24,8},{28,12},{1,17},{... | collective-permute-start | bytes 589832 | tf_op jit(solution)/shard_map/stage_0_15/ppermute | solution.py:44
  42.5 25.1 %collective-permute-start.17 = (f32[768,128]{1,0:T(8,128)S(1)}, f32[768,128]{1,0:T(8,128)S(1)}, u32[]{:S(2)}, u32[]{:S(2)}) collective-permute-start(f32[768,128]{1,0:T(8,128)S(1)} %get-tuple-element.254), channel_id=1, source_target_pairs={{0,8},{4,12},{8,0},{12,4},{16,24},{20,28},{24,16},{28,20},{1,9},{5... | collective-permute-start | bytes 1179656 | tf_op jit(solution)/shard_map/stage_2_16/ppermute | solution.py:44
  52.6 12.7 %collective-permute-start.14 = (f32[384,128]{1,0:T(8,128)S(1)}, f32[384,128]{1,0:T(8,128)S(1)}, u32[]{:S(2)}, u32[]{:S(2)}) collective-permute-start(f32[384,128]{1,0:T(8,128)S(1)} %get-tuple-element.258), channel_id=1, source_target_pairs={{0,16},{4,20},{8,24},{12,28},{16,0},{20,4},{24,8},{28,12},{1,17},{... | collective-permute-start | bytes 589832 | tf_op jit(solution)/shard_map/stage_1_17/ppermute | solution.py:44
  60.0 37.1 %collective-permute-start.23 = (f32[384,128]{1,0:T(8,128)S(1)}, f32[384,128]{1,0:T(8,128)S(1)}, u32[]{:S(2)}, u32[]{:S(2)}) collective-permute-start(f32[384,128]{1,0:T(8,128)S(1)} %get-tuple-element.292.refs_0_), channel_id=1, source_target_pairs={{0,16},{4,20},{8,24},{12,28},{16,0},{20,4},{24,8},{28,12},{1,17},{... | collective-permute-start | bytes 589832 | tf_op jit(solution)/shard_map/stage_0_19/ppermute | solution.py:44
  61.9 20.9 %collective-permute-start.20 = (f32[768,128]{1,0:T(8,128)S(1)}, f32[768,128]{1,0:T(8,128)S(1)}, u32[]{:S(2)}, u32[]{:S(2)}) collective-permute-start(f32[768,128]{1,0:T(8,128)S(1)} %get-tuple-element.271), channel_id=1, source_target_pairs={{0,8},{4,12},{8,0},{12,4},{16,24},{20,28},{24,16},{28,20},{1,9},{5... | collective-permute-start | bytes 1179656 | tf_op jit(solution)/shard_map/stage_3_20/ppermute | solution.py:44
  64.3 50.8 %collective-permute-start.27 = (f32[768,512]{1,0:T(8,128)S(1)}, f32[768,512]{1,0:T(8,128)S(1)}, u32[]{:S(2)}, u32[]{:S(2)}) collective-permute-start(f32[768,512]{1,0:T(8,128)S(1)} %stage_x_21.1.refs_0_), channel_id=1, source_target_pairs={{0,1},{1,0},{2,3},{3,2},{4,5},{5,4},{6,7},{7,6},{8,9},{9,8},{10,11... | collective-permute-start | bytes 4718600 | tf_op jit(solution)/shard_map/stage_x_21/ppermute | solution.py:44
  65.4 18.5 %collective-permute-start.19 = (f32[384,128]{1,0:T(8,128)S(1)}, f32[384,128]{1,0:T(8,128)S(1)}, u32[]{:S(2)}, u32[]{:S(2)}) collective-permute-start(f32[384,128]{1,0:T(8,128)S(1)} %get-tuple-element.286.refs_0_), channel_id=1, source_target_pairs={{0,16},{4,20},{8,24},{12,28},{16,0},{20,4},{24,8},{28,12},{1,17},{... | collective-permute-start | bytes 589832 | tf_op jit(solution)/shard_map/stage_1_22/ppermute | solution.py:44
  67.7 29.2 %collective-permute-start.18 = (f32[384,128]{1,0:T(8,128)S(1)}, f32[384,128]{1,0:T(8,128)S(1)}, u32[]{:S(2)}, u32[]{:S(2)}) collective-permute-start(f32[384,128]{1,0:T(8,128)S(1)} %get-tuple-element.281), channel_id=1, source_target_pairs={{0,16},{4,20},{8,24},{12,28},{16,0},{20,4},{24,8},{28,12},{1,17},{... | collective-permute-start | bytes 589832 | tf_op jit(solution)/shard_map/stage_2_23/ppermute | solution.py:44
  82.8 24.7 %collective-permute-start.21 = (f32[384,128]{1,0:T(8,128)S(1)}, f32[384,128]{1,0:T(8,128)S(1)}, u32[]{:S(2)}, u32[]{:S(2)}) collective-permute-start(f32[384,128]{1,0:T(8,128)S(1)} %get-tuple-element.285), channel_id=1, source_target_pairs={{0,16},{4,20},{8,24},{12,28},{16,0},{20,4},{24,8},{28,12},{1,17},{... | collective-permute-start | bytes 589832 | tf_op jit(solution)/shard_map/stage_3_24/ppermute | solution.py:44
  84.0 17.9 %collective-permute-start.22 = (f32[768,128]{1,0:T(8,128)S(1)}, f32[768,128]{1,0:T(8,128)S(1)}, u32[]{:S(2)}, u32[]{:S(2)}) collective-permute-start(f32[768,128]{1,0:T(8,128)S(1)} %stage_1_25.1.refs_0_), channel_id=1, source_target_pairs={{0,8},{4,12},{8,0},{12,4},{16,24},{20,28},{24,16},{28,20},{1,9},{5... | collective-permute-start | bytes 1179656 | tf_op jit(solution)/shard_map/stage_1_25/ppermute | solution.py:44
  97.0 19.0 %collective-permute-start.26 = (f32[384,128]{1,0:T(8,128)S(1)}, f32[384,128]{1,0:T(8,128)S(1)}, u32[]{:S(2)}, u32[]{:S(2)}) collective-permute-start(f32[384,128]{1,0:T(8,128)S(1)} %get-tuple-element.309.refs_0_), channel_id=1, source_target_pairs={{0,16},{4,20},{8,24},{12,28},{16,0},{20,4},{24,8},{28,12},{1,17},{... | collective-permute-start | bytes 589832 | tf_op jit(solution)/shard_map/stage_2_26/ppermute | solution.py:44
  97.2 20.7 %collective-permute-start.25 = (f32[768,128]{1,0:T(8,128)S(1)}, f32[768,128]{1,0:T(8,128)S(1)}, u32[]{:S(2)}, u32[]{:S(2)}) collective-permute-start(f32[768,128]{1,0:T(8,128)S(1)} %stage_0_27.1.refs_0_), channel_id=1, source_target_pairs={{0,8},{4,12},{8,0},{12,4},{16,24},{20,28},{24,16},{28,20},{1,9},{5... | collective-permute-start | bytes 1179656 | tf_op jit(solution)/shard_map/stage_0_27/ppermute | solution.py:44
  102.0 7.5 %collective-permute-start.28 = (f32[1536,128]{1,0:T(8,128)S(1)}, f32[1536,128]{1,0:T(8,128)S(1)}, u32[]{:S(2)}, u32[]{:S(2)}) collective-permute-start(f32[1536,128]{1,0:T(8,128)S(1)} %stage_1_28.1.rest_0_), channel_id=1, source_target_pairs={{0,4},{4,0},{8,12},{12,8},{16,20},{20,16},{24,28},{28,24},{1,5},{5... | collective-permute-start | bytes 2359304 | tf_op jit(solution)/shard_map/stage_1_28/ppermute | solution.py:44
  107.7 14.0 %collective-permute-start.24 = (f32[384,128]{1,0:T(8,128)S(1)}, f32[384,128]{1,0:T(8,128)S(1)}, u32[]{:S(2)}, u32[]{:S(2)}) collective-permute-start(f32[384,128]{1,0:T(8,128)S(1)} %get-tuple-element.313.refs_0_), channel_id=1, source_target_pairs={{0,16},{4,20},{8,24},{12,28},{16,0},{20,4},{24,8},{28,12},{1,17},{... | collective-permute-start | bytes 589832 | tf_op jit(solution)/shard_map/stage_3_29/ppermute | solution.py:44
  113.9 44.3 %collective-permute-start.42 = (f32[768,128]{1,0:T(8,128)}, f32[768,128]{1,0:T(8,128)}, u32[]{:S(2)}, u32[]{:S(2)}) collective-permute-start(f32[768,128]{1,0:T(8,128)} %get-tuple-element.327.rest_3_), channel_id=1, source_target_pairs={{0,2},{1,3},{2,0},{3,1},{4,6},{5,7},{6,4},{7,5},{8,10},{9,11},{10,... | collective-permute-start | bytes 1179656 | tf_op jit(solution)/shard_map/stage_1_30/ppermute | solution.py:44
  116.1 12.2 %collective-permute-start.30 = (f32[768,128]{1,0:T(8,128)S(1)}, f32[768,128]{1,0:T(8,128)S(1)}, u32[]{:S(2)}, u32[]{:S(2)}) collective-permute-start(f32[768,128]{1,0:T(8,128)S(1)} %stage_2_32.1.refs_0_), channel_id=1, source_target_pairs={{0,8},{4,12},{8,0},{12,4},{16,24},{20,28},{24,16},{28,20},{1,9},{5... | collective-permute-start | bytes 1179656 | tf_op jit(solution)/shard_map/stage_2_32/ppermute | solution.py:44
  118.0 5.6 %collective-permute-start.31 = (f32[1536,128]{1,0:T(8,128)S(1)}, f32[1536,128]{1,0:T(8,128)S(1)}, u32[]{:S(2)}, u32[]{:S(2)}) collective-permute-start(f32[1536,128]{1,0:T(8,128)S(1)} %stage_0_33.1.rest_0_), channel_id=1, source_target_pairs={{0,4},{4,0},{8,12},{12,8},{16,20},{20,16},{24,28},{28,24},{1,5},{5... | collective-permute-start | bytes 2359304 | tf_op jit(solution)/shard_map/stage_0_33/ppermute | solution.py:44
  121.7 18.0 %collective-permute-start.29 = (f32[768,128]{1,0:T(8,128)S(1)}, f32[768,128]{1,0:T(8,128)S(1)}, u32[]{:S(2)}, u32[]{:S(2)}) collective-permute-start(f32[768,128]{1,0:T(8,128)S(1)} %stage_3_34.1.refs_0_), channel_id=1, source_target_pairs={{0,8},{4,12},{8,0},{12,4},{16,24},{20,28},{24,16},{28,20},{1,9},{5... | collective-permute-start | bytes 1179656 | tf_op jit(solution)/shard_map/stage_3_34/ppermute | solution.py:44
  128.6 6.7 %collective-permute-start.32 = (f32[1536,128]{1,0:T(8,128)S(1)}, f32[1536,128]{1,0:T(8,128)S(1)}, u32[]{:S(2)}, u32[]{:S(2)}) collective-permute-start(f32[1536,128]{1,0:T(8,128)S(1)} %stage_2_36.1.rest_0_), channel_id=1, source_target_pairs={{0,4},{4,0},{8,12},{12,8},{16,20},{20,16},{24,28},{28,24},{1,5},{5... | collective-permute-start | bytes 2359304 | tf_op jit(solution)/shard_map/stage_2_36/ppermute | solution.py:44
  130.3 10.7 %collective-permute-start.35 = (f32[768,128]{1,0:T(8,128)S(1)}, f32[768,128]{1,0:T(8,128)S(1)}, u32[]{:S(2)}, u32[]{:S(2)}) collective-permute-start(f32[768,128]{1,0:T(8,128)S(1)} %get-tuple-element.325.rest_1_), channel_id=1, source_target_pairs={{0,1},{1,0},{2,3},{3,2},{4,5},{5,4},{6,7},{7,6},{8,9},{9,8},{10,11... | collective-permute-start | bytes 1179656 | tf_op jit(solution)/shard_map/stage_0_35/ppermute | solution.py:44
  134.9 8.8 %collective-permute-start.34 = (f32[256,256]{1,0:T(8,128)S(1)}, f32[256,256]{1,0:T(8,128)S(1)}, u32[]{:S(2)}, u32[]{:S(2)}) collective-permute-start(f32[256,256]{1,0:T(8,128)S(1)} %get-tuple-element.329), channel_id=1, source_target_pairs={{0,4},{4,0},{8,12},{12,8},{16,20},{20,16},{24,28},{28,24},{1,5},{5... | collective-permute-start | bytes 786440 | tf_op jit(solution)/shard_map/stage_v_37/ppermute | solution.py:44
  139.0 18.0 %collective-permute-start.43 = (f32[768,128]{1,0:T(8,128)S(1)}, f32[768,128]{1,0:T(8,128)S(1)}, u32[]{:S(2)}, u32[]{:S(2)}) collective-permute-start(f32[768,128]{1,0:T(8,128)S(1)} %get-tuple-element.355.rest_1_), channel_id=1, source_target_pairs={{0,1},{1,0},{2,3},{3,2},{4,5},{5,4},{6,7},{7,6},{8,9},{9,8},{10,11... | collective-permute-start | bytes 1179656 | tf_op jit(solution)/shard_map/stage_2_38/ppermute | solution.py:44
  139.9 5.3 %collective-permute-start.33 = (f32[1536,128]{1,0:T(8,128)S(1)}, f32[1536,128]{1,0:T(8,128)S(1)}, u32[]{:S(2)}, u32[]{:S(2)}) collective-permute-start(f32[1536,128]{1,0:T(8,128)S(1)} %stage_3_39.1.rest_0_), channel_id=1, source_target_pairs={{0,4},{4,0},{8,12},{12,8},{16,20},{20,16},{24,28},{28,24},{1,5},{5... | collective-permute-start | bytes 2359304 | tf_op jit(solution)/shard_map/stage_3_39/ppermute | solution.py:44
  141.0 7.9 %collective-permute-start.38 = (f32[384,128]{1,0:T(8,128)S(1)}, f32[384,128]{1,0:T(8,128)S(1)}, u32[]{:S(2)}, u32[]{:S(2)}) collective-permute-start(f32[384,128]{1,0:T(8,128)S(1)} %get-tuple-element.340), channel_id=1, source_target_pairs={{0,2},{1,3},{2,0},{3,1},{4,6},{5,7},{6,4},{7,5},{8,10},{9,11},{10,... | collective-permute-start | bytes 589832 | tf_op jit(solution)/shard_map/stage_0_40/ppermute | solution.py:44
  143.8 10.4 %collective-permute-start.37 = (f32[128,256]{1,0:T(8,128)S(1)}, f32[128,256]{1,0:T(8,128)S(1)}, u32[]{:S(2)}, u32[]{:S(2)}) collective-permute-start(f32[128,256]{1,0:T(8,128)S(1)} %get-tuple-element.344), channel_id=1, source_target_pairs={{0,1},{1,0},{2,3},{3,2},{4,5},{5,4},{6,7},{7,6},{8,9},{9,8},{10,11... | collective-permute-start | bytes 393224 | tf_op jit(solution)/shard_map/stage_v_41/ppermute | solution.py:44
  148.9 14.8 %collective-permute-start.36 = (f32[768,128]{1,0:T(8,128)S(1)}, f32[768,128]{1,0:T(8,128)S(1)}, u32[]{:S(2)}, u32[]{:S(2)}) collective-permute-start(f32[768,128]{1,0:T(8,128)S(1)} %get-tuple-element.357.rest_3_), channel_id=1, source_target_pairs={{0,2},{1,3},{2,0},{3,1},{4,6},{5,7},{6,4},{7,5},{8,10},{9,11},{10,... | collective-permute-start | bytes 1179656 | tf_op jit(solution)/shard_map/stage_3_42/ppermute | solution.py:44
  154.2 7.9 %collective-permute-start.39 = (f32[64,256]{1,0:T(8,128)S(1)}, f32[64,256]{1,0:T(8,128)S(1)}, u32[]{:S(2)}, u32[]{:S(2)}) collective-permute-start(f32[64,256]{1,0:T(8,128)S(1)} %get-tuple-element.363), channel_id=1, source_target_pairs={{0,2},{1,3},{2,0},{3,1},{4,6},{5,7},{6,4},{7,5},{8,10},{9,11},{10,... | collective-permute-start | bytes 196616 | tf_op jit(solution)/shard_map/stage_v_45/ppermute | solution.py:44
  156.5 23.6 %collective-permute-start.56 = (f32[8,512]{1,0:T(8,128)S(1)}, f32[8,512]{1,0:T(8,128)S(1)}, u32[]{:S(2)}, u32[]{:S(2)}) collective-permute-start(f32[8,512]{1,0:T(8,128)S(1)} %constant_dynamic-update-slice_fusion), channel_id=1, source_target_pairs={{0,1},{1,0},{2,3},{3,2},{4,5},{5,4},{6,7},{7,6},{8,9},{9,8},{10,11... | collective-permute-start | bytes 49160 | tf_op jit(solution)/shard_map/stage_b_57/ppermute | solution.py:44
  158.2 9.0 %collective-permute-start.47 = (f32[384,128]{1,0:T(8,128)S(1)}, f32[384,128]{1,0:T(8,128)S(1)}, u32[]{:S(2)}, u32[]{:S(2)}) collective-permute-start(f32[384,128]{1,0:T(8,128)S(1)} %get-tuple-element.371), channel_id=1, source_target_pairs={{0,2},{1,3},{2,0},{3,1},{4,6},{5,7},{6,4},{7,5},{8,10},{9,11},{10,... | collective-permute-start | bytes 589832 | tf_op jit(solution)/shard_map/stage_2_47/ppermute | solution.py:44
  161.4 15.7 %collective-permute-start.51 = (f32[384,128]{1,0:T(8,128)S(1)}, f32[384,128]{1,0:T(8,128)S(1)}, u32[]{:S(2)}, u32[]{:S(2)}) collective-permute-start(f32[384,128]{1,0:T(8,128)S(1)} %get-tuple-element.375), channel_id=1, source_target_pairs={{0,1},{1,0},{2,3},{3,2},{4,5},{5,4},{6,7},{7,6},{8,9},{9,8},{10,11... | collective-permute-start | bytes 589832 | tf_op jit(solution)/shard_map/stage_1_48/ppermute | solution.py:44
  166.4 23.7 %collective-permute-start.44 = (f32[384,128]{1,0:T(8,128)S(1)}, f32[384,128]{1,0:T(8,128)S(1)}, u32[]{:S(2)}, u32[]{:S(2)}) collective-permute-start(f32[384,128]{1,0:T(8,128)S(1)} %get-tuple-element.385), channel_id=1, source_target_pairs={{0,1},{1,0},{2,3},{3,2},{4,5},{5,4},{6,7},{7,6},{8,9},{9,8},{10,11... | collective-permute-start | bytes 589832 | tf_op jit(solution)/shard_map/stage_3_51/ppermute | solution.py:44
  170.4 5.4 %collective-permute-start.49 = (f32[64,256]{1,0:T(8,128)S(1)}, f32[64,256]{1,0:T(8,128)S(1)}, u32[]{:S(2)}, u32[]{:S(2)}) collective-permute-start(f32[64,256]{1,0:T(8,128)S(1)} %stage_w_55.1.refs_0_), channel_id=1, source_target_pairs={{0,16},{4,20},{8,24},{12,28},{16,0},{20,4},{24,8},{28,12},{1,17},{... | collective-permute-start | bytes 196616 | tf_op jit(solution)/shard_map/stage_w_55/ppermute | solution.py:44
  171.3 5.7 %collective-permute-start.53 = (f32[64,256]{1,0:T(8,128)S(1)}, f32[64,256]{1,0:T(8,128)S(1)}, u32[]{:S(2)}, u32[]{:S(2)}) collective-permute-start(f32[64,256]{1,0:T(8,128)S(1)} %stage_v_56.1.refs_0_), channel_id=1, source_target_pairs={{0,2},{1,3},{2,0},{3,1},{4,6},{5,7},{6,4},{7,5},{8,10},{9,11},{10,... | collective-permute-start | bytes 196616 | tf_op jit(solution)/shard_map/stage_v_56/ppermute | solution.py:44
  179.2 8.1 %collective-permute-start.54 = (f32[128,256]{1,0:T(8,128)S(1)}, f32[128,256]{1,0:T(8,128)S(1)}, u32[]{:S(2)}, u32[]{:S(2)}) collective-permute-start(f32[128,256]{1,0:T(8,128)S(1)} %stage_w_61.1.refs_0_), channel_id=1, source_target_pairs={{0,1},{1,0},{2,3},{3,2},{4,5},{5,4},{6,7},{7,6},{8,9},{9,8},{10,11... | collective-permute-start | bytes 393224 | tf_op jit(solution)/shard_map/stage_w_61/ppermute | solution.py:44
  180.1 11.4 %collective-permute-start.59 = (f32[8,512]{1,0:T(8,128)S(1)}, f32[8,512]{1,0:T(8,128)S(1)}, u32[]{:S(2)}, u32[]{:S(2)}) collective-permute-start(f32[8,512]{1,0:T(8,128)S(1)} %add.24), channel_id=1, source_target_pairs={{0,2},{1,3},{2,0},{3,1},{4,6},{5,7},{6,4},{7,5},{8,10},{9,11},{10,... | collective-permute-start | bytes 49160 | tf_op jit(solution)/shard_map/stage_b_62/ppermute | solution.py:44
  180.9 10.6 %collective-permute-start.57 = (f32[256,256]{1,0:T(8,128)S(1)}, f32[256,256]{1,0:T(8,128)S(1)}, u32[]{:S(2)}, u32[]{:S(2)}) collective-permute-start(f32[256,256]{1,0:T(8,128)S(1)} %stage_v_63.1.refs_0_), channel_id=1, source_target_pairs={{0,4},{4,0},{8,12},{12,8},{16,20},{20,16},{24,28},{28,24},{1,5},{5... | collective-permute-start | bytes 786440 | tf_op jit(solution)/shard_map/stage_v_63/ppermute | solution.py:44
  (18 other events, 73.1 us)
